TPU v7x, 32 devices: a whole 2x2x4 slice. The times are simulated.
32 devices in a mesh: grp: 2 (over x), seq: 8 (over z, y), mp: 2 (over core).
Axes of the slice: x: 2, y: 2, z: 4, core: 2. Of those that a mesh axis runs over, the one named last changes fastest.
Arguments:
- frames: bfloat16 [1536, 8192], P(('grp', 'seq'), 'mp'), may hold values from -80 to 80
- token_session: int32 [1536], P(('grp', 'seq')), may hold values from 0 to 127, as said below
- ln_gain: float32 [8192], P('mp'), may hold values from 0.3 to 1.7
- w_key: bfloat16 [8192, 512], P('mp'), may hold values from -0.0625 to 0.0625
- w_value: bfloat16 [8192, 512], P('mp'), may hold values from -0.0625 to 0.0625
- k_bias: float32 [512], P('mp'), may hold values from -4 to 4
- v_bias: float32 [512], P('mp'), may hold values from -4 to 4
- queries: bfloat16 [128, 4096], P(('grp', 'seq'), 'mp'), may hold values from -4 to 4
- cache_key: bfloat16 [128, 128, 512], P(('grp', 'seq'), None, 'mp'), may hold values from -11 to 11
- cache_value: bfloat16 [128, 128, 512], P(('grp', 'seq'), None, 'mp'), may hold values from -6 to 6
- cache_start: int32 [128], P(('grp', 'seq')), may hold values from 0 to 127
- cache_len: int32 [128], P(('grp', 'seq')), may hold values from 1 to 128
Outputs:
- attended: bfloat16 [128, 4096], P(('grp', 'seq'), 'mp')
Inputs may be any that keep to these rules, and one draw needn't show every extreme that they name: `token_session`: each new frame token names a session; within the rows of one device at most 16 rows name sessions of one block of 8 consecutive sessions, and in every draw one such block gets exactly 16 rows from every device.
All inputs are finite; a program needn't handle non-finite values.
Results may differ from a plain program's by a relative error of at most 0.0023.
The roundings to bfloat16 on the way count: a program that leaves them out, or rounds other values in their place, can miss the bound.
Values may be sent and summed in bfloat16 or wider, within the bound.
No kernel may reach another device: no remote copies, remote signals or barrier semaphores. Data moves between devices by JAX's collectives and lax.ppermute only.
A program may use at most 64 MiB of HBM per device.

v0:
```python
import jax
import jax.numpy as jnp
from jax import lax
from jax.sharding import PartitionSpec as P

D = 8192
HEAD = 128
GROUP = 8


epsilon = 1e-06


def project(frame_rows, ln_gain, w_key, w_value, k_bias, v_bias):
    values32 = frame_rows.astype(jnp.float32)
    partial_squares = jnp.sum(values32 * values32, axis=1)
    squares = lax.psum(partial_squares, "mp")
    inverse_rms = lax.rsqrt(squares / D + epsilon)
    normed = (values32 * inverse_rms[:, None] * ln_gain[None, :]).astype(jnp.bfloat16)
    part_key = jnp.dot(normed, w_key, preferred_element_type=jnp.float32)
    part_value = jnp.dot(normed, w_value, preferred_element_type=jnp.float32)
    key_sums, value_sums = (
        lax.psum_scatter(part_key, "mp", scatter_dimension=1, tiled=True),
        lax.psum_scatter(part_value, "mp", scatter_dimension=1, tiled=True),
    )
    new_keys = (key_sums + k_bias[None, :]).astype(jnp.bfloat16)
    new_values = (value_sums + v_bias[None, :]).astype(jnp.bfloat16)
    return (new_keys, new_values)


def slot_sources(token_session, per_shard, partition_count, capacity):
    row_count = token_session.shape[0]
    target = token_session // per_shard
    one_hot = (target[:, None] == jnp.arange(partition_count, dtype=jnp.int32)[None, :]).astype(
        jnp.int32
    )
    order_in = jnp.sum((jnp.cumsum(one_hot, axis=0) - one_hot) * one_hot, axis=1)
    slot_index = target * capacity + order_in
    matches = (
        slot_index[None, :] == jnp.arange(partition_count * capacity, dtype=jnp.int32)[:, None]
    )
    source = jnp.sum(jnp.where(matches, jnp.arange(row_count, dtype=jnp.int32)[None, :], 0), axis=1)
    filled = jnp.any(matches, axis=1)
    sessions = jnp.where(filled, jnp.mod(token_session[source], per_shard), -1)
    return (source, filled, sessions)


def local(
    frames,
    token_session,
    ln_gain,
    w_key,
    w_value,
    k_bias,
    v_bias,
    queries,
    cache_key,
    cache_value,
    cache_start,
    cache_len,
):
    partition_count = lax.axis_size(("grp", "seq"))
    per_shard = queries.shape[0]
    rows_here = frames.shape[0]
    capacity = max(2, 5 * rows_here // (2 * partition_count) + 1)
    source, filled, sessions = slot_sources(token_session, per_shard, partition_count, capacity)
    session_slots = sessions.reshape(partition_count, capacity)
    nothing = jnp.zeros((), jnp.bfloat16)
    own_keys, own_values = project(frames, ln_gain, w_key, w_value, k_bias, v_bias)
    send_keys = jnp.where(filled[:, None], own_keys[source], nothing).reshape(
        partition_count, capacity, -1
    )
    send_values = jnp.where(filled[:, None], own_values[source], nothing).reshape(
        partition_count, capacity, -1
    )
    got_keys, got_values, got_sessions = (
        lax.all_to_all(send_keys, ("grp", "seq"), split_axis=0, concat_axis=0, tiled=True),
        lax.all_to_all(send_values, ("grp", "seq"), split_axis=0, concat_axis=0, tiled=True),
        lax.all_to_all(session_slots, ("grp", "seq"), split_axis=0, concat_axis=0, tiled=True),
    )
    new_keys = got_keys.reshape(partition_count * capacity, -1)
    new_values = got_values.reshape(partition_count * capacity, -1)
    new_sessions = got_sessions.reshape(-1)
    heads_kv = new_keys.shape[1] // HEAD
    window = cache_key.shape[1]
    score_scale = HEAD ** (-0.5)
    query_heads = queries.reshape(per_shard, heads_kv, GROUP, HEAD)
    cached_keys = cache_key.reshape(per_shard, window, heads_kv, HEAD)
    cached_values = cache_value.reshape(per_shard, window, heads_kv, HEAD)
    fresh_keys = new_keys.reshape(-1, heads_kv, HEAD)
    fresh_values = new_values.reshape(-1, heads_kv, HEAD)
    cached_scores = (
        jnp.einsum("sghd,swgd->sghw", query_heads, cached_keys, preferred_element_type=jnp.float32)
        * score_scale
    )
    positions = jnp.arange(window, dtype=jnp.int32)
    live_slots = jnp.mod(positions[None, :] - cache_start[:, None], window) < cache_len[:, None]
    cached_scores = jnp.where(live_slots[:, None, None, :], cached_scores, -jnp.inf)
    fresh_scores = (
        jnp.einsum("sghd,ngd->sghn", query_heads, fresh_keys, preferred_element_type=jnp.float32)
        * score_scale
    )
    own_rows = new_sessions[None, :] == jnp.arange(per_shard, dtype=jnp.int32)[:, None]
    fresh_scores = jnp.where(own_rows[:, None, None, :], fresh_scores, -jnp.inf)
    largest = jnp.maximum(jnp.max(cached_scores, axis=3), jnp.max(fresh_scores, axis=3))
    cached_exp = jnp.exp(cached_scores - largest[..., None])
    fresh_exp = jnp.exp(fresh_scores - largest[..., None])
    totals = jnp.sum(cached_exp, axis=3) + jnp.sum(fresh_exp, axis=3)
    cached_weights = (cached_exp / totals[..., None]).astype(jnp.bfloat16)
    fresh_weights = (fresh_exp / totals[..., None]).astype(jnp.bfloat16)
    attended = jnp.einsum(
        "sghw,swgd->sghd", cached_weights, cached_values, preferred_element_type=jnp.float32
    )
    attended = attended + jnp.einsum(
        "sghn,ngd->sghd", fresh_weights, fresh_values, preferred_element_type=jnp.float32
    )
    return attended.reshape(per_shard, -1).astype(jnp.bfloat16)


def solution(mesh):
    return jax.shard_map(
        local,
        mesh=mesh,
        in_specs=(
            P(("grp", "seq"), "mp"),
            P(("grp", "seq")),
            P("mp"),
            P("mp", None),
            P("mp", None),
            P("mp"),
            P("mp"),
            P(("grp", "seq"), "mp"),
            P(("grp", "seq"), None, "mp"),
            P(("grp", "seq"), None, "mp"),
            P(("grp", "seq")),
            P(("grp", "seq")),
        ),
        out_specs=P(("grp", "seq"), "mp"),
        check_vma=False,
    )
```

profile of v0, /device:TPU:0, one launch (start us, length us, event | category | flops | bytes accessed | tf_op | source)
XLA Modules:
  0.0 75.6 jit_solution(11946905259340128428)
XLA Ops:
  6.5 0.0 copy-start
  6.5 0.0 reduce-scatter.3.cloned.1.call-start
  6.5 1.4 %fusion = f32[96]{0:T(128)S(1)} fusion(bf16[96,4096]{1,0:T(8,128)(2,1)} %param.12), kind=kLoop, calls=%fused_computation.5 | loop fusion | flops 1179552 | bytes 786816 | tf_op jit(solution)/shard_map/reduce_sum | solution.py:16
  8.0 2.6 %psum.7 = f32[96]{0:T(128)S(1)} all-reduce(f32[96]{0:T(128)S(1)} %fusion), channel_id=1, replica_groups=mesh['grp'=2,'seq'=8,'mp'=2] {'mp'}, use_global_device_ids=true, to_apply=%region_6.7 | all-reduce | flops 96 | bytes 768 | tf_op jit(solution)/shard_map/psum | solution.py:17
  10.6 0.0 copy-start.1
  10.6 0.0 copy-start.3
  10.6 4.0 %fusion.16 = f32[96,512]{1,0:T(8,128)} fusion(bf16[4096,512]{1,0:T(8,128)(2,1)} %param.15, bf16[96,4096]{1,0:T(8,128)(2,1)} %param.12, f32[4096]{0:T(1024)} %param.14, f32[96]{0:T(128)S(1)} %add_rsqrt_fusion), kind=kOutput, calls=%fused_computation.23 | convolution fusion | flops 404226048 | bytes 5194112 | tf_op jit(solution)/shard_map/dot_general | solution.py:20
  14.6 0.0 copy-start.2
  14.6 0.0 reduce-scatter.3.cloned.1.call-update
  14.6 0.0 copy-done.1
  14.6 0.1 fusion.25
  14.7 0.1 reduce_window_sum.11
  14.9 0.2 select_reduce_fusion.1
  15.1 0.1 select_reduce_fusion
  15.2 0.1 fusion.22
  15.3 1.9 %gather_fusion = s32[256]{0:T(256)S(1)} fusion(s32[96]{0:T(128)S(1)} %copy-done.1, s32[1024]{0:T(1024)S(1)} %pad_clamp_fusion), kind=kCustom, calls=%fused_computation | custom fusion | bytes 3072 | tf_op jit(solution)/shard_map/gather | solution.py:44
  17.2 0.1 gather.16
  17.2 0.1 reduce_or.12
  17.3 0.6 fusion.31
  18.0 8.2 %all-to-all-start = ((s32[16,1,16]{2,1,0:T(1,128)}), s32[16,1,16]{2,1,0:T(1,128)S(1)}, u32[]{:S(2)}, u32[]{:S(2)}) async-start(s32[16,1,16]{2,1,0:T(1,128)} %bitcast.3), calls=%async_computation | async-start | bytes 16384 | tf_op jit(solution)/shard_map/all_to_all | solution.py:79
  26.2 0.0 copy-start.7
  26.2 0.0 copy-start.8
  26.2 0.0 copy-start.5
  26.2 0.0 copy-start.6
  26.2 0.0 reduce-scatter.5.cloned.1.call-start
  26.3 0.0 copy-done.3
  26.3 0.0 copy-done.2
  26.3 3.7 %fusion.14 = f32[96,512]{1,0:T(8,128)} fusion(bf16[4096,512]{1,0:T(8,128)(2,1)} %param.16, bf16[96,4096]{1,0:T(8,128)(2,1)S(1)} %copy-done.2, f32[4096]{0:T(1024)S(1)} %copy-done.3, f32[96]{0:T(128)S(1)} %add_rsqrt_fusion), kind=kOutput, calls=%fused_computation.22 | convolution fusion | flops 404226048 | bytes 5194112 | tf_op jit(solution)/shard_map/dot_general | solution.py:21
  30.0 0.0 reduce-scatter.5.cloned.1.call-update
  30.0 0.1 broadcast_in_dim.88
  30.1 0.0 copy-done.7
  30.1 0.0 copy-done.8
  30.1 0.1 fusion.33
  30.2 0.0 reduce-scatter.3.cloned.1.call-done
  30.2 0.0 copy-done.5
  30.2 0.9 %add_convert_fusion.1 = bf16[96,256]{1,0:T(8,128)(2,1)S(1)} fusion(f32[96,256]{1,0:T(8,128)} %reduce-scatter.3.cloned.1.call-done, f32[256]{0:T(256)S(1)} %copy-done.5), kind=kLoop, calls=%fused_computation.33 | loop fusion | flops 49152 | bytes 148480 | tf_op jit(solution)/shard_map/convert_element_type | solution.py:26
  31.1 0.0 copy-start.4
  31.1 1.2 %gather_fusion.1 = bf16[256,256]{1,0:T(8,128)(2,1)S(1)} fusion(bf16[96,256]{1,0:T(8,128)(2,1)S(1)} %add_convert_fusion.1, s32[1024]{0:T(1024)S(1)} %pad_clamp_fusion), kind=kCustom, calls=%fused_computation.1 | custom fusion | bytes 263168 | tf_op jit(solution)/shard_map/gather | solution.py:70
  32.3 6.7 %reduce-scatter.5.cloned.1.call-done = f32[96,256]{1,0:T(8,128)} async-done(((f32[96,512]{1,0:T(8,128)}), f32[96,256]{1,0:T(8,128)}) %reduce-scatter.5.cloned.1.call-update) | async-done | bytes 98320 | tf_op jit(solution)/shard_map/reduce_scatter | solution.py:24
  39.0 0.0 copy-done.6
  39.0 0.9 %add_convert_fusion = bf16[96,256]{1,0:T(8,128)(2,1)S(1)} fusion(f32[96,256]{1,0:T(8,128)} %reduce-scatter.5.cloned.1.call-done, f32[256]{0:T(256)S(1)} %copy-done.6), kind=kLoop, calls=%fused_computation.32 | loop fusion | flops 49152 | bytes 148480 | tf_op jit(solution)/shard_map/convert_element_type | solution.py:27
  39.9 1.2 %gather_fusion.2 = bf16[256,256]{1,0:T(8,128)(2,1)S(1)} fusion(bf16[96,256]{1,0:T(8,128)(2,1)S(1)} %add_convert_fusion, s32[1024]{0:T(1024)S(1)} %pad_clamp_fusion), kind=kCustom, calls=%fused_computation.2 | custom fusion | bytes 263168 | tf_op jit(solution)/shard_map/gather | solution.py:73
  41.1 0.0 copy-start.9
  41.1 0.8 %broadcast_select_fusion = (bf16[16,16,256]{2,1,0:T(8,128)(2,1)}, bf16[16,16,256]{2,1,0:T(8,128)(2,1)}) fusion(bf16[16,16,256]{2,1,0:T(8,128)(2,1)S(1)} %bitcast.47, pred[16,16]{1,0:T(8,128)(4,1)S(1)} %broadcast_in_dim.88, bf16[16,16,256]{2,1,0:T(8,128)(2,1)S(1)} %bitcast.46), kind=kLoop, calls=%fused_computation.29 | loop fusion | flops 131072 | bytes 524544 | tf_op jit(solution)/shard_map/jit(_where)/select_n | solution.py:73
  41.9 0.0 all-to-all-done
  41.9 6.8 %all-to-all-start.1 = ((bf16[16,16,256]{2,1,0:T(8,128)(2,1)}), bf16[16,16,256]{2,1,0:T(8,128)(2,1)S(1)}, u32[]{:S(2)}, u32[]{:S(2)}) async-start(bf16[16,16,256]{2,1,0:T(8,128)(2,1)} %get-tuple-element.6), calls=%async_computation.2 | async-start | bytes 262144 | tf_op jit(solution)/shard_map/all_to_all | solution.py:77
  48.7 0.0 copy-done
  48.7 0.0 copy-done.4
  48.7 0.5 fusion.38
  49.2 0.5 broadcast.169
  49.7 0.7 reduce.3
  50.4 0.1 eq.55
  50.4 6.1 %all-to-all-done.1 = bf16[16,16,256]{2,1,0:T(8,128)(2,1)S(1)} async-done(((bf16[16,16,256]{2,1,0:T(8,128)(2,1)}), bf16[16,16,256]{2,1,0:T(8,128)(2,1)S(1)}, u32[]{:S(2)}, u32[]{:S(2)}) %all-to-all-start.1) | async-done | bytes 131104 | tf_op jit(solution)/shard_map/all_to_all | solution.py:77
  56.6 3.5 %all-to-all-start.2 = ((bf16[16,16,256]{2,1,0:T(8,128)(2,1)}), bf16[16,16,256]{2,1,0:T(8,128)(2,1)S(1)}, u32[]{:S(2)}, u32[]{:S(2)}) async-start(bf16[16,16,256]{2,1,0:T(8,128)(2,1)} %get-tuple-element.5), calls=%async_computation.4 | async-start | bytes 262144 | tf_op jit(solution)/shard_map/all_to_all | solution.py:78
  60.1 0.3 fusion.37
  60.4 0.2 fusion.21
  60.6 0.2 fusion.24
  60.8 0.0 copy-done.9
  60.8 0.3 fusion.9
  61.1 6.8 %all-to-all-done.2 = bf16[16,16,256]{2,1,0:T(8,128)(2,1)S(1)} async-done(((bf16[16,16,256]{2,1,0:T(8,128)(2,1)}), bf16[16,16,256]{2,1,0:T(8,128)(2,1)S(1)}, u32[]{:S(2)}, u32[]{:S(2)}) %all-to-all-start.2) | async-done | bytes 131104 | tf_op jit(solution)/shard_map/all_to_all | solution.py:78
  67.9 0.2 fusion.8
  68.1 0.6 copy.112
  (12 shorter events, 0.1 us)
Async XLA Ops:
  6.5 42.1 %copy-start = (bf16[8,128,256]{2,1,0:T(8,128)(2,1)S(1)}, bf16[8,128,256]{2,1,0:T(8,128)(2,1)}, u32[]{:S(2)}) copy-start(bf16[8,128,256]{2,1,0:T(8,128)(2,1)} %param.20) | copy-start | bytes 1572868
  6.5 23.7 %reduce-scatter.3.cloned.1.call-start = ((), (), s32[]{:S(2)}) async-start(), calls=%async_computation.5 | async-start | bytes 294912 | tf_op jit(solution)/shard_map/reduce_scatter | solution.py:23
  10.6 4.0 %copy-start.1 = (s32[96]{0:T(128)S(1)}, s32[96]{0:T(128)}, u32[]{:S(2)}) copy-start(s32[96]{0:T(128)} %param.13) | copy-start | bytes 1156
  10.6 15.7 %copy-start.3 = (f32[4096]{0:T(1024)S(1)}, f32[4096]{0:T(1024)}, u32[]{:S(2)}) copy-start(f32[4096]{0:T(1024)} %param.14) | copy-start | bytes 49156
  14.6 11.7 %copy-start.2 = (bf16[96,4096]{1,0:T(8,128)(2,1)S(1)}, bf16[96,4096]{1,0:T(8,128)(2,1)}, u32[]{:S(2)}) copy-start(bf16[96,4096]{1,0:T(8,128)(2,1)} %param.12) | copy-start | bytes 2359300
  18.0 24.0 %all-to-all-start = ((s32[16,1,16]{2,1,0:T(1,128)}), s32[16,1,16]{2,1,0:T(1,128)S(1)}, u32[]{:S(2)}, u32[]{:S(2)}) async-start(s32[16,1,16]{2,1,0:T(1,128)} %bitcast.3), calls=%async_computation | async-start | bytes 16384 | tf_op jit(solution)/shard_map/all_to_all | solution.py:79
  26.2 3.9 %copy-start.7 = (s32[8]{0:T(128)S(1)}, s32[8]{0:T(128)}, u32[]{:S(2)}) copy-start(s32[8]{0:T(128)} %param.23) | copy-start | bytes 100
  26.2 3.9 %copy-start.8 = (s32[8]{0:T(128)S(1)}, s32[8]{0:T(128)}, u32[]{:S(2)}) copy-start(s32[8]{0:T(128)} %param.22) | copy-start | bytes 100
  26.2 4.0 %copy-start.5 = (f32[256]{0:T(256)S(1)}, f32[256]{0:T(256)}, u32[]{:S(2)}) copy-start(f32[256]{0:T(256)} %param.17) | copy-start | bytes 3076
  26.2 12.8 %copy-start.6 = (f32[256]{0:T(256)S(1)}, f32[256]{0:T(256)}, u32[]{:S(2)}) copy-start(f32[256]{0:T(256)} %param.18) | copy-start | bytes 3076
  26.2 12.8 %reduce-scatter.5.cloned.1.call-start = ((), (), s32[]{:S(2)}) async-start(), calls=%async_computation.6 | async-start | bytes 294912 | tf_op jit(solution)/shard_map/reduce_scatter | solution.py:24
  31.1 17.6 %copy-start.4 = (bf16[8,2048]{1,0:T(8,128)(2,1)S(1)}, bf16[8,2048]{1,0:T(8,128)(2,1)}, u32[]{:S(2)}) copy-start(bf16[8,2048]{1,0:T(8,128)(2,1)} %param.19) | copy-start | bytes 98308
  41.1 19.7 %copy-start.9 = (bf16[8,128,256]{2,1,0:T(8,128)(2,1)S(1)}, bf16[8,128,256]{2,1,0:T(8,128)(2,1)}, u32[]{:S(2)}) copy-start(bf16[8,128,256]{2,1,0:T(8,128)(2,1)} %param.21) | copy-start | bytes 1572868
  41.9 14.7 %all-to-all-start.1 = ((bf16[16,16,256]{2,1,0:T(8,128)(2,1)}), bf16[16,16,256]{2,1,0:T(8,128)(2,1)S(1)}, u32[]{:S(2)}, u32[]{:S(2)}) async-start(bf16[16,16,256]{2,1,0:T(8,128)(2,1)} %get-tuple-element.6), calls=%async_computation.2 | async-start | bytes 262144 | tf_op jit(solution)/shard_map/all_to_all | solution.py:77
  56.6 11.3 %all-to-all-start.2 = ((bf16[16,16,256]{2,1,0:T(8,128)(2,1)}), bf16[16,16,256]{2,1,0:T(8,128)(2,1)S(1)}, u32[]{:S(2)}, u32[]{:S(2)}) async-start(bf16[16,16,256]{2,1,0:T(8,128)(2,1)} %get-tuple-element.5), calls=%async_computation.4 | async-start | bytes 262144 | tf_op jit(solution)/shard_map/all_to_all | solution.py:78
Sparse Core Ops, SparseCore 0:
  14.7 10.1 reduce-scatter.2
  30.1 8.8 reduce-scatter.4
where the time goes:
time: 76 us; the launch traced here: 75.6 us
  waiting for transfers between devices  19.7 us (26%)
  starting transfers between devices  18.5 us (24%)
  between operations  13.7 us (18%)
  matrix products  8.96 us (12%)
  other arithmetic  6.42 us (8%)
  local copies, waits for them, and re-layouts  5.79 us (8%)
  blocking collectives  2.59 us (3%)
    all_to_all x1, starting transfers between devices, local(): lax.all_to_all(session_slots, ('grp', 'seq'), split_axis=0, concat_axis=0...  8.2 us
    all_to_all x1, starting transfers between devices, local(): lax.all_to_all(send_keys, ('grp', 'seq'), split_axis=0, concat_axis=0, ti...  6.76 us
    all_to_all x1, waiting for transfers between devices, local(): lax.all_to_all(send_values, ('grp', 'seq'), split_axis=0, concat_axis=0,...  6.75 us
    reduce_scatter x1, waiting for transfers between devices, project(): lax.psum_scatter(part_value, 'mp', scatter_dimension=1, tiled=True)  6.74 us
    all_to_all x1, waiting for transfers between devices, local(): lax.all_to_all(send_keys, ('grp', 'seq'), split_axis=0, concat_axis=0, ti...  6.13 us
    dot_general x1, matrix products, project(): part_key = jnp.dot(normed, w_key, preferred_element_type=jnp.float32)  4 us
    dot_general x1, matrix products, project(): part_value = jnp.dot(normed, w_value, preferred_element_type=jnp.float32)  3.72 us
    all_to_all x1, starting transfers between devices, local(): lax.all_to_all(send_values, ('grp', 'seq'), split_axis=0, concat_axis=0,...  3.51 us
  transfers between devices with their start and end apart: 5, of which 3 were waited for; matrix products, arithmetic and copies ran while one was open for 20% of the time, Pallas kernels for 0%

commit v1 on v0

--- a/solution.py
+++ b/solution.py
@@ -1,21 +1,275 @@
+import functools
+
 import jax
 import jax.numpy as jnp
 from jax import lax
+from jax.experimental import pallas as pl
+from jax.experimental.pallas import tpu as pltpu
 from jax.sharding import PartitionSpec as P
 
-D = 8192
 HEAD = 128
 GROUP = 8
 
-
 epsilon = 1e-06
+
+
+def params(mib):
+    return pltpu.CompilerParams(vmem_limit_bytes=mib << 20)
+
+
+def cost(flops, nbytes):
+    return pl.CostEstimate(flops=flops, bytes_accessed=nbytes, transcendentals=0)
+
+
+def nt_dot(a, b):
+    return lax.dot_general(a, b, (((1,), (1,)), ((), ())), preferred_element_type=jnp.float32)
+
+
+def dot(a, b):
+    return jnp.dot(a, b, preferred_element_type=jnp.float32)
+
+
+def squares_kernel(frames_ref, out_ref):
+    columns = frames_ref.shape[1]
+    total = None
+    for at in range(0, columns, HEAD):
+        part = frames_ref[:, at : at + HEAD].astype(jnp.float32)
+        part = part * part
+        total = part if total is None else total + part
+    out_ref[...] = total
+
+
+def partial_squares(frames):
+    rows, columns = frames.shape
+    return pl.pallas_call(
+        squares_kernel,
+        out_shape=jax.ShapeDtypeStruct((rows, HEAD), jnp.float32),
+        compiler_params=params(8),
+        cost_estimate=cost(2 * rows * columns, 2 * rows * columns),
+        name="partial_squares",
+    )(frames)
+
+
+def halves(index_ref, normed, w_ref, sent_ref, kept_ref):
+    mine = index_ref[0]
+    width = sent_ref.shape[1]
+    for half, out_ref in ((1 - mine, sent_ref), (mine, kept_ref)):
+        columns = pl.ds(pl.multiple_of(half * width, width), width)
+        out_ref[...] = dot(normed, w_ref[:, columns])
+
+
+def key_kernel(
+    features, index_ref, frames_ref, own_ref, other_ref, gain_ref, w_ref, normed_ref, sent_ref, kept_ref
+):
+    squares = jnp.sum(own_ref[...] + other_ref[...], axis=1, keepdims=True)
+    inverse_rms = lax.rsqrt(squares / features + epsilon)
+    normed_ref[...] = (
+        frames_ref[...].astype(jnp.float32) * inverse_rms * gain_ref[...]
+    ).astype(jnp.bfloat16)
+    halves(index_ref, normed_ref[...], w_ref, sent_ref, kept_ref)
+
+
+def value_kernel(index_ref, normed_ref, w_ref, sent_ref, kept_ref):
+    halves(index_ref, normed_ref[...], w_ref, sent_ref, kept_ref)
+
+
+SMEM = pl.BlockSpec(memory_space=pltpu.SMEM)
+VMEM = pl.BlockSpec(memory_space=pltpu.VMEM)
+
+
+def project_keys(index, frames, own, other, gain, w, features):
+    rows, columns = frames.shape
+    width = w.shape[1] // 2
+    half = jax.ShapeDtypeStruct((rows, width), jnp.float32)
+    return pl.pallas_call(
+        functools.partial(key_kernel, features),
+        out_shape=(jax.ShapeDtypeStruct(frames.shape, jnp.bfloat16), half, half),
+        in_specs=[SMEM] + [VMEM] * 5,
+        out_specs=(VMEM, VMEM, VMEM),
+        compiler_params=params(16),
+        cost_estimate=cost(4 * rows * columns * width, 2 * w.size),
+        name="project_keys",
+    )(index, frames, own, other, gain, w)
+
+
+def project_values(index, normed, w):
+    rows, columns = normed.shape
+    width = w.shape[1] // 2
+    half = jax.ShapeDtypeStruct((rows, width), jnp.float32)
+    return pl.pallas_call(
+        value_kernel,
+        out_shape=(half, half),
+        in_specs=[SMEM] + [VMEM] * 2,
+        out_specs=(VMEM, VMEM),
+        compiler_params=params(16),
+        cost_estimate=cost(4 * rows * columns * width, 2 * w.size),
+        name="project_values",
+    )(index, normed, w)
+
+
+def pack_kernel(
+    per_shard,
+    capacity,
+    here_ref,
+    session_ref,
+    kept_key_ref,
+    got_key_ref,
+    kept_value_ref,
+    got_value_ref,
+    key_bias_ref,
+    value_bias_ref,
+    out_ref,
+):
+    partitions, _, _ = out_ref.shape
+    rows, width = kept_key_ref.shape
+    slots = partitions * capacity
+    session = session_ref[...]
+    target = lax.div(session, per_shard)
+    local = session - target * per_shard
+    to = lax.broadcasted_iota(jnp.int32, (partitions, rows), 0) == target
+    to = to.astype(jnp.float32)
+    earlier = lax.broadcasted_iota(jnp.int32, (rows, rows), 0) < lax.broadcasted_iota(
+        jnp.int32, (rows, rows), 1
+    )
+    ahead = dot(to.astype(jnp.bfloat16), earlier.astype(jnp.bfloat16))
+    order = jnp.sum(to * ahead, axis=0, keepdims=True).astype(jnp.int32)
+    place = lax.broadcasted_iota(jnp.int32, (slots, rows), 0)
+    pick = (place == target * capacity + order).astype(jnp.bfloat16)
+    lane = (place == here_ref[0] * capacity + order).astype(jnp.bfloat16)
+    ids = nt_dot((to * (local + 1).astype(jnp.float32)).astype(jnp.bfloat16), lane)
+    key = (kept_key_ref[...] + got_key_ref[...] + key_bias_ref[...]).astype(jnp.bfloat16)
+    value = (kept_value_ref[...] + got_value_ref[...] + value_bias_ref[...]).astype(jnp.bfloat16)
+    at = 0
+    for source in (key, value):
+        laid = dot(pick, source).astype(jnp.bfloat16).reshape(partitions, capacity, width)
+        for column in range(0, width, HEAD):
+            out_ref[:, at : at + capacity, :] = laid[:, :, column : column + HEAD]
+            at += capacity
+    ids = ids.astype(jnp.bfloat16)
+    extra = out_ref.shape[1] - at
+    row = lax.broadcasted_iota(jnp.int32, (partitions, extra, HEAD), 1)
+    block = jnp.zeros((partitions, extra, HEAD), jnp.float32)
+    for j in range(slots // HEAD):
+        part = ids[:, j * HEAD : (j + 1) * HEAD].astype(jnp.float32)
+        block = jnp.where(row == j, part[:, None, :], block)
+    out_ref[:, at:, :] = block.astype(jnp.bfloat16)
+
+
+def pack(here, session, kept_key, got_key, kept_value, got_value, key_bias, value_bias, sizes):
+    partitions, per_shard, capacity = sizes
+    rows, width = kept_key.shape
+    id_rows = -(-partitions * capacity // HEAD)
+    block = 2 * width // HEAD * capacity + -(-id_rows // 8) * 8
+    return pl.pallas_call(
+        functools.partial(pack_kernel, per_shard, capacity),
+        out_shape=jax.ShapeDtypeStruct((partitions, block, HEAD), jnp.bfloat16),
+        in_specs=[SMEM] + [VMEM] * 7,
+        out_specs=VMEM,
+        compiler_params=params(8),
+        cost_estimate=cost(4 * rows * width * partitions * capacity, 16 * rows * width),
+        name="pack",
+    )(here, session, kept_key, got_key, kept_value, got_value, key_bias, value_bias)
+
+
+def queries_of(queries_ref, head):
+    columns = [
+        queries_ref[:, at * HEAD : (at + 1) * HEAD].astype(jnp.float32)
+        for at in range(head * GROUP, (head + 1) * GROUP)
+    ]
+    return jnp.concatenate(columns, axis=0).astype(jnp.bfloat16)
+
+
+def cached_kernel(start_ref, len_ref, queries_ref, key_ref, out_ref):
+    heads, rows, window = out_ref.shape
+    sessions = queries_ref.shape[0]
+    row_session = lax.broadcasted_iota(jnp.int32, (rows, window), 0) % sessions
+    slot = lax.broadcasted_iota(jnp.int32, (rows, window), 1)
+    live = []
+    for session in range(sessions):
+        since = slot - start_ref[session]
+        since = jnp.where(since < 0, since + window, since)
+        live.append(since < len_ref[session])
+    for head in range(heads):
+        query = queries_of(queries_ref, head)
+        total = jnp.full((rows, window), -jnp.inf, jnp.float32)
+        for session in range(sessions):
+            key = key_ref[session, :, head * HEAD : (head + 1) * HEAD]
+            score = nt_dot(query, key) * (HEAD**-0.5)
+            total = jnp.where((row_session == session) & live[session], score, total)
+        out_ref[head] = total
+
+
+def cached_scores(start, length, queries, cache_key):
+    sessions, window, width = cache_key.shape
+    heads = width // HEAD
+    return pl.pallas_call(
+        cached_kernel,
+        out_shape=jax.ShapeDtypeStruct((heads, GROUP * sessions, window), jnp.float32),
+        in_specs=[SMEM, SMEM, VMEM, VMEM],
+        out_specs=VMEM,
+        compiler_params=params(8),
+        cost_estimate=cost(2 * GROUP * sessions * cache_key.size, 2 * cache_key.size),
+        name="cached_scores",
+    )(start, length, queries, cache_key)
+
+
+def attend_kernel(capacity, got_ref, queries_ref, score_ref, cache_ref, out_ref):
+    heads, rows, window = score_ref.shape
+    sessions = queries_ref.shape[0]
+    partitions = got_ref.shape[0]
+    slots = partitions * capacity
+    at = 2 * heads * capacity
+    ids = jnp.concatenate(
+        [
+            jnp.sum(got_ref[:, at + j : at + j + 1, :].astype(jnp.float32), axis=0)
+            for j in range(slots // HEAD)
+        ],
+        axis=1,
+    ).astype(jnp.int32)
+    own = lax.broadcasted_iota(jnp.int32, (rows, slots), 0) % sessions + 1 == ids
+    row_session = lax.broadcasted_iota(jnp.int32, (rows, window), 0) % sessions
+    for head in range(heads):
+        query = queries_of(queries_ref, head)
+        key = got_ref[:, head * capacity : (head + 1) * capacity, :].reshape(slots, HEAD)
+        first = (heads + head) * capacity
+        value = got_ref[:, first : first + capacity, :].reshape(slots, HEAD)
+        cached = score_ref[head]
+        fresh = jnp.where(own, nt_dot(query, key) * (HEAD**-0.5), -jnp.inf)
+        largest = jnp.maximum(
+            jnp.max(cached, axis=1, keepdims=True), jnp.max(fresh, axis=1, keepdims=True)
+        )
+        cached = jnp.exp(cached - largest)
+        fresh = jnp.exp(fresh - largest)
+        total = jnp.sum(cached, axis=1, keepdims=True) + jnp.sum(fresh, axis=1, keepdims=True)
+        cached = cached / total
+        attended = dot((fresh / total).astype(jnp.bfloat16), value)
+        for session in range(sessions):
+            weights = jnp.where(row_session == session, cached, 0.0).astype(jnp.bfloat16)
+            attended += dot(weights, cache_ref[session, :, head * HEAD : (head + 1) * HEAD])
+        for q in range(GROUP):
+            column = (head * GROUP + q) * HEAD
+            out_ref[:, column : column + HEAD] = attended[
+                q * sessions : (q + 1) * sessions
+            ].astype(jnp.bfloat16)
+
+
+def attend(got, queries, scores, cache_value, capacity):
+    return pl.pallas_call(
+        functools.partial(attend_kernel, capacity),
+        out_shape=jax.ShapeDtypeStruct(queries.shape, jnp.bfloat16),
+        in_specs=[VMEM] * 4,
+        out_specs=VMEM,
+        compiler_params=params(8),
+        cost_estimate=cost(4 * queries.shape[0] * GROUP * cache_value.size, 2 * cache_value.size),
+        name="attend",
+    )(got, queries, scores, cache_value)
 
 
 def project(frame_rows, ln_gain, w_key, w_value, k_bias, v_bias):
     values32 = frame_rows.astype(jnp.float32)
     partial_squares = jnp.sum(values32 * values32, axis=1)
     squares = lax.psum(partial_squares, "mp")
-    inverse_rms = lax.rsqrt(squares / D + epsilon)
+    inverse_rms = lax.rsqrt(squares / (frame_rows.shape[1] * lax.axis_size("mp")) + epsilon)
     normed = (values32 * inverse_rms[:, None] * ln_gain[None, :]).astype(jnp.bfloat16)
     part_key = jnp.dot(normed, w_key, preferred_element_type=jnp.float32)
     part_value = jnp.dot(normed, w_value, preferred_element_type=jnp.float32)
@@ -45,7 +299,7 @@
     return (source, filled, sessions)
 
 
-def local(
+def general(
     frames,
     token_session,
     ln_gain,
@@ -117,6 +371,50 @@
     return attended.reshape(per_shard, -1).astype(jnp.bfloat16)
 
 
+def local(
+    frames,
+    token_session,
+    ln_gain,
+    w_key,
+    w_value,
+    k_bias,
+    v_bias,
+    queries,
+    cache_key,
+    cache_value,
+    cache_start,
+    cache_len,
+):
+    partitions = lax.axis_size(("grp", "seq"))
+    shares = lax.axis_size("mp")
+    per_shard = queries.shape[0]
+    rows = frames.shape[0]
+    capacity = max(2, 5 * rows // (2 * partitions) + 1)
+    if shares != 2 or per_shard % 8 or capacity % 16 or partitions * capacity % HEAD:
+        return general(
+            frames, token_session, ln_gain, w_key, w_value, k_bias, v_bias, queries, cache_key, cache_value,
+            cache_start, cache_len,
+        )
+    swap = [(0, 1), (1, 0)]
+    index = lax.axis_index("mp").astype(jnp.int32).reshape(1)
+    here = lax.axis_index(("grp", "seq")).astype(jnp.int32).reshape(1)
+    own = partial_squares(frames)
+    other = lax.ppermute(own, "mp", swap)
+    normed, sent_key, kept_key = project_keys(
+        index, frames, own, other, ln_gain[None, :], w_key, frames.shape[1] * shares
+    )
+    got_key = lax.ppermute(sent_key, "mp", swap)
+    sent_value, kept_value = project_values(index, normed, w_value)
+    got_value = lax.ppermute(sent_value, "mp", swap)
+    blocks = pack(
+        here, token_session[None, :], kept_key, got_key, kept_value, got_value, k_bias[None, :],
+        v_bias[None, :], (partitions, per_shard, capacity),
+    )
+    got = lax.all_to_all(blocks, ("grp", "seq"), split_axis=0, concat_axis=0, tiled=True)
+    scores = cached_scores(cache_start, cache_len, queries, cache_key)
+    return attend(got, queries, scores, cache_value, capacity)
+
+
 def solution(mesh):
     return jax.shard_map(
         local,

time: 76 us -> 32.4 us (0.43)
  between operations: 13.7 us -> 0.1 us
  starting transfers between devices: 18.5 us -> 9.37 us
  matrix products: 8.96 us -> 0 us
  waiting for transfers between devices: 19.7 us -> 11.8 us
  other arithmetic: 6.42 us -> 0 us
  Pallas kernels: 0 us -> 5.17 us
  blocking collectives: 2.59 us -> 0 us
    all_to_all x3 -> x1, starting transfers between devices: 18.5 us -> 8.2 us  [local(): lax.all_to_all(blocks, ('grp', 'seq'), split_axis=0, concat_axis=0, tiled...]
    dot_general x6 -> x0, matrix products: 8.96 us -> none  [the longest x1 4 us: project(): part_key = jnp.dot(normed, w_key, preferred_element_type=jnp.float32)]
    reduce_scatter x2 -> x0, waiting for transfers between devices: 6.75 us -> none  [the longest x1 6.74 us: project(): lax.psum_scatter(part_value, 'mp', scatter_dimension=1, tiled=True)]
    pallas_call x0 -> x6, Pallas kernels: none -> 5.17 us  [the longest x1 1.23 us: attend(): pl.pallas_call(functools.partial(attend_kernel, capacity), out_shape=jax....]
    unnamed x21 -> x26, local copies, waits for them, and re-layouts: 0.68 us -> 5.6 us
    gather x4 -> x0, local copies, waits for them, and re-layouts: 4.25 us -> none  [the longest x2 1.94 us: slot_sources(): sessions = jnp.where(filled, jnp.mod(token_session[source], per_shard), -1)]
    all_to_all x3 -> x1, waiting for transfers between devices: 12.9 us -> 9.94 us  [local(): lax.all_to_all(blocks, ('grp', 'seq'), split_axis=0, concat_axis=0, tiled...]
    psum x1 -> x0, blocking collectives: 2.59 us -> none  [project(): squares = lax.psum(partial_squares, 'mp')]
  transfers between devices with their start and end apart: 5 -> 4, of which waited for: 3 -> 3; matrix products, arithmetic and copies ran while one was open for 20% -> 0% of each run, Pallas kernels for 0% -> 6%
where the time goes in v1:
time: 32.4 us; the launch traced here: 32 us
  waiting for transfers between devices  11.8 us (36%)
  starting transfers between devices  9.37 us (29%)
  local copies, waits for them, and re-layouts  5.6 us (17%)
  Pallas kernels  5.17 us (16%)
    all_to_all x1, waiting for transfers between devices, local(): lax.all_to_all(blocks, ('grp', 'seq'), split_axis=0, concat_axis=0, tiled...  9.94 us
    all_to_all x1, starting transfers between devices, local(): lax.all_to_all(blocks, ('grp', 'seq'), split_axis=0, concat_axis=0, tiled...  8.2 us
    unnamed x26, local copies, waits for them, and re-layouts  5.6 us
    pallas_call x1, Pallas kernels, attend(): pl.pallas_call(functools.partial(attend_kernel, capacity), out_shape=jax....  1.23 us
    pallas_call x1, Pallas kernels, pack(): pl.pallas_call(functools.partial(pack_kernel, per_shard, capacity), out_s...  1.08 us
    pallas_call x1, Pallas kernels, cached_scores(): pl.pallas_call(cached_kernel, out_shape=jax.ShapeDtypeStruct((heads, GROU...  1 us
    ppermute x1, waiting for transfers between devices, local(): got_value = lax.ppermute(sent_value, 'mp', swap)  0.94 us
    pallas_call x1, Pallas kernels, project_keys(): pl.pallas_call(functools.partial(key_kernel, features), out_shape=(jax.Sh...  0.89 us
  transfers between devices with their start and end apart: 4, of which 3 were waited for; matrix products, arithmetic and copies ran while one was open for 0% of the time, Pallas kernels for 6%

profile of v1, /device:TPU:0, one launch (start us, length us, event | category | flops | bytes accessed | tf_op | source)
XLA Modules:
  0.0 32.0 jit_solution(14124294613450919932)
XLA Ops:
  0.0 0.0 copy-start.2
  0.0 1.1 %copy-done.2 = bf16[96,4096]{1,0:T(8,128)(2,1)S(1)} copy-done((bf16[96,4096]{1,0:T(8,128)(2,1)S(1)}, bf16[96,4096]{1,0:T(8,128)(2,1)}, u32[]{:S(2)}) %copy-start.2) | copy-done | bytes 786456
  1.1 0.2 partial_squares.1.own_ref
  1.3 0.5 %collective-permute-start = (f32[96,128]{1,0:T(8,128)S(1)}, f32[96,128]{1,0:T(8,128)S(1)}, u32[]{:S(2)}, u32[]{:S(2)}) collective-permute-start(f32[96,128]{1,0:T(8,128)S(1)} %partial_squares.1.own_ref), channel_id=1, source_target_pairs={{0,1},{1,0},{2,3},{3,2},{4,5},{5,4},{6,7},{7,6},{8,9},{9,8},{10,11... | collective-permute-start | bytes 147464 | tf_op jit(solution)/shard_map/ppermute | solution.py:402
  1.8 0.0 copy-start
  1.8 0.9 %collective-permute-done.other_ref = f32[96,128]{1,0:T(8,128)S(1)} collective-permute-done((f32[96,128]{1,0:T(8,128)S(1)}, f32[96,128]{1,0:T(8,128)S(1)}, u32[]{:S(2)}, u32[]{:S(2)}) %collective-permute-start) | collective-permute-done | bytes 49184 | tf_op jit(solution)/shard_map/ppermute | solution.py:402
  2.7 0.0 copy-start.1
  2.7 2.6 %copy-done.1 = bf16[4096,512]{1,0:T(8,128)(2,1)S(1)} copy-done((bf16[4096,512]{1,0:T(8,128)(2,1)S(1)}, bf16[4096,512]{1,0:T(8,128)(2,1)}, u32[]{:S(2)}) %copy-start.1) | copy-done | bytes 4194328
  5.3 0.0 copy-start.3
  5.3 1.1 %copy-done.3 = bf16[96,4096]{1,0:T(8,128)(2,1)S(1)} copy-done((bf16[96,4096]{1,0:T(8,128)(2,1)S(1)}, bf16[96,4096]{1,0:T(8,128)(2,1)}, u32[]{:S(2)}) %copy-start.3) | copy-done | bytes 786456
  6.4 0.0 copy-start.7
  6.4 0.7 %copy-done.7 = f32[4096]{0:T(1024)S(1)} copy-done((f32[4096]{0:T(1024)S(1)}, f32[4096]{0:T(1024)}, u32[]{:S(2)}) %copy-start.7) | copy-done | bytes 16408
  7.1 0.0 copy-start.8
  7.1 0.0 copy-start.9
  7.1 0.0 copy-start.12
  7.1 0.9 %project_keys.1 = (bf16[96,4096]{1,0:T(8,128)(2,1)S(1)}, f32[96,256]{1,0:T(8,128)S(1)}, f32[96,256]{1,0:T(8,128)S(1)}) custom-call(s32[1]{0:T(128)} %bitcast.2.index_ref, bf16[96,4096]{1,0:T(8,128)(2,1)S(1)} %copy-done.3, f32[96,128]{1,0:T(8,128)S(1)} %partial_squares.1.own_ref, f32[96,128]{1,0:T(8,128)S(1)} %collective-permute-done.other_ref, ...), custom_call_target="tpu_custom_call" | custom-call | flops 402653184 | bytes 4194304 | tf_op jit(solution)/shard_map/project_keys/pallas_call | solution.py:84
  8.0 0.0 copy-start.4
  8.0 0.0 copy-start.6
  8.0 0.0 copy-start.10
  8.1 0.0 copy-start.11
  8.1 0.0 copy-start.5
  8.1 0.1 collective-permute-start.1
  8.2 0.0 copy-done
  8.2 0.8 %project_values.1 = (f32[96,256]{1,0:T(8,128)S(1)}, f32[96,256]{1,0:T(8,128)S(1)}) custom-call(s32[1]{0:T(128)} %bitcast.2.index_ref, bf16[96,4096]{1,0:T(8,128)(2,1)S(1)} %get-tuple-element.12.normed_ref, bf16[4096,512]{1,0:T(8,128)(2,1)S(1)} %copy-done), custom_call_target="tpu_custom_call" | custom-call | flops 402653184 | bytes 4194304 | tf_op jit(solution)/shard_map/project_values/pallas_call | solution.py:99
  9.0 0.5 %collective-permute-start.2 = (f32[96,256]{1,0:T(8,128)S(1)}, f32[96,256]{1,0:T(8,128)S(1)}, u32[]{:S(2)}, u32[]{:S(2)}) collective-permute-start(f32[96,256]{1,0:T(8,128)S(1)} %get-tuple-element.14), channel_id=1, source_target_pairs={{0,1},{1,0},{2,3},{3,2},{4,5},{5,4},{6,7},{7,6},{8,9},{9,8},{10,11... | collective-permute-start | bytes 294920 | tf_op jit(solution)/shard_map/ppermute | solution.py:408
  9.5 0.0 collective-permute-done.1.got_key_ref
  9.5 0.9 %collective-permute-done.2.got_value_ref = f32[96,256]{1,0:T(8,128)S(1)} collective-permute-done((f32[96,256]{1,0:T(8,128)S(1)}, f32[96,256]{1,0:T(8,128)S(1)}, u32[]{:S(2)}, u32[]{:S(2)}) %collective-permute-start.2) | collective-permute-done | bytes 98336 | tf_op jit(solution)/shard_map/ppermute | solution.py:408
  10.5 0.0 copy-done.8
  10.5 0.0 copy-done.9
  10.5 0.0 copy-done.12
  10.5 1.1 %pack.1 = bf16[16,72,128]{2,1,0:T(8,128)(2,1)} custom-call(s32[1]{0:T(128)} %bitcast.here_ref, s32[1,96]{1,0:T(1,128)S(1)} %bitcast.9, f32[96,256]{1,0:T(8,128)S(1)} %get-tuple-element.10.kept_key_ref, f32[96,256]{1,0:T(8,128)S(1)} %collective-permute-done.1.got_key_ref, f32[96,256]{1,0:T(8,128)S(1)} %get-tuple-element.13.kept_value_ref, ...), custom_call_target="tpu_custom_call" | custom-call | flops 25165824 | bytes 393216 | tf_op jit(solution)/shard_map/pack/pallas_call | solution.py:163
  11.6 8.2 %all-to-all-start = ((bf16[16,72,128]{2,1,0:T(8,128)(2,1)}), bf16[16,72,128]{2,1,0:T(8,128)(2,1)S(1)}, u32[]{:S(2)}, u32[]{:S(2)}) async-start(bf16[16,72,128]{2,1,0:T(8,128)(2,1)} %pack.1), calls=%async_computation | async-start | bytes 589824 | tf_op jit(solution)/shard_map/all_to_all | solution.py:413
  19.8 0.0 copy-done.4
  19.8 0.0 copy-done.6
  19.8 0.0 copy-done.10
  19.8 0.0 copy-done.11
  19.8 1.0 %cached_scores.1.score_ref = f32[2,64,128]{2,1,0:T(8,128)S(1)} custom-call(s32[8]{0:T(128)S(1)} %copy-done.10, s32[8]{0:T(128)S(1)} %copy-done.11, bf16[8,2048]{1,0:T(8,128)(2,1)S(1)} %copy-done.6, bf16[8,128,256]{2,1,0:T(8,128)(2,1)S(1)} %copy-done.4), custom_call_target="tpu_custom_call" | custom-call | flops 33554432 | bytes 524288 | tf_op jit(solution)/shard_map/cached_scores/pallas_call | solution.py:205
  20.8 9.9 %all-to-all-done.got_ref = bf16[16,72,128]{2,1,0:T(8,128)(2,1)S(1)} async-done(((bf16[16,72,128]{2,1,0:T(8,128)(2,1)}), bf16[16,72,128]{2,1,0:T(8,128)(2,1)S(1)}, u32[]{:S(2)}, u32[]{:S(2)}) %all-to-all-start) | async-done | bytes 294944 | tf_op jit(solution)/shard_map/all_to_all | solution.py:413
  30.8 0.0 copy-done.5
  30.8 1.2 %attend.1 = bf16[8,2048]{1,0:T(8,128)(2,1)} custom-call(bf16[16,72,128]{2,1,0:T(8,128)(2,1)S(1)} %all-to-all-done.got_ref, bf16[8,2048]{1,0:T(8,128)(2,1)S(1)} %copy-done.6, f32[2,64,128]{2,1,0:T(8,128)S(1)} %cached_scores.1.score_ref, bf16[8,128,256]{2,1,0:T(8,128)(2,1)S(1)} %copy-done.5), custom_call_target="tpu_custom_call" | custom-call | flops 67108864 | bytes 524288 | tf_op jit(solution)/shard_map/attend/pallas_call | solution.py:257
Async XLA Ops:
  0.0 1.1 %copy-start.2 = (bf16[96,4096]{1,0:T(8,128)(2,1)S(1)}, bf16[96,4096]{1,0:T(8,128)(2,1)}, u32[]{:S(2)}) copy-start(bf16[96,4096]{1,0:T(8,128)(2,1)} %frames_ref.3) | copy-start | bytes 2359300
  1.3 1.4 %collective-permute-start = (f32[96,128]{1,0:T(8,128)S(1)}, f32[96,128]{1,0:T(8,128)S(1)}, u32[]{:S(2)}, u32[]{:S(2)}) collective-permute-start(f32[96,128]{1,0:T(8,128)S(1)} %partial_squares.1.own_ref), channel_id=1, source_target_pairs={{0,1},{1,0},{2,3},{3,2},{4,5},{5,4},{6,7},{7,6},{8,9},{9,8},{10,11... | collective-permute-start | bytes 147464 | tf_op jit(solution)/shard_map/ppermute | solution.py:402
  1.8 6.4 %copy-start = (bf16[4096,512]{1,0:T(8,128)(2,1)S(1)}, bf16[4096,512]{1,0:T(8,128)(2,1)}, u32[]{:S(2)}) copy-start(bf16[4096,512]{1,0:T(8,128)(2,1)} %w_ref.3) | copy-start | bytes 12582916
  2.7 2.6 %copy-start.1 = (bf16[4096,512]{1,0:T(8,128)(2,1)S(1)}, bf16[4096,512]{1,0:T(8,128)(2,1)}, u32[]{:S(2)}) copy-start(bf16[4096,512]{1,0:T(8,128)(2,1)} %w_ref.2) | copy-start | bytes 12582916
  5.3 1.1 %copy-start.3 = (bf16[96,4096]{1,0:T(8,128)(2,1)S(1)}, bf16[96,4096]{1,0:T(8,128)(2,1)}, u32[]{:S(2)}) copy-start(bf16[96,4096]{1,0:T(8,128)(2,1)} %frames_ref.3) | copy-start | bytes 2359300
  6.4 0.7 %copy-start.7 = (f32[4096]{0:T(1024)S(1)}, f32[4096]{0:T(1024)}, u32[]{:S(2)}) copy-start(f32[4096]{0:T(1024)} %param.14) | copy-start | bytes 49156
  7.1 3.4 %copy-start.8 = (f32[256]{0:T(256)S(1)}, f32[256]{0:T(256)}, u32[]{:S(2)}) copy-start(f32[256]{0:T(256)} %param.17) | copy-start | bytes 3076
  7.1 3.4 %copy-start.9 = (f32[256]{0:T(256)S(1)}, f32[256]{0:T(256)}, u32[]{:S(2)}) copy-start(f32[256]{0:T(256)} %param.18) | copy-start | bytes 3076
  7.1 3.4 %copy-start.12 = (s32[96]{0:T(128)S(1)}, s32[96]{0:T(128)}, u32[]{:S(2)}) copy-start(s32[96]{0:T(128)} %param.13) | copy-start | bytes 1156
  8.0 11.8 %copy-start.4 = (bf16[8,128,256]{2,1,0:T(8,128)(2,1)S(1)}, bf16[8,128,256]{2,1,0:T(8,128)(2,1)}, u32[]{:S(2)}) copy-start(bf16[8,128,256]{2,1,0:T(8,128)(2,1)} %key_ref.1) | copy-start | bytes 1572868
  8.0 11.8 %copy-start.6 = (bf16[8,2048]{1,0:T(8,128)(2,1)S(1)}, bf16[8,2048]{1,0:T(8,128)(2,1)}, u32[]{:S(2)}) copy-start(bf16[8,2048]{1,0:T(8,128)(2,1)} %queries_ref.3) | copy-start | bytes 98308
  8.0 11.8 %copy-start.10 = (s32[8]{0:T(128)S(1)}, s32[8]{0:T(128)}, u32[]{:S(2)}) copy-start(s32[8]{0:T(128)} %start_ref.1) | copy-start | bytes 100
  8.1 11.8 %copy-start.11 = (s32[8]{0:T(128)S(1)}, s32[8]{0:T(128)}, u32[]{:S(2)}) copy-start(s32[8]{0:T(128)} %len_ref.1) | copy-start | bytes 100
  8.1 22.7 %copy-start.5 = (bf16[8,128,256]{2,1,0:T(8,128)(2,1)S(1)}, bf16[8,128,256]{2,1,0:T(8,128)(2,1)}, u32[]{:S(2)}) copy-start(bf16[8,128,256]{2,1,0:T(8,128)(2,1)} %cache_ref.1) | copy-start | bytes 1572868
  8.1 1.5 %collective-permute-start.1 = (f32[96,256]{1,0:T(8,128)S(1)}, f32[96,256]{1,0:T(8,128)S(1)}, u32[]{:S(2)}, u32[]{:S(2)}) collective-permute-start(f32[96,256]{1,0:T(8,128)S(1)} %get-tuple-element.11), channel_id=1, source_target_pairs={{0,1},{1,0},{2,3},{3,2},{4,5},{5,4},{6,7},{7,6},{8,9},{9,8},{10,11... | collective-permute-start | bytes 294920 | tf_op jit(solution)/shard_map/ppermute | solution.py:406
  9.0 1.5 %collective-permute-start.2 = (f32[96,256]{1,0:T(8,128)S(1)}, f32[96,256]{1,0:T(8,128)S(1)}, u32[]{:S(2)}, u32[]{:S(2)}) collective-permute-start(f32[96,256]{1,0:T(8,128)S(1)} %get-tuple-element.14), channel_id=1, source_target_pairs={{0,1},{1,0},{2,3},{3,2},{4,5},{5,4},{6,7},{7,6},{8,9},{9,8},{10,11... | collective-permute-start | bytes 294920 | tf_op jit(solution)/shard_map/ppermute | solution.py:408
  11.6 19.2 %all-to-all-start = ((bf16[16,72,128]{2,1,0:T(8,128)(2,1)}), bf16[16,72,128]{2,1,0:T(8,128)(2,1)S(1)}, u32[]{:S(2)}, u32[]{:S(2)}) async-start(bf16[16,72,128]{2,1,0:T(8,128)(2,1)} %pack.1), calls=%async_computation | async-start | bytes 589824 | tf_op jit(solution)/shard_map/all_to_all | solution.py:413

commit v2 on v1

--- a/solution.py
+++ b/solution.py
@@ -29,101 +29,127 @@
     return jnp.dot(a, b, preferred_element_type=jnp.float32)
 
 
-def squares_kernel(frames_ref, out_ref):
-    columns = frames_ref.shape[1]
+SMEM = pl.BlockSpec(memory_space=pltpu.SMEM)
+VMEM = pl.BlockSpec(memory_space=pltpu.VMEM)
+HBM = pl.BlockSpec(memory_space=pltpu.HBM)
+
+
+def in_hbm(array):
+    return pltpu.with_memory_space_constraint(array, pltpu.HBM)
+
+
+def squares_kernel(frames_ref, out_ref, held_ref, arrived):
+    chunks, columns = arrived.shape[0], frames_ref.shape[1]
+    wide = columns // chunks
+    copies = []
+    for chunk in range(chunks):
+        part = (slice(None), pl.ds(chunk * wide, wide))
+        copies.append(
+            pltpu.make_async_copy(frames_ref.at[part], held_ref.at[part], arrived.at[chunk])
+        )
+        copies[-1].start()
     total = None
-    for at in range(0, columns, HEAD):
-        part = frames_ref[:, at : at + HEAD].astype(jnp.float32)
-        part = part * part
-        total = part if total is None else total + part
+    for chunk in range(chunks):
+        copies[chunk].wait()
+        for at in range(chunk * wide, (chunk + 1) * wide, HEAD):
+            part = held_ref[:, at : at + HEAD].astype(jnp.float32)
+            part = part * part
+            total = part if total is None else total + part
     out_ref[...] = total
 
 
 def partial_squares(frames):
     rows, columns = frames.shape
+    chunks = 2 if columns % (2 * HEAD) == 0 else 1
     return pl.pallas_call(
         squares_kernel,
-        out_shape=jax.ShapeDtypeStruct((rows, HEAD), jnp.float32),
+        out_shape=(jax.ShapeDtypeStruct((rows, HEAD), jnp.float32), jax.ShapeDtypeStruct(frames.shape, frames.dtype)),
+        in_specs=[HBM],
+        out_specs=(VMEM, VMEM),
+        scratch_shapes=[pltpu.SemaphoreType.DMA((chunks,))],
         compiler_params=params(8),
         cost_estimate=cost(2 * rows * columns, 2 * rows * columns),
         name="partial_squares",
-    )(frames)
-
-
-def halves(index_ref, normed, w_ref, sent_ref, kept_ref):
-    mine = index_ref[0]
-    width = sent_ref.shape[1]
-    for half, out_ref in ((1 - mine, sent_ref), (mine, kept_ref)):
-        columns = pl.ds(pl.multiple_of(half * width, width), width)
-        out_ref[...] = dot(normed, w_ref[:, columns])
-
-
-def key_kernel(
-    features, index_ref, frames_ref, own_ref, other_ref, gain_ref, w_ref, normed_ref, sent_ref, kept_ref
+    )(in_hbm(frames))
+
+
+def products(normed_ref, half, key_ref, value_ref, out_ref):
+    width = key_ref.shape[1] // 2
+    columns = pl.ds(pl.multiple_of(half * width, width), width)
+    out_ref[:, :width] = dot(normed_ref[...], key_ref[:, columns])
+    out_ref[:, width:] = dot(normed_ref[...], value_ref[:, columns])
+
+
+def send_kernel(
+    features, index_ref, frames_ref, own_ref, other_ref, gain_ref, key_ref, value_ref, normed_ref, out_ref
 ):
     squares = jnp.sum(own_ref[...] + other_ref[...], axis=1, keepdims=True)
     inverse_rms = lax.rsqrt(squares / features + epsilon)
     normed_ref[...] = (
         frames_ref[...].astype(jnp.float32) * inverse_rms * gain_ref[...]
     ).astype(jnp.bfloat16)
-    halves(index_ref, normed_ref[...], w_ref, sent_ref, kept_ref)
-
-
-def value_kernel(index_ref, normed_ref, w_ref, sent_ref, kept_ref):
-    halves(index_ref, normed_ref[...], w_ref, sent_ref, kept_ref)
-
-
-SMEM = pl.BlockSpec(memory_space=pltpu.SMEM)
-VMEM = pl.BlockSpec(memory_space=pltpu.VMEM)
-
-
-def project_keys(index, frames, own, other, gain, w, features):
+    products(normed_ref, 1 - index_ref[0], key_ref, value_ref, out_ref)
+
+
+def send_products(index, frames, own, other, gain, key, value, features):
     rows, columns = frames.shape
-    width = w.shape[1] // 2
-    half = jax.ShapeDtypeStruct((rows, width), jnp.float32)
-    return pl.pallas_call(
-        functools.partial(key_kernel, features),
-        out_shape=(jax.ShapeDtypeStruct(frames.shape, jnp.bfloat16), half, half),
-        in_specs=[SMEM] + [VMEM] * 5,
-        out_specs=(VMEM, VMEM, VMEM),
-        compiler_params=params(16),
-        cost_estimate=cost(4 * rows * columns * width, 2 * w.size),
-        name="project_keys",
-    )(index, frames, own, other, gain, w)
-
-
-def project_values(index, normed, w):
-    rows, columns = normed.shape
-    width = w.shape[1] // 2
-    half = jax.ShapeDtypeStruct((rows, width), jnp.float32)
-    return pl.pallas_call(
-        value_kernel,
-        out_shape=(half, half),
-        in_specs=[SMEM] + [VMEM] * 2,
+    width = key.shape[1]
+    return pl.pallas_call(
+        functools.partial(send_kernel, features),
+        out_shape=(
+            jax.ShapeDtypeStruct(frames.shape, jnp.bfloat16),
+            jax.ShapeDtypeStruct((rows, width), jnp.float32),
+        ),
+        in_specs=[SMEM] + [VMEM] * 6,
         out_specs=(VMEM, VMEM),
         compiler_params=params(16),
-        cost_estimate=cost(4 * rows * columns * width, 2 * w.size),
-        name="project_values",
-    )(index, normed, w)
-
-
-def pack_kernel(
+        cost_estimate=cost(2 * rows * columns * width, 2 * key.size),
+        name="send_products",
+    )(index, frames, own, other, gain, key, value)
+
+
+def keep_kernel(index_ref, normed_ref, key_ref, value_ref, out_ref):
+    products(normed_ref, index_ref[0], key_ref, value_ref, out_ref)
+
+
+def keep_products(index, normed, key, value):
+    rows, columns = normed.shape
+    width = key.shape[1]
+    return pl.pallas_call(
+        keep_kernel,
+        out_shape=jax.ShapeDtypeStruct((rows, width), jnp.float32),
+        in_specs=[SMEM] + [VMEM] * 3,
+        out_specs=VMEM,
+        compiler_params=params(16),
+        cost_estimate=cost(2 * rows * columns * width, 2 * key.size),
+        name="keep_products",
+    )(index, normed, key, value)
+
+
+def route_kernel(
     per_shard,
     capacity,
     here_ref,
     session_ref,
-    kept_key_ref,
-    got_key_ref,
-    kept_value_ref,
-    got_value_ref,
-    key_bias_ref,
-    value_bias_ref,
-    out_ref,
+    w_key_ref,
+    w_value_ref,
+    pick_ref,
+    ids_ref,
+    held_key_ref,
+    held_value_ref,
+    held_session,
+    arrived,
 ):
-    partitions, _, _ = out_ref.shape
-    rows, width = kept_key_ref.shape
-    slots = partitions * capacity
-    session = session_ref[...]
+    copies = []
+    for at, (source, held) in enumerate(
+        ((session_ref, held_session), (w_key_ref, held_key_ref), (w_value_ref, held_value_ref))
+    ):
+        copies.append(pltpu.make_async_copy(source, held, arrived.at[at]))
+        copies[-1].start()
+    copies[0].wait()
+    slots, rows = pick_ref.shape
+    partitions = slots // capacity
+    session = held_session[...]
     target = lax.div(session, per_shard)
     local = session - target * per_shard
     to = lax.broadcasted_iota(jnp.int32, (partitions, rows), 0) == target
@@ -134,41 +160,78 @@
     ahead = dot(to.astype(jnp.bfloat16), earlier.astype(jnp.bfloat16))
     order = jnp.sum(to * ahead, axis=0, keepdims=True).astype(jnp.int32)
     place = lax.broadcasted_iota(jnp.int32, (slots, rows), 0)
-    pick = (place == target * capacity + order).astype(jnp.bfloat16)
+    pick_ref[...] = (place == target * capacity + order).astype(jnp.bfloat16)
     lane = (place == here_ref[0] * capacity + order).astype(jnp.bfloat16)
     ids = nt_dot((to * (local + 1).astype(jnp.float32)).astype(jnp.bfloat16), lane)
-    key = (kept_key_ref[...] + got_key_ref[...] + key_bias_ref[...]).astype(jnp.bfloat16)
-    value = (kept_value_ref[...] + got_value_ref[...] + value_bias_ref[...]).astype(jnp.bfloat16)
+    row = lax.broadcasted_iota(jnp.int32, ids_ref.shape, 1)
+    block = jnp.zeros(ids_ref.shape, jnp.float32)
+    for j in range(slots // HEAD):
+        part = ids[:, j * HEAD : (j + 1) * HEAD]
+        block = jnp.where(row == j, part[:, None, :], block)
+    ids_ref[...] = block
+    for copy in copies[1:]:
+        copy.wait()
+
+
+def route(here, session, w_key, w_value, partitions, per_shard, capacity):
+    rows, slots = session.shape[1], partitions * capacity
+    id_rows = -(-slots // (8 * HEAD)) * 8
+    return pl.pallas_call(
+        functools.partial(route_kernel, per_shard, capacity),
+        out_shape=(
+            jax.ShapeDtypeStruct((slots, rows), jnp.bfloat16),
+            jax.ShapeDtypeStruct((partitions, id_rows, HEAD), jnp.float32),
+            jax.ShapeDtypeStruct(w_key.shape, w_key.dtype),
+            jax.ShapeDtypeStruct(w_value.shape, w_value.dtype),
+        ),
+        in_specs=[SMEM, HBM, HBM, HBM],
+        out_specs=(VMEM, VMEM, VMEM, VMEM),
+        scratch_shapes=[pltpu.VMEM(session.shape, session.dtype), pltpu.SemaphoreType.DMA((3,))],
+        compiler_params=params(16),
+        cost_estimate=cost(4 * rows * rows * slots, 2 * w_key.size),
+        name="route",
+    )(here, in_hbm(session), in_hbm(w_key), in_hbm(w_value))
+
+
+def pack_kernel(
+    pick_ref,
+    ids_ref,
+    kept_ref,
+    got_ref,
+    key_bias_ref,
+    value_bias_ref,
+    out_ref,
+):
+    partitions = out_ref.shape[0]
+    slots = pick_ref.shape[0]
+    capacity = slots // partitions
+    width = key_bias_ref.shape[1]
+    sums = kept_ref[...] + got_ref[...]
+    key = (sums[:, :width] + key_bias_ref[...]).astype(jnp.bfloat16)
+    value = (sums[:, width:] + value_bias_ref[...]).astype(jnp.bfloat16)
     at = 0
     for source in (key, value):
-        laid = dot(pick, source).astype(jnp.bfloat16).reshape(partitions, capacity, width)
+        laid = dot(pick_ref[...], source).astype(jnp.bfloat16).reshape(partitions, capacity, width)
         for column in range(0, width, HEAD):
             out_ref[:, at : at + capacity, :] = laid[:, :, column : column + HEAD]
             at += capacity
-    ids = ids.astype(jnp.bfloat16)
-    extra = out_ref.shape[1] - at
-    row = lax.broadcasted_iota(jnp.int32, (partitions, extra, HEAD), 1)
-    block = jnp.zeros((partitions, extra, HEAD), jnp.float32)
-    for j in range(slots // HEAD):
-        part = ids[:, j * HEAD : (j + 1) * HEAD].astype(jnp.float32)
-        block = jnp.where(row == j, part[:, None, :], block)
-    out_ref[:, at:, :] = block.astype(jnp.bfloat16)
-
-
-def pack(here, session, kept_key, got_key, kept_value, got_value, key_bias, value_bias, sizes):
-    partitions, per_shard, capacity = sizes
-    rows, width = kept_key.shape
-    id_rows = -(-partitions * capacity // HEAD)
-    block = 2 * width // HEAD * capacity + -(-id_rows // 8) * 8
-    return pl.pallas_call(
-        functools.partial(pack_kernel, per_shard, capacity),
+    out_ref[:, at:, :] = ids_ref[...].astype(jnp.bfloat16)
+
+
+def pack(pick, ids, kept, got, key_bias, value_bias):
+    rows, width = kept.shape
+    partitions, id_rows, _ = ids.shape
+    capacity = pick.shape[0] // partitions
+    block = width // HEAD * capacity + id_rows
+    return pl.pallas_call(
+        pack_kernel,
         out_shape=jax.ShapeDtypeStruct((partitions, block, HEAD), jnp.bfloat16),
-        in_specs=[SMEM] + [VMEM] * 7,
+        in_specs=[VMEM] * 6,
         out_specs=VMEM,
         compiler_params=params(8),
-        cost_estimate=cost(4 * rows * width * partitions * capacity, 16 * rows * width),
+        cost_estimate=cost(2 * rows * width * partitions * capacity, 8 * rows * width),
         name="pack",
-    )(here, session, kept_key, got_key, kept_value, got_value, key_bias, value_bias)
+    )(pick, ids, kept, got, key_bias, value_bias)
 
 
 def queries_of(queries_ref, head):
@@ -179,7 +242,7 @@
     return jnp.concatenate(columns, axis=0).astype(jnp.bfloat16)
 
 
-def cached_kernel(start_ref, len_ref, queries_ref, key_ref, out_ref):
+def cached_kernel(start_ref, len_ref, queries_ref, key_ref, out_ref, laid_ref):
     heads, rows, window = out_ref.shape
     sessions = queries_ref.shape[0]
     row_session = lax.broadcasted_iota(jnp.int32, (rows, window), 0) % sessions
@@ -191,6 +254,7 @@
         live.append(since < len_ref[session])
     for head in range(heads):
         query = queries_of(queries_ref, head)
+        laid_ref[head] = query
         total = jnp.full((rows, window), -jnp.inf, jnp.float32)
         for session in range(sessions):
             key = key_ref[session, :, head * HEAD : (head + 1) * HEAD]
@@ -204,9 +268,12 @@
     heads = width // HEAD
     return pl.pallas_call(
         cached_kernel,
-        out_shape=jax.ShapeDtypeStruct((heads, GROUP * sessions, window), jnp.float32),
+        out_shape=(
+            jax.ShapeDtypeStruct((heads, GROUP * sessions, window), jnp.float32),
+            jax.ShapeDtypeStruct((heads, GROUP * sessions, HEAD), jnp.bfloat16),
+        ),
         in_specs=[SMEM, SMEM, VMEM, VMEM],
-        out_specs=VMEM,
+        out_specs=(VMEM, VMEM),
         compiler_params=params(8),
         cost_estimate=cost(2 * GROUP * sessions * cache_key.size, 2 * cache_key.size),
         name="cached_scores",
@@ -215,7 +282,7 @@
 
 def attend_kernel(capacity, got_ref, queries_ref, score_ref, cache_ref, out_ref):
     heads, rows, window = score_ref.shape
-    sessions = queries_ref.shape[0]
+    sessions = cache_ref.shape[0]
     partitions = got_ref.shape[0]
     slots = partitions * capacity
     at = 2 * heads * capacity
@@ -229,7 +296,7 @@
     own = lax.broadcasted_iota(jnp.int32, (rows, slots), 0) % sessions + 1 == ids
     row_session = lax.broadcasted_iota(jnp.int32, (rows, window), 0) % sessions
     for head in range(heads):
-        query = queries_of(queries_ref, head)
+        query = queries_ref[head]
         key = got_ref[:, head * capacity : (head + 1) * capacity, :].reshape(slots, HEAD)
         first = (heads + head) * capacity
         value = got_ref[:, first : first + capacity, :].reshape(slots, HEAD)
@@ -256,11 +323,13 @@
 def attend(got, queries, scores, cache_value, capacity):
     return pl.pallas_call(
         functools.partial(attend_kernel, capacity),
-        out_shape=jax.ShapeDtypeStruct(queries.shape, jnp.bfloat16),
+        out_shape=jax.ShapeDtypeStruct(
+            (cache_value.shape[0], queries.shape[0] * GROUP * HEAD), jnp.bfloat16
+        ),
         in_specs=[VMEM] * 4,
         out_specs=VMEM,
         compiler_params=params(8),
-        cost_estimate=cost(4 * queries.shape[0] * GROUP * cache_value.size, 2 * cache_value.size),
+        cost_estimate=cost(4 * queries.shape[1] * cache_value.size, 2 * cache_value.size),
         name="attend",
     )(got, queries, scores, cache_value)
 
@@ -398,21 +467,20 @@
     swap = [(0, 1), (1, 0)]
     index = lax.axis_index("mp").astype(jnp.int32).reshape(1)
     here = lax.axis_index(("grp", "seq")).astype(jnp.int32).reshape(1)
-    own = partial_squares(frames)
+    own, held = partial_squares(frames)
     other = lax.ppermute(own, "mp", swap)
-    normed, sent_key, kept_key = project_keys(
-        index, frames, own, other, ln_gain[None, :], w_key, frames.shape[1] * shares
-    )
-    got_key = lax.ppermute(sent_key, "mp", swap)
-    sent_value, kept_value = project_values(index, normed, w_value)
-    got_value = lax.ppermute(sent_value, "mp", swap)
-    blocks = pack(
-        here, token_session[None, :], kept_key, got_key, kept_value, got_value, k_bias[None, :],
-        v_bias[None, :], (partitions, per_shard, capacity),
-    )
+    pick, ids, held_key, held_value = route(
+        here, token_session[None, :], w_key, w_value, partitions, per_shard, capacity
+    )
+    normed, sent = send_products(
+        index, held, own, other, ln_gain[None, :], held_key, held_value, frames.shape[1] * shares
+    )
+    arrived = lax.ppermute(sent, "mp", swap)
+    kept = keep_products(index, normed, held_key, held_value)
+    blocks = pack(pick, ids, kept, arrived, k_bias[None, :], v_bias[None, :])
     got = lax.all_to_all(blocks, ("grp", "seq"), split_axis=0, concat_axis=0, tiled=True)
-    scores = cached_scores(cache_start, cache_len, queries, cache_key)
-    return attend(got, queries, scores, cache_value, capacity)
+    scores, laid = cached_scores(cache_start, cache_len, queries, cache_key)
+    return attend(got, laid, scores, cache_value, capacity)
 
 
 def solution(mesh):

time: 32.4 us -> 29.3 us (0.904)
  local copies, waits for them, and re-layouts: 5.6 us -> 0.04 us
  Pallas kernels: 5.17 us -> 9.59 us
  waiting for transfers between devices: 11.8 us -> 10.6 us
  starting transfers between devices: 9.37 us -> 8.71 us
    unnamed x26 -> x16, local copies, waits for them, and re-layouts: 5.6 us -> 0.04 us
    pallas_call x5 -> x6, Pallas kernels: 3.94 us -> 8.36 us  [the longest x1 3.51 us: route(): pl.pallas_call(functools.partial(route_kernel, per_shard, capacity), out_...]
    ppermute x1, waiting for transfers between devices: 0.88 us -> 0.01 us  [local(): other = lax.ppermute(own, 'mp', swap)]
    ppermute x2 -> x1, starting transfers between devices: 0.66 us -> 0.15 us  [local(): arrived = lax.ppermute(sent, 'mp', swap)]
    ppermute x2 -> x1, waiting for transfers between devices: 0.94 us -> 0.48 us  [local(): arrived = lax.ppermute(sent, 'mp', swap)]
  transfers between devices with their start and end apart: 4 -> 3, of which waited for: 3 -> 2; matrix products, arithmetic and copies ran while one was open for 0% -> 0% of each run, Pallas kernels for 6% -> 18%
where the time goes in v2:
time: 29.3 us; the launch traced here: 29.1 us
  waiting for transfers between devices  10.6 us (36%)
  Pallas kernels  9.59 us (33%)
  starting transfers between devices  8.71 us (30%)
    all_to_all x1, waiting for transfers between devices, local(): lax.all_to_all(blocks, ('grp', 'seq'), split_axis=0, concat_axis=0, tiled...  10.2 us
    all_to_all x1, starting transfers between devices, local(): lax.all_to_all(blocks, ('grp', 'seq'), split_axis=0, concat_axis=0, tiled...  8.04 us
    pallas_call x1, Pallas kernels, route(): pl.pallas_call(functools.partial(route_kernel, per_shard, capacity), out_...  3.51 us
    pallas_call x1, Pallas kernels, attend(): pl.pallas_call(functools.partial(attend_kernel, capacity), out_shape=jax....  1.23 us
    pallas_call x1, Pallas kernels, partial_squares(): pl.pallas_call(squares_kernel, out_shape=(jax.ShapeDtypeStruct((rows, HEA...  1.21 us
    pallas_call x1, Pallas kernels, cached_scores(): pl.pallas_call(cached_kernel, out_shape=(jax.ShapeDtypeStruct((heads, GRO...  1 us
    pallas_call x1, Pallas kernels, pack(): pl.pallas_call(pack_kernel, out_shape=jax.ShapeDtypeStruct((partitions, b...  0.92 us
    pallas_call x1, Pallas kernels, send_products(): pl.pallas_call(functools.partial(send_kernel, features), out_shape=(jax.S...  0.88 us
  transfers between devices with their start and end apart: 3, of which 2 were waited for; matrix products, arithmetic and copies ran while one was open for 0% of the time, Pallas kernels for 18%

profile of v2, /device:TPU:0, one launch (start us, length us, event | category | flops | bytes accessed | tf_op | source)
XLA Modules:
  0.0 29.1 jit_solution(4552283016895427913)
XLA Ops:
  0.0 1.2 %partial_squares.1 = (f32[96,128]{1,0:T(8,128)S(1)}, bf16[96,4096]{1,0:T(8,128)(2,1)S(1)}) custom-call(bf16[96,4096]{1,0:T(8,128)(2,1)} %frames_ref.1), custom_call_target="tpu_custom_call" | custom-call | flops 786432 | bytes 786432 | tf_op jit(solution)/shard_map/partial_squares/pallas_call | solution.py:64
  1.2 0.5 %collective-permute-start = (f32[96,128]{1,0:T(8,128)S(1)}, f32[96,128]{1,0:T(8,128)S(1)}, u32[]{:S(2)}, u32[]{:S(2)}) collective-permute-start(f32[96,128]{1,0:T(8,128)S(1)} %get-tuple-element.18.own_ref), channel_id=1, source_target_pairs={{0,1},{1,0},{2,3},{3,2},{4,5},{5,4},{6,7},{7,6},{8,9},{9,8},{10,11... | collective-permute-start | bytes 147464 | tf_op jit(solution)/shard_map/ppermute | solution.py:471
  1.7 0.0 copy-start.3
  1.7 3.5 %route.1 = (bf16[256,96]{1,0:T(8,128)(2,1)S(1)}, f32[16,8,128]{2,1,0:T(8,128)S(1)}, bf16[4096,512]{1,0:T(8,128)(2,1)S(1)}, bf16[4096,512]{1,0:T(8,128)(2,1)S(1)}) custom-call(s32[1]{0:T(128)} %bitcast.here_ref, s32[1,96]{1,0:T(1,128)} %bitcast.9, bf16[4096,512]{1,0:T(8,128)(2,1)} %w_key_ref.1, bf16[4096,512]{1,0:T(8,128)(2,1)} %w_value_ref.1), custom_call_target="tpu_custom_call" | custom-call | flops 9437184 | bytes 4194304 | tf_op jit(solution)/shard_map/route/pallas_call | solution.py:179
  5.3 0.0 collective-permute-done.other_ref
  5.3 0.0 copy-done.3
  5.3 0.9 %send_products.1 = (bf16[96,4096]{1,0:T(8,128)(2,1)S(1)}, f32[96,512]{1,0:T(8,128)S(1)}) custom-call(s32[1]{0:T(128)} %bitcast.2.index_ref, bf16[96,4096]{1,0:T(8,128)(2,1)S(1)} %get-tuple-element.17.frames_ref, f32[96,128]{1,0:T(8,128)S(1)} %get-tuple-element.18.own_ref, f32[96,128]{1,0:T(8,128)S(1)} %collective-permute-done.other_ref, ...), custom_call_target="tpu_custom_call" | custom-call | flops 402653184 | bytes 4194304 | tf_op jit(solution)/shard_map/send_products/pallas_call | solution.py:97
  6.2 0.2 collective-permute-start.1
  6.3 0.0 copy-start.4
  6.3 0.0 copy-start.5
  6.3 0.0 copy-start
  6.3 0.0 copy-start.2
  6.3 0.0 copy-start.6
  6.3 0.0 copy-start.7
  6.4 0.0 copy-start.1
  6.4 0.8 %keep_products.1.kept_ref = f32[96,512]{1,0:T(8,128)S(1)} custom-call(s32[1]{0:T(128)} %bitcast.2.index_ref, bf16[96,4096]{1,0:T(8,128)(2,1)S(1)} %get-tuple-element.21.normed_ref, bf16[4096,512]{1,0:T(8,128)(2,1)S(1)} %get-tuple-element.19.key_ref, bf16[4096,512]{1,0:T(8,128)(2,1)S(1)} %get-tuple-element.20.value_ref), custom_call_target="tpu_custom_call" | custom-call | flops 402653184 | bytes 4194304 | tf_op jit(solution)/shard_map/keep_products/pallas_call | solution.py:118
  7.2 0.5 %collective-permute-done.1.got_ref = f32[96,512]{1,0:T(8,128)S(1)} collective-permute-done((f32[96,512]{1,0:T(8,128)S(1)}, f32[96,512]{1,0:T(8,128)S(1)}, u32[]{:S(2)}, u32[]{:S(2)}) %collective-permute-start.1) | collective-permute-done | bytes 196640 | tf_op jit(solution)/shard_map/ppermute | solution.py:478
  7.7 0.0 copy-done.4
  7.7 0.0 copy-done.5
  7.7 0.9 %pack.1 = bf16[16,72,128]{2,1,0:T(8,128)(2,1)} custom-call(bf16[256,96]{1,0:T(8,128)(2,1)S(1)} %get-tuple-element.15.pick_ref, f32[16,8,128]{2,1,0:T(8,128)S(1)} %get-tuple-element.16.ids_ref, f32[96,512]{1,0:T(8,128)S(1)} %keep_products.1.kept_ref, f32[96,512]{1,0:T(8,128)S(1)} %collective-permute-done.1.got_ref, f32[1,256]{1,0:T(1,128)S(1)} %bitcast.7, ...), custom_call_target="tpu_custom_call" | custom-call | flops 25165824 | bytes 393216 | tf_op jit(solution)/shard_map/pack/pallas_call | solution.py:226
  8.6 8.0 %all-to-all-start = ((bf16[16,72,128]{2,1,0:T(8,128)(2,1)}), bf16[16,72,128]{2,1,0:T(8,128)(2,1)S(1)}, u32[]{:S(2)}, u32[]{:S(2)}) async-start(bf16[16,72,128]{2,1,0:T(8,128)(2,1)} %pack.1), calls=%async_computation | async-start | bytes 589824 | tf_op jit(solution)/shard_map/all_to_all | solution.py:481
  16.6 0.0 copy-done
  16.7 0.0 copy-done.2
  16.7 0.0 copy-done.6
  16.7 0.0 copy-done.7
  16.7 1.0 %cached_scores.1 = (f32[2,64,128]{2,1,0:T(8,128)S(1)}, bf16[2,64,128]{2,1,0:T(8,128)(2,1)S(1)}) custom-call(s32[8]{0:T(128)S(1)} %copy-done.6, s32[8]{0:T(128)S(1)} %copy-done.7, bf16[8,2048]{1,0:T(8,128)(2,1)S(1)} %copy-done.2, bf16[8,128,256]{2,1,0:T(8,128)(2,1)S(1)} %copy-done), custom_call_target="tpu_custom_call" | custom-call | flops 33554432 | bytes 524288 | tf_op jit(solution)/shard_map/cached_scores/pallas_call | solution.py:269
  17.7 10.2 %all-to-all-done.got_ref = bf16[16,72,128]{2,1,0:T(8,128)(2,1)S(1)} async-done(((bf16[16,72,128]{2,1,0:T(8,128)(2,1)}), bf16[16,72,128]{2,1,0:T(8,128)(2,1)S(1)}, u32[]{:S(2)}, u32[]{:S(2)}) %all-to-all-start) | async-done | bytes 294944 | tf_op jit(solution)/shard_map/all_to_all | solution.py:481
  27.9 0.0 copy-done.1
  27.9 1.2 %attend.1 = bf16[8,2048]{1,0:T(8,128)(2,1)} custom-call(bf16[16,72,128]{2,1,0:T(8,128)(2,1)S(1)} %all-to-all-done.got_ref, bf16[2,64,128]{2,1,0:T(8,128)(2,1)S(1)} %get-tuple-element.23.queries_ref, f32[2,64,128]{2,1,0:T(8,128)S(1)} %get-tuple-element.24.score_ref, bf16[8,128,256]{2,1,0:T(8,128)(2,1)S(1)} %copy-done.1), custom_call_target="tpu_custom_call" | custom-call | flops 67108864 | bytes 524288 | tf_op jit(solution)/shard_map/attend/pallas_call | solution.py:324
Async XLA Ops:
  1.2 4.0 %collective-permute-start = (f32[96,128]{1,0:T(8,128)S(1)}, f32[96,128]{1,0:T(8,128)S(1)}, u32[]{:S(2)}, u32[]{:S(2)}) collective-permute-start(f32[96,128]{1,0:T(8,128)S(1)} %get-tuple-element.18.own_ref), channel_id=1, source_target_pairs={{0,1},{1,0},{2,3},{3,2},{4,5},{5,4},{6,7},{7,6},{8,9},{9,8},{10,11... | collective-permute-start | bytes 147464 | tf_op jit(solution)/shard_map/ppermute | solution.py:471
  1.7 3.5 %copy-start.3 = (f32[4096]{0:T(1024)S(1)}, f32[4096]{0:T(1024)}, u32[]{:S(2)}) copy-start(f32[4096]{0:T(1024)} %param.14) | copy-start | bytes 49156
  6.2 1.5 %collective-permute-start.1 = (f32[96,512]{1,0:T(8,128)S(1)}, f32[96,512]{1,0:T(8,128)S(1)}, u32[]{:S(2)}, u32[]{:S(2)}) collective-permute-start(f32[96,512]{1,0:T(8,128)S(1)} %get-tuple-element.22), channel_id=1, source_target_pairs={{0,1},{1,0},{2,3},{3,2},{4,5},{5,4},{6,7},{7,6},{8,9},{9,8},{10,11... | collective-permute-start | bytes 589832 | tf_op jit(solution)/shard_map/ppermute | solution.py:478
  6.3 1.4 %copy-start.4 = (f32[256]{0:T(256)S(1)}, f32[256]{0:T(256)}, u32[]{:S(2)}) copy-start(f32[256]{0:T(256)} %param.17) | copy-start | bytes 3076
  6.3 1.4 %copy-start.5 = (f32[256]{0:T(256)S(1)}, f32[256]{0:T(256)}, u32[]{:S(2)}) copy-start(f32[256]{0:T(256)} %param.18) | copy-start | bytes 3076
  6.3 10.3 %copy-start = (bf16[8,128,256]{2,1,0:T(8,128)(2,1)S(1)}, bf16[8,128,256]{2,1,0:T(8,128)(2,1)}, u32[]{:S(2)}) copy-start(bf16[8,128,256]{2,1,0:T(8,128)(2,1)} %key_ref.1) | copy-start | bytes 1572868
  6.3 10.3 %copy-start.2 = (bf16[8,2048]{1,0:T(8,128)(2,1)S(1)}, bf16[8,2048]{1,0:T(8,128)(2,1)}, u32[]{:S(2)}) copy-start(bf16[8,2048]{1,0:T(8,128)(2,1)} %queries_ref.1) | copy-start | bytes 98308
  6.3 10.3 %copy-start.6 = (s32[8]{0:T(128)S(1)}, s32[8]{0:T(128)}, u32[]{:S(2)}) copy-start(s32[8]{0:T(128)} %start_ref.1) | copy-start | bytes 100
  6.3 10.3 %copy-start.7 = (s32[8]{0:T(128)S(1)}, s32[8]{0:T(128)}, u32[]{:S(2)}) copy-start(s32[8]{0:T(128)} %len_ref.1) | copy-start | bytes 100
  6.4 21.5 %copy-start.1 = (bf16[8,128,256]{2,1,0:T(8,128)(2,1)S(1)}, bf16[8,128,256]{2,1,0:T(8,128)(2,1)}, u32[]{:S(2)}) copy-start(bf16[8,128,256]{2,1,0:T(8,128)(2,1)} %cache_ref.1) | copy-start | bytes 1572868
  8.6 19.3 %all-to-all-start = ((bf16[16,72,128]{2,1,0:T(8,128)(2,1)}), bf16[16,72,128]{2,1,0:T(8,128)(2,1)S(1)}, u32[]{:S(2)}, u32[]{:S(2)}) async-start(bf16[16,72,128]{2,1,0:T(8,128)(2,1)} %pack.1), calls=%async_computation | async-start | bytes 589824 | tf_op jit(solution)/shard_map/all_to_all | solution.py:481

commit v3 on v2

--- a/solution.py
+++ b/solution.py
@@ -213,19 +213,20 @@
     for source in (key, value):
         laid = dot(pick_ref[...], source).astype(jnp.bfloat16).reshape(partitions, capacity, width)
         for column in range(0, width, HEAD):
-            out_ref[:, at : at + capacity, :] = laid[:, :, column : column + HEAD]
-            at += capacity
-    out_ref[:, at:, :] = ids_ref[...].astype(jnp.bfloat16)
+            part = laid[:, :, column : column + HEAD]
+            out_ref[:, at : at + capacity // 2] = part.reshape(partitions, capacity // 2, 2, HEAD)
+            at += capacity // 2
+    out_ref[:, at] = ids_ref[:, :2, :].astype(jnp.bfloat16)
 
 
 def pack(pick, ids, kept, got, key_bias, value_bias):
     rows, width = kept.shape
     partitions, id_rows, _ = ids.shape
     capacity = pick.shape[0] // partitions
-    block = width // HEAD * capacity + id_rows
+    block = width // HEAD * capacity // 2 + 1
     return pl.pallas_call(
         pack_kernel,
-        out_shape=jax.ShapeDtypeStruct((partitions, block, HEAD), jnp.bfloat16),
+        out_shape=jax.ShapeDtypeStruct((partitions, block, 2, HEAD), jnp.bfloat16),
         in_specs=[VMEM] * 6,
         out_specs=VMEM,
         compiler_params=params(8),
@@ -285,10 +286,10 @@
     sessions = cache_ref.shape[0]
     partitions = got_ref.shape[0]
     slots = partitions * capacity
-    at = 2 * heads * capacity
+    at = heads * capacity
     ids = jnp.concatenate(
         [
-            jnp.sum(got_ref[:, at + j : at + j + 1, :].astype(jnp.float32), axis=0)
+            jnp.sum(got_ref[:, at, j : j + 1, :].astype(jnp.float32), axis=0)
             for j in range(slots // HEAD)
         ],
         axis=1,
@@ -297,9 +298,9 @@
     row_session = lax.broadcasted_iota(jnp.int32, (rows, window), 0) % sessions
     for head in range(heads):
         query = queries_ref[head]
-        key = got_ref[:, head * capacity : (head + 1) * capacity, :].reshape(slots, HEAD)
-        first = (heads + head) * capacity
-        value = got_ref[:, first : first + capacity, :].reshape(slots, HEAD)
+        key = got_ref[:, head * capacity // 2 : (head + 1) * capacity // 2].reshape(slots, HEAD)
+        first = (heads + head) * capacity // 2
+        value = got_ref[:, first : first + capacity // 2].reshape(slots, HEAD)
         cached = score_ref[head]
         fresh = jnp.where(own, nt_dot(query, key) * (HEAD**-0.5), -jnp.inf)
         largest = jnp.maximum(

time: 29.3 us -> 28.8 us (0.983)
  waiting for transfers between devices: 10.6 us -> 9.98 us
    all_to_all x1, waiting for transfers between devices: 10.2 us -> 9.5 us  [local(): lax.all_to_all(blocks, ('grp', 'seq'), split_axis=0, concat_axis=0, tiled...]
  transfers between devices with their start and end apart: 3 -> 3, of which waited for: 2 -> 2; matrix products, arithmetic and copies ran while one was open for 0% -> 0% of each run, Pallas kernels for 18% -> 19%
where the time goes in v3:
time: 28.8 us; the launch traced here: 28.6 us
  waiting for transfers between devices  9.98 us (35%)
  Pallas kernels  9.72 us (34%)
  starting transfers between devices  8.71 us (30%)
    all_to_all x1, waiting for transfers between devices, local(): lax.all_to_all(blocks, ('grp', 'seq'), split_axis=0, concat_axis=0, tiled...  9.5 us
    all_to_all x1, starting transfers between devices, local(): lax.all_to_all(blocks, ('grp', 'seq'), split_axis=0, concat_axis=0, tiled...  8.04 us
    pallas_call x1, Pallas kernels, route(): pl.pallas_call(functools.partial(route_kernel, per_shard, capacity), out_...  3.51 us
    pallas_call x1, Pallas kernels, attend(): pl.pallas_call(functools.partial(attend_kernel, capacity), out_shape=jax....  1.27 us
    pallas_call x1, Pallas kernels, partial_squares(): pl.pallas_call(squares_kernel, out_shape=(jax.ShapeDtypeStruct((rows, HEA...  1.21 us
    pallas_call x1, Pallas kernels, pack(): pl.pallas_call(pack_kernel, out_shape=jax.ShapeDtypeStruct((partitions, b...  1.01 us
    pallas_call x1, Pallas kernels, cached_scores(): pl.pallas_call(cached_kernel, out_shape=(jax.ShapeDtypeStruct((heads, GRO...  1 us
    pallas_call x1, Pallas kernels, send_products(): pl.pallas_call(functools.partial(send_kernel, features), out_shape=(jax.S...  0.88 us
  transfers between devices with their start and end apart: 3, of which 2 were waited for; matrix products, arithmetic and copies ran while one was open for 0% of the time, Pallas kernels for 19%

profile of v3, /device:TPU:0, one launch (start us, length us, event | category | flops | bytes accessed | tf_op | source)
XLA Modules:
  0.0 28.6 jit_solution(12795588999646381454)
XLA Ops:
  0.0 1.2 %partial_squares.1 = (f32[96,128]{1,0:T(8,128)S(1)}, bf16[96,4096]{1,0:T(8,128)(2,1)S(1)}) custom-call(bf16[96,4096]{1,0:T(8,128)(2,1)} %frames_ref.1), custom_call_target="tpu_custom_call" | custom-call | flops 786432 | bytes 786432 | tf_op jit(solution)/shard_map/partial_squares/pallas_call | solution.py:64
  1.2 0.5 %collective-permute-start = (f32[96,128]{1,0:T(8,128)S(1)}, f32[96,128]{1,0:T(8,128)S(1)}, u32[]{:S(2)}, u32[]{:S(2)}) collective-permute-start(f32[96,128]{1,0:T(8,128)S(1)} %get-tuple-element.18.own_ref), channel_id=1, source_target_pairs={{0,1},{1,0},{2,3},{3,2},{4,5},{5,4},{6,7},{7,6},{8,9},{9,8},{10,11... | collective-permute-start | bytes 147464 | tf_op jit(solution)/shard_map/ppermute | solution.py:472
  1.7 0.0 copy-start.3
  1.7 3.5 %route.1 = (bf16[256,96]{1,0:T(8,128)(2,1)S(1)}, f32[16,8,128]{2,1,0:T(8,128)S(1)}, bf16[4096,512]{1,0:T(8,128)(2,1)S(1)}, bf16[4096,512]{1,0:T(8,128)(2,1)S(1)}) custom-call(s32[1]{0:T(128)} %bitcast.here_ref, s32[1,96]{1,0:T(1,128)} %bitcast.9, bf16[4096,512]{1,0:T(8,128)(2,1)} %w_key_ref.1, bf16[4096,512]{1,0:T(8,128)(2,1)} %w_value_ref.1), custom_call_target="tpu_custom_call" | custom-call | flops 9437184 | bytes 4194304 | tf_op jit(solution)/shard_map/route/pallas_call | solution.py:179
  5.3 0.0 collective-permute-done.other_ref
  5.3 0.0 copy-done.3
  5.3 0.9 %send_products.1 = (bf16[96,4096]{1,0:T(8,128)(2,1)S(1)}, f32[96,512]{1,0:T(8,128)S(1)}) custom-call(s32[1]{0:T(128)} %bitcast.2.index_ref, bf16[96,4096]{1,0:T(8,128)(2,1)S(1)} %get-tuple-element.17.frames_ref, f32[96,128]{1,0:T(8,128)S(1)} %get-tuple-element.18.own_ref, f32[96,128]{1,0:T(8,128)S(1)} %collective-permute-done.other_ref, ...), custom_call_target="tpu_custom_call" | custom-call | flops 402653184 | bytes 4194304 | tf_op jit(solution)/shard_map/send_products/pallas_call | solution.py:97
  6.2 0.2 collective-permute-start.1
  6.3 0.0 copy-start.4
  6.3 0.0 copy-start.5
  6.3 0.0 copy-start.1
  6.3 0.0 copy-start.2
  6.3 0.0 copy-start.6
  6.3 0.0 copy-start.7
  6.4 0.0 copy-start
  6.4 0.8 %keep_products.1.kept_ref = f32[96,512]{1,0:T(8,128)S(1)} custom-call(s32[1]{0:T(128)} %bitcast.2.index_ref, bf16[96,4096]{1,0:T(8,128)(2,1)S(1)} %get-tuple-element.21.normed_ref, bf16[4096,512]{1,0:T(8,128)(2,1)S(1)} %get-tuple-element.19.key_ref, bf16[4096,512]{1,0:T(8,128)(2,1)S(1)} %get-tuple-element.20.value_ref), custom_call_target="tpu_custom_call" | custom-call | flops 402653184 | bytes 4194304 | tf_op jit(solution)/shard_map/keep_products/pallas_call | solution.py:118
  7.2 0.5 %collective-permute-done.1.got_ref = f32[96,512]{1,0:T(8,128)S(1)} collective-permute-done((f32[96,512]{1,0:T(8,128)S(1)}, f32[96,512]{1,0:T(8,128)S(1)}, u32[]{:S(2)}, u32[]{:S(2)}) %collective-permute-start.1) | collective-permute-done | bytes 196640 | tf_op jit(solution)/shard_map/ppermute | solution.py:479
  7.7 0.0 copy-done.4
  7.7 0.0 copy-done.5
  7.7 1.0 %pack.1 = bf16[16,33,2,128]{3,2,1,0:T(2,128)(2,1)} custom-call(bf16[256,96]{1,0:T(8,128)(2,1)S(1)} %get-tuple-element.15.pick_ref, f32[16,8,128]{2,1,0:T(8,128)S(1)} %get-tuple-element.16.ids_ref, f32[96,512]{1,0:T(8,128)S(1)} %keep_products.1.kept_ref, f32[96,512]{1,0:T(8,128)S(1)} %collective-permute-done.1.got_ref, f32[1,256]{1,0:T(1,128)S(1)} %bitcast.7, ...), custom_call_target="tpu_custom_call" | custom-call | flops 25165824 | bytes 393216 | tf_op jit(solution)/shard_map/pack/pallas_call | solution.py:227
  8.7 8.0 %all-to-all-start = ((bf16[16,33,2,128]{3,2,1,0:T(2,128)(2,1)}), bf16[16,33,2,128]{3,2,1,0:T(2,128)(2,1)S(1)}, u32[]{:S(2)}, u32[]{:S(2)}) async-start(bf16[16,33,2,128]{3,2,1,0:T(2,128)(2,1)} %pack.1), calls=%async_computation | async-start | bytes 540672 | tf_op jit(solution)/shard_map/all_to_all | solution.py:482
  16.7 0.0 copy-done.1
  16.7 0.0 copy-done.2
  16.8 0.0 copy-done.6
  16.8 0.0 copy-done.7
  16.8 1.0 %cached_scores.1 = (f32[2,64,128]{2,1,0:T(8,128)S(1)}, bf16[2,64,128]{2,1,0:T(8,128)(2,1)S(1)}) custom-call(s32[8]{0:T(128)S(1)} %copy-done.6, s32[8]{0:T(128)S(1)} %copy-done.7, bf16[8,2048]{1,0:T(8,128)(2,1)S(1)} %copy-done.2, bf16[8,128,256]{2,1,0:T(8,128)(2,1)S(1)} %copy-done.1), custom_call_target="tpu_custom_call" | custom-call | flops 33554432 | bytes 524288 | tf_op jit(solution)/shard_map/cached_scores/pallas_call | solution.py:270
  17.8 9.5 %all-to-all-done.got_ref = bf16[16,33,2,128]{3,2,1,0:T(2,128)(2,1)S(1)} async-done(((bf16[16,33,2,128]{3,2,1,0:T(2,128)(2,1)}), bf16[16,33,2,128]{3,2,1,0:T(2,128)(2,1)S(1)}, u32[]{:S(2)}, u32[]{:S(2)}) %all-to-all-start) | async-done | bytes 270368 | tf_op jit(solution)/shard_map/all_to_all | solution.py:482
  27.3 0.0 copy-done
  27.3 1.3 %attend.1 = bf16[8,2048]{1,0:T(8,128)(2,1)} custom-call(bf16[16,33,2,128]{3,2,1,0:T(2,128)(2,1)S(1)} %all-to-all-done.got_ref, bf16[2,64,128]{2,1,0:T(8,128)(2,1)S(1)} %get-tuple-element.23.queries_ref, f32[2,64,128]{2,1,0:T(8,128)S(1)} %get-tuple-element.24.score_ref, bf16[8,128,256]{2,1,0:T(8,128)(2,1)S(1)} %copy-done), custom_call_target="tpu_custom_call" | custom-call | flops 67108864 | bytes 524288 | tf_op jit(solution)/shard_map/attend/pallas_call | solution.py:325
Async XLA Ops:
  1.2 4.0 %collective-permute-start = (f32[96,128]{1,0:T(8,128)S(1)}, f32[96,128]{1,0:T(8,128)S(1)}, u32[]{:S(2)}, u32[]{:S(2)}) collective-permute-start(f32[96,128]{1,0:T(8,128)S(1)} %get-tuple-element.18.own_ref), channel_id=1, source_target_pairs={{0,1},{1,0},{2,3},{3,2},{4,5},{5,4},{6,7},{7,6},{8,9},{9,8},{10,11... | collective-permute-start | bytes 147464 | tf_op jit(solution)/shard_map/ppermute | solution.py:472
  1.7 3.5 %copy-start.3 = (f32[4096]{0:T(1024)S(1)}, f32[4096]{0:T(1024)}, u32[]{:S(2)}) copy-start(f32[4096]{0:T(1024)} %param.14) | copy-start | bytes 49156
  6.2 1.5 %collective-permute-start.1 = (f32[96,512]{1,0:T(8,128)S(1)}, f32[96,512]{1,0:T(8,128)S(1)}, u32[]{:S(2)}, u32[]{:S(2)}) collective-permute-start(f32[96,512]{1,0:T(8,128)S(1)} %get-tuple-element.22), channel_id=1, source_target_pairs={{0,1},{1,0},{2,3},{3,2},{4,5},{5,4},{6,7},{7,6},{8,9},{9,8},{10,11... | collective-permute-start | bytes 589832 | tf_op jit(solution)/shard_map/ppermute | solution.py:479
  6.3 1.4 %copy-start.4 = (f32[256]{0:T(256)S(1)}, f32[256]{0:T(256)}, u32[]{:S(2)}) copy-start(f32[256]{0:T(256)} %param.17) | copy-start | bytes 3076
  6.3 1.4 %copy-start.5 = (f32[256]{0:T(256)S(1)}, f32[256]{0:T(256)}, u32[]{:S(2)}) copy-start(f32[256]{0:T(256)} %param.18) | copy-start | bytes 3076
  6.3 10.4 %copy-start.1 = (bf16[8,128,256]{2,1,0:T(8,128)(2,1)S(1)}, bf16[8,128,256]{2,1,0:T(8,128)(2,1)}, u32[]{:S(2)}) copy-start(bf16[8,128,256]{2,1,0:T(8,128)(2,1)} %key_ref.1) | copy-start | bytes 1572868
  6.3 10.4 %copy-start.2 = (bf16[8,2048]{1,0:T(8,128)(2,1)S(1)}, bf16[8,2048]{1,0:T(8,128)(2,1)}, u32[]{:S(2)}) copy-start(bf16[8,2048]{1,0:T(8,128)(2,1)} %queries_ref.1) | copy-start | bytes 98308
  6.3 10.4 %copy-start.6 = (s32[8]{0:T(128)S(1)}, s32[8]{0:T(128)}, u32[]{:S(2)}) copy-start(s32[8]{0:T(128)} %start_ref.1) | copy-start | bytes 100
  6.3 10.4 %copy-start.7 = (s32[8]{0:T(128)S(1)}, s32[8]{0:T(128)}, u32[]{:S(2)}) copy-start(s32[8]{0:T(128)} %len_ref.1) | copy-start | bytes 100
  6.4 20.9 %copy-start = (bf16[8,128,256]{2,1,0:T(8,128)(2,1)S(1)}, bf16[8,128,256]{2,1,0:T(8,128)(2,1)}, u32[]{:S(2)}) copy-start(bf16[8,128,256]{2,1,0:T(8,128)(2,1)} %cache_ref.1) | copy-start | bytes 1572868
  8.7 18.6 %all-to-all-start = ((bf16[16,33,2,128]{3,2,1,0:T(2,128)(2,1)}), bf16[16,33,2,128]{3,2,1,0:T(2,128)(2,1)S(1)}, u32[]{:S(2)}, u32[]{:S(2)}) async-start(bf16[16,33,2,128]{3,2,1,0:T(2,128)(2,1)} %pack.1), calls=%async_computation | async-start | bytes 540672 | tf_op jit(solution)/shard_map/all_to_all | solution.py:482

commit v4 on v3

--- a/solution.py
+++ b/solution.py
@@ -126,30 +126,9 @@
     )(index, normed, key, value)
 
 
-def route_kernel(
-    per_shard,
-    capacity,
-    here_ref,
-    session_ref,
-    w_key_ref,
-    w_value_ref,
-    pick_ref,
-    ids_ref,
-    held_key_ref,
-    held_value_ref,
-    held_session,
-    arrived,
-):
-    copies = []
-    for at, (source, held) in enumerate(
-        ((session_ref, held_session), (w_key_ref, held_key_ref), (w_value_ref, held_value_ref))
-    ):
-        copies.append(pltpu.make_async_copy(source, held, arrived.at[at]))
-        copies[-1].start()
-    copies[0].wait()
+def route(per_shard, capacity, here, session, pick_ref, ids_ref):
     slots, rows = pick_ref.shape
     partitions = slots // capacity
-    session = held_session[...]
     target = lax.div(session, per_shard)
     local = session - target * per_shard
     to = lax.broadcasted_iota(jnp.int32, (partitions, rows), 0) == target
@@ -161,7 +140,7 @@
     order = jnp.sum(to * ahead, axis=0, keepdims=True).astype(jnp.int32)
     place = lax.broadcasted_iota(jnp.int32, (slots, rows), 0)
     pick_ref[...] = (place == target * capacity + order).astype(jnp.bfloat16)
-    lane = (place == here_ref[0] * capacity + order).astype(jnp.bfloat16)
+    lane = (place == here * capacity + order).astype(jnp.bfloat16)
     ids = nt_dot((to * (local + 1).astype(jnp.float32)).astype(jnp.bfloat16), lane)
     row = lax.broadcasted_iota(jnp.int32, ids_ref.shape, 1)
     block = jnp.zeros(ids_ref.shape, jnp.float32)
@@ -169,28 +148,112 @@
         part = ids[:, j * HEAD : (j + 1) * HEAD]
         block = jnp.where(row == j, part[:, None, :], block)
     ids_ref[...] = block
-    for copy in copies[1:]:
+
+
+def queries_of(queries_ref, head):
+    columns = [
+        queries_ref[:, at * HEAD : (at + 1) * HEAD].astype(jnp.float32)
+        for at in range(head * GROUP, (head + 1) * GROUP)
+    ]
+    return jnp.concatenate(columns, axis=0).astype(jnp.bfloat16)
+
+
+def score_cache(start_ref, len_ref, queries_ref, key_ref, out_ref, laid_ref):
+    heads, rows, window = out_ref.shape
+    sessions = queries_ref.shape[0]
+
+    def by_row(ref):
+        mine = lax.broadcasted_iota(jnp.int32, (rows, sessions), 0) % sessions
+        mine = mine == lax.broadcasted_iota(jnp.int32, (rows, sessions), 1)
+        values = jnp.where(mine, ref[...].astype(jnp.float32), 0.0)
+        return jnp.sum(values, axis=1, keepdims=True).astype(jnp.int32)
+
+    since = lax.broadcasted_iota(jnp.int32, (rows, window), 1) - by_row(start_ref)
+    since = jnp.where(since < 0, since + window, since)
+    live = since < by_row(len_ref)
+    row_session = lax.broadcasted_iota(jnp.int32, (rows, window), 0) % sessions
+    for head in range(heads):
+        query = queries_of(queries_ref, head)
+        laid_ref[head] = query
+        total = jnp.zeros((rows, window), jnp.float32)
+        for session in range(sessions):
+            key = key_ref[session, :, head * HEAD : (head + 1) * HEAD]
+            total = jnp.where(row_session == session, nt_dot(query, key), total)
+        out_ref[head] = jnp.where(live, total * (HEAD**-0.5), -jnp.inf)
+
+
+def beside_kernel(
+    per_shard,
+    capacity,
+    here_ref,
+    session_ref,
+    start_ref,
+    len_ref,
+    queries_ref,
+    cache_ref,
+    w_key_ref,
+    w_value_ref,
+    held_key_ref,
+    held_value_ref,
+    pick_ref,
+    ids_ref,
+    score_ref,
+    laid_ref,
+    session,
+    start,
+    length,
+    queries,
+    cache,
+    arrived,
+):
+    copies = []
+    for at, (source, held) in enumerate(
+        (
+            (session_ref, session),
+            (start_ref, start),
+            (len_ref, length),
+            (queries_ref, queries),
+            (cache_ref, cache),
+            (w_key_ref, held_key_ref),
+            (w_value_ref, held_value_ref),
+        )
+    ):
+        copies.append(pltpu.make_async_copy(source, held, arrived.at[at]))
+        copies[-1].start()
+    copies[0].wait()
+    route(per_shard, capacity, here_ref[0], session[...], pick_ref, ids_ref)
+    for copy in copies[1:5]:
         copy.wait()
-
-
-def route(here, session, w_key, w_value, partitions, per_shard, capacity):
-    rows, slots = session.shape[1], partitions * capacity
+    score_cache(start, length, queries, cache, score_ref, laid_ref)
+    for copy in copies[5:]:
+        copy.wait()
+
+
+def beside(here, session, start, length, queries, cache_key, w_key, w_value, sizes):
+    partitions, per_shard, capacity = sizes
+    slots, rows = partitions * capacity, session.shape[1]
+    sessions, window, width = cache_key.shape
+    heads = width // HEAD
     id_rows = -(-slots // (8 * HEAD)) * 8
+    copied = (session, start, length, queries, cache_key)
     return pl.pallas_call(
-        functools.partial(route_kernel, per_shard, capacity),
+        functools.partial(beside_kernel, per_shard, capacity),
         out_shape=(
+            jax.ShapeDtypeStruct(w_key.shape, w_key.dtype),
+            jax.ShapeDtypeStruct(w_value.shape, w_value.dtype),
             jax.ShapeDtypeStruct((slots, rows), jnp.bfloat16),
             jax.ShapeDtypeStruct((partitions, id_rows, HEAD), jnp.float32),
-            jax.ShapeDtypeStruct(w_key.shape, w_key.dtype),
-            jax.ShapeDtypeStruct(w_value.shape, w_value.dtype),
+            jax.ShapeDtypeStruct((heads, GROUP * sessions, window), jnp.float32),
+            jax.ShapeDtypeStruct((heads, GROUP * sessions, HEAD), jnp.bfloat16),
         ),
-        in_specs=[SMEM, HBM, HBM, HBM],
-        out_specs=(VMEM, VMEM, VMEM, VMEM),
-        scratch_shapes=[pltpu.VMEM(session.shape, session.dtype), pltpu.SemaphoreType.DMA((3,))],
-        compiler_params=params(16),
-        cost_estimate=cost(4 * rows * rows * slots, 2 * w_key.size),
-        name="route",
-    )(here, in_hbm(session), in_hbm(w_key), in_hbm(w_value))
+        in_specs=[SMEM] + [HBM] * 7,
+        out_specs=(VMEM,) * 6,
+        scratch_shapes=[pltpu.VMEM(array.shape, array.dtype) for array in copied]
+        + [pltpu.SemaphoreType.DMA((7,))],
+        compiler_params=params(24),
+        cost_estimate=cost(2 * GROUP * sessions * cache_key.size, 4 * w_key.size),
+        name="beside",
+    )(here, *map(in_hbm, copied), in_hbm(w_key), in_hbm(w_value))
 
 
 def pack_kernel(
@@ -233,52 +296,6 @@
         cost_estimate=cost(2 * rows * width * partitions * capacity, 8 * rows * width),
         name="pack",
     )(pick, ids, kept, got, key_bias, value_bias)
-
-
-def queries_of(queries_ref, head):
-    columns = [
-        queries_ref[:, at * HEAD : (at + 1) * HEAD].astype(jnp.float32)
-        for at in range(head * GROUP, (head + 1) * GROUP)
-    ]
-    return jnp.concatenate(columns, axis=0).astype(jnp.bfloat16)
-
-
-def cached_kernel(start_ref, len_ref, queries_ref, key_ref, out_ref, laid_ref):
-    heads, rows, window = out_ref.shape
-    sessions = queries_ref.shape[0]
-    row_session = lax.broadcasted_iota(jnp.int32, (rows, window), 0) % sessions
-    slot = lax.broadcasted_iota(jnp.int32, (rows, window), 1)
-    live = []
-    for session in range(sessions):
-        since = slot - start_ref[session]
-        since = jnp.where(since < 0, since + window, since)
-        live.append(since < len_ref[session])
-    for head in range(heads):
-        query = queries_of(queries_ref, head)
-        laid_ref[head] = query
-        total = jnp.full((rows, window), -jnp.inf, jnp.float32)
-        for session in range(sessions):
-            key = key_ref[session, :, head * HEAD : (head + 1) * HEAD]
-            score = nt_dot(query, key) * (HEAD**-0.5)
-            total = jnp.where((row_session == session) & live[session], score, total)
-        out_ref[head] = total
-
-
-def cached_scores(start, length, queries, cache_key):
-    sessions, window, width = cache_key.shape
-    heads = width // HEAD
-    return pl.pallas_call(
-        cached_kernel,
-        out_shape=(
-            jax.ShapeDtypeStruct((heads, GROUP * sessions, window), jnp.float32),
-            jax.ShapeDtypeStruct((heads, GROUP * sessions, HEAD), jnp.bfloat16),
-        ),
-        in_specs=[SMEM, SMEM, VMEM, VMEM],
-        out_specs=(VMEM, VMEM),
-        compiler_params=params(8),
-        cost_estimate=cost(2 * GROUP * sessions * cache_key.size, 2 * cache_key.size),
-        name="cached_scores",
-    )(start, length, queries, cache_key)
 
 
 def attend_kernel(capacity, got_ref, queries_ref, score_ref, cache_ref, out_ref):
@@ -470,8 +487,9 @@
     here = lax.axis_index(("grp", "seq")).astype(jnp.int32).reshape(1)
     own, held = partial_squares(frames)
     other = lax.ppermute(own, "mp", swap)
-    pick, ids, held_key, held_value = route(
-        here, token_session[None, :], w_key, w_value, partitions, per_shard, capacity
+    held_key, held_value, pick, ids, scores, laid = beside(
+        here, token_session[None, :], cache_start[None, :], cache_len[None, :], queries, cache_key, w_key,
+        w_value, (partitions, per_shard, capacity),
     )
     normed, sent = send_products(
         index, held, own, other, ln_gain[None, :], held_key, held_value, frames.shape[1] * shares
@@ -480,7 +498,6 @@
     kept = keep_products(index, normed, held_key, held_value)
     blocks = pack(pick, ids, kept, arrived, k_bias[None, :], v_bias[None, :])
     got = lax.all_to_all(blocks, ("grp", "seq"), split_axis=0, concat_axis=0, tiled=True)
-    scores, laid = cached_scores(cache_start, cache_len, queries, cache_key)
     return attend(got, laid, scores, cache_value, capacity)
 
 

time: 28.8 us -> 28.1 us (0.976)
  blocking collectives: 0 us -> 18.4 us
  waiting for transfers between devices: 9.98 us -> 0.56 us
  starting transfers between devices: 8.71 us -> 0.67 us
  Pallas kernels: 9.72 us -> 8.22 us
    all_to_all x0 -> x1, blocking collectives: none -> 18.4 us  [local(): lax.all_to_all(blocks, ('grp', 'seq'), split_axis=0, concat_axis=0, tiled...]
    all_to_all x1 -> x0, waiting for transfers between devices: 9.5 us -> none  [local(): lax.all_to_all(blocks, ('grp', 'seq'), split_axis=0, concat_axis=0, tiled...]
    all_to_all x1 -> x0, starting transfers between devices: 8.04 us -> none  [local(): lax.all_to_all(blocks, ('grp', 'seq'), split_axis=0, concat_axis=0, tiled...]
    pallas_call x2 -> x1, Pallas kernels: 4.51 us -> 3.75 us  [beside(): pl.pallas_call(functools.partial(beside_kernel, per_shard, capacity), out...]
    pallas_call x1, Pallas kernels: 1.01 us -> 0.31 us  [pack(): pl.pallas_call(pack_kernel, out_shape=jax.ShapeDtypeStruct((partitions, b...]
  transfers between devices with their start and end apart: 3 -> 2, of which waited for: 2 -> 1; matrix products, arithmetic and copies ran while one was open for 0% -> 0% of each run, Pallas kernels for 19% -> 16%
where the time goes in v4:
time: 28.1 us; the launch traced here: 27.9 us
  blocking collectives  18.4 us (65%)
  Pallas kernels  8.22 us (29%)
  starting transfers between devices  0.67 us (2%)
  waiting for transfers between devices  0.56 us (2%)
    all_to_all x1, blocking collectives, local(): lax.all_to_all(blocks, ('grp', 'seq'), split_axis=0, concat_axis=0, tiled...  18.4 us
    pallas_call x1, Pallas kernels, beside(): pl.pallas_call(functools.partial(beside_kernel, per_shard, capacity), out...  3.75 us
    pallas_call x1, Pallas kernels, attend(): pl.pallas_call(functools.partial(attend_kernel, capacity), out_shape=jax....  1.27 us
    pallas_call x1, Pallas kernels, partial_squares(): pl.pallas_call(squares_kernel, out_shape=(jax.ShapeDtypeStruct((rows, HEA...  1.21 us
    pallas_call x1, Pallas kernels, send_products(): pl.pallas_call(functools.partial(send_kernel, features), out_shape=(jax.S...  0.88 us
    pallas_call x1, Pallas kernels, keep_products(): pl.pallas_call(keep_kernel, out_shape=jax.ShapeDtypeStruct((rows, width),...  0.8 us
  transfers between devices with their start and end apart: 2, of which 1 were waited for; matrix products, arithmetic and copies ran while one was open for 0% of the time, Pallas kernels for 16%

profile of v4, /device:TPU:0, one launch (start us, length us, event | category | flops | bytes accessed | tf_op | source)
XLA Modules:
  0.0 27.9 jit_solution(3197359801204974657)
XLA Ops:
  0.0 1.2 %partial_squares.1 = (f32[96,128]{1,0:T(8,128)S(1)}, bf16[96,4096]{1,0:T(8,128)(2,1)S(1)}) custom-call(bf16[96,4096]{1,0:T(8,128)(2,1)} %frames_ref.1), custom_call_target="tpu_custom_call" | custom-call | flops 786432 | bytes 786432 | tf_op jit(solution)/shard_map/partial_squares/pallas_call | solution.py:64
  1.2 0.5 %collective-permute-start = (f32[96,128]{1,0:T(8,128)S(1)}, f32[96,128]{1,0:T(8,128)S(1)}, u32[]{:S(2)}, u32[]{:S(2)}) collective-permute-start(f32[96,128]{1,0:T(8,128)S(1)} %get-tuple-element.18.own_ref), channel_id=1, source_target_pairs={{0,1},{1,0},{2,3},{3,2},{4,5},{5,4},{6,7},{7,6},{8,9},{9,8},{10,11... | collective-permute-start | bytes 147464 | tf_op jit(solution)/shard_map/ppermute | solution.py:489
  1.7 0.0 copy-start.1
  1.7 3.8 %beside.1 = (bf16[4096,512]{1,0:T(8,128)(2,1)S(1)}, bf16[4096,512]{1,0:T(8,128)(2,1)S(1)}, bf16[256,96]{1,0:T(8,128)(2,1)S(1)}, f32[16,8,128]{2,1,0:T(8,128)S(1)...) custom-call(s32[1]{0:T(128)} %bitcast.here_ref, s32[1,96]{1,0:T(1,128)} %bitcast.11, s32[1,8]{1,0:T(1,128)} %bitcast.12, ...), custom_call_target="tpu_custom_call" | custom-call | flops 33554432 | bytes 8388608 | tf_op jit(solution)/shard_map/beside/pallas_call | solution.py:239
  5.5 0.0 collective-permute-done.other_ref
  5.5 0.0 copy-done.1
  5.5 0.9 %send_products.1 = (bf16[96,4096]{1,0:T(8,128)(2,1)S(1)}, f32[96,512]{1,0:T(8,128)S(1)}) custom-call(s32[1]{0:T(128)} %bitcast.4.index_ref, bf16[96,4096]{1,0:T(8,128)(2,1)S(1)} %get-tuple-element.17.frames_ref, f32[96,128]{1,0:T(8,128)S(1)} %get-tuple-element.18.own_ref, f32[96,128]{1,0:T(8,128)S(1)} %collective-permute-done.other_ref, ...), custom_call_target="tpu_custom_call" | custom-call | flops 402653184 | bytes 4194304 | tf_op jit(solution)/shard_map/send_products/pallas_call | solution.py:97
  6.4 0.1 collective-permute-start.1
  6.6 0.0 copy-start.2
  6.6 0.0 copy-start.3
  6.6 0.0 copy-start
  6.6 0.8 %keep_products.1.kept_ref = f32[96,512]{1,0:T(8,128)S(1)} custom-call(s32[1]{0:T(128)} %bitcast.4.index_ref, bf16[96,4096]{1,0:T(8,128)(2,1)S(1)} %get-tuple-element.21.normed_ref, bf16[4096,512]{1,0:T(8,128)(2,1)S(1)} %get-tuple-element.19.key_ref, bf16[4096,512]{1,0:T(8,128)(2,1)S(1)} %get-tuple-element.20.value_ref), custom_call_target="tpu_custom_call" | custom-call | flops 402653184 | bytes 4194304 | tf_op jit(solution)/shard_map/keep_products/pallas_call | solution.py:118
  7.4 0.6 %collective-permute-done.1.got_ref = f32[96,512]{1,0:T(8,128)S(1)} collective-permute-done((f32[96,512]{1,0:T(8,128)S(1)}, f32[96,512]{1,0:T(8,128)S(1)}, u32[]{:S(2)}, u32[]{:S(2)}) %collective-permute-start.1) | collective-permute-done | bytes 196640 | tf_op jit(solution)/shard_map/ppermute | solution.py:497
  7.9 0.0 copy-done.2
  7.9 0.0 copy-done.3
  7.9 0.3 %pack.1 = bf16[16,33,2,128]{3,2,1,0:T(2,128)(2,1)S(1)} custom-call(bf16[256,96]{1,0:T(8,128)(2,1)S(1)} %get-tuple-element.15.pick_ref, f32[16,8,128]{2,1,0:T(8,128)S(1)} %get-tuple-element.16.ids_ref, f32[96,512]{1,0:T(8,128)S(1)} %keep_products.1.kept_ref, f32[96,512]{1,0:T(8,128)S(1)} %collective-permute-done.1.got_ref, f32[1,256]{1,0:T(1,128)S(1)} %bitcast.9, ...), custom_call_target="tpu_custom_call" | custom-call | flops 25165824 | bytes 393216 | tf_op jit(solution)/shard_map/pack/pallas_call | solution.py:290
  8.2 18.4 %all_to_all.5.got_ref = bf16[16,33,2,128]{3,2,1,0:T(2,128)(2,1)S(1)} all-to-all(bf16[16,33,2,128]{3,2,1,0:T(2,128)(2,1)S(1)} %pack.1), channel_id=1, replica_groups=mesh['grp'=2,'seq'=8,'mp'=2] {'grp','seq'}, dimensions={0} | all-to-all | bytes 540672 | tf_op jit(solution)/shard_map/all_to_all | solution.py:500
  26.6 0.0 copy-done
  26.6 1.3 %attend.1 = bf16[8,2048]{1,0:T(8,128)(2,1)} custom-call(bf16[16,33,2,128]{3,2,1,0:T(2,128)(2,1)S(1)} %all_to_all.5.got_ref, bf16[2,64,128]{2,1,0:T(8,128)(2,1)S(1)} %get-tuple-element.23.queries_ref, f32[2,64,128]{2,1,0:T(8,128)S(1)} %get-tuple-element.24.score_ref, bf16[8,128,256]{2,1,0:T(8,128)(2,1)S(1)} %copy-done), custom_call_target="tpu_custom_call" | custom-call | flops 67108864 | bytes 524288 | tf_op jit(solution)/shard_map/attend/pallas_call | solution.py:342
Async XLA Ops:
  1.2 4.3 %collective-permute-start = (f32[96,128]{1,0:T(8,128)S(1)}, f32[96,128]{1,0:T(8,128)S(1)}, u32[]{:S(2)}, u32[]{:S(2)}) collective-permute-start(f32[96,128]{1,0:T(8,128)S(1)} %get-tuple-element.18.own_ref), channel_id=1, source_target_pairs={{0,1},{1,0},{2,3},{3,2},{4,5},{5,4},{6,7},{7,6},{8,9},{9,8},{10,11... | collective-permute-start | bytes 147464 | tf_op jit(solution)/shard_map/ppermute | solution.py:489
  1.7 3.8 %copy-start.1 = (f32[4096]{0:T(1024)S(1)}, f32[4096]{0:T(1024)}, u32[]{:S(2)}) copy-start(f32[4096]{0:T(1024)} %param.14) | copy-start | bytes 49156
  6.4 1.5 %collective-permute-start.1 = (f32[96,512]{1,0:T(8,128)S(1)}, f32[96,512]{1,0:T(8,128)S(1)}, u32[]{:S(2)}, u32[]{:S(2)}) collective-permute-start(f32[96,512]{1,0:T(8,128)S(1)} %get-tuple-element.22), channel_id=1, source_target_pairs={{0,1},{1,0},{2,3},{3,2},{4,5},{5,4},{6,7},{7,6},{8,9},{9,8},{10,11... | collective-permute-start | bytes 589832 | tf_op jit(solution)/shard_map/ppermute | solution.py:497
  6.6 1.4 %copy-start.2 = (f32[256]{0:T(256)S(1)}, f32[256]{0:T(256)}, u32[]{:S(2)}) copy-start(f32[256]{0:T(256)} %param.17) | copy-start | bytes 3076
  6.6 1.4 %copy-start.3 = (f32[256]{0:T(256)S(1)}, f32[256]{0:T(256)}, u32[]{:S(2)}) copy-start(f32[256]{0:T(256)} %param.18) | copy-start | bytes 3076
  6.6 20.1 %copy-start = (bf16[8,128,256]{2,1,0:T(8,128)(2,1)S(1)}, bf16[8,128,256]{2,1,0:T(8,128)(2,1)}, u32[]{:S(2)}) copy-start(bf16[8,128,256]{2,1,0:T(8,128)(2,1)} %cache_ref.3) | copy-start | bytes 1572868

commit v5 on v4

--- a/solution.py
+++ b/solution.py
@@ -126,12 +126,32 @@
     )(index, normed, key, value)
 
 
-def route(per_shard, capacity, here, session, pick_ref, ids_ref):
+def max_bits(masks):
+    return functools.reduce(lambda a, b: a | b, masks)
+
+
+def stage_masks(groups, members):
+    if groups & (groups - 1) or members & (members - 1) or members < 4:
+        return None
+    near = sorted((g * members + m for g in range(groups) for m in range(2)), reverse=True)
+    far = sorted(range(0, members, 2), reverse=True)
+    return tuple(tuple([0] + masks[:-1]) for masks in (near, far))
+
+
+def route(per_shard, capacity, stages, here, session, pick_ref, ids_ref):
     slots, rows = pick_ref.shape
     partitions = slots // capacity
+    near, far = stages
     target = lax.div(session, per_shard)
     local = session - target * per_shard
-    to = lax.broadcasted_iota(jnp.int32, (partitions, rows), 0) == target
+    apart = target ^ here
+    step = [
+        sum(jnp.where((apart & max_bits(masks)) == mask, at, 0) for at, mask in enumerate(masks))
+        for masks in stages
+    ]
+    leaves = step[0] * len(far) + step[1]
+    lands = step[1] * len(near) + step[0]
+    to = lax.broadcasted_iota(jnp.int32, (partitions, rows), 0) == leaves
     to = to.astype(jnp.float32)
     earlier = lax.broadcasted_iota(jnp.int32, (rows, rows), 0) < lax.broadcasted_iota(
         jnp.int32, (rows, rows), 1
@@ -139,8 +159,8 @@
     ahead = dot(to.astype(jnp.bfloat16), earlier.astype(jnp.bfloat16))
     order = jnp.sum(to * ahead, axis=0, keepdims=True).astype(jnp.int32)
     place = lax.broadcasted_iota(jnp.int32, (slots, rows), 0)
-    pick_ref[...] = (place == target * capacity + order).astype(jnp.bfloat16)
-    lane = (place == here * capacity + order).astype(jnp.bfloat16)
+    pick_ref[...] = (place == leaves * capacity + order).astype(jnp.bfloat16)
+    lane = (place == lands * capacity + order).astype(jnp.bfloat16)
     ids = nt_dot((to * (local + 1).astype(jnp.float32)).astype(jnp.bfloat16), lane)
     row = lax.broadcasted_iota(jnp.int32, ids_ref.shape, 1)
     block = jnp.zeros(ids_ref.shape, jnp.float32)
@@ -185,6 +205,7 @@
 def beside_kernel(
     per_shard,
     capacity,
+    stages,
     here_ref,
     session_ref,
     start_ref,
@@ -221,7 +242,7 @@
         copies.append(pltpu.make_async_copy(source, held, arrived.at[at]))
         copies[-1].start()
     copies[0].wait()
-    route(per_shard, capacity, here_ref[0], session[...], pick_ref, ids_ref)
+    route(per_shard, capacity, stages, here_ref[0], session[...], pick_ref, ids_ref)
     for copy in copies[1:5]:
         copy.wait()
     score_cache(start, length, queries, cache, score_ref, laid_ref)
@@ -230,14 +251,14 @@
 
 
 def beside(here, session, start, length, queries, cache_key, w_key, w_value, sizes):
-    partitions, per_shard, capacity = sizes
+    partitions, per_shard, capacity, stages = sizes
     slots, rows = partitions * capacity, session.shape[1]
     sessions, window, width = cache_key.shape
     heads = width // HEAD
     id_rows = -(-slots // (8 * HEAD)) * 8
     copied = (session, start, length, queries, cache_key)
     return pl.pallas_call(
-        functools.partial(beside_kernel, per_shard, capacity),
+        functools.partial(beside_kernel, per_shard, capacity, stages),
         out_shape=(
             jax.ShapeDtypeStruct(w_key.shape, w_key.dtype),
             jax.ShapeDtypeStruct(w_value.shape, w_value.dtype),
@@ -263,9 +284,10 @@
     got_ref,
     key_bias_ref,
     value_bias_ref,
-    out_ref,
+    *out_refs,
 ):
-    partitions = out_ref.shape[0]
+    partitions = ids_ref.shape[0]
+    far = partitions // len(out_refs)
     slots = pick_ref.shape[0]
     capacity = slots // partitions
     width = key_bias_ref.shape[1]
@@ -277,47 +299,75 @@
         laid = dot(pick_ref[...], source).astype(jnp.bfloat16).reshape(partitions, capacity, width)
         for column in range(0, width, HEAD):
             part = laid[:, :, column : column + HEAD]
-            out_ref[:, at : at + capacity // 2] = part.reshape(partitions, capacity // 2, 2, HEAD)
+            part = part.reshape(partitions, capacity // 2, 2, HEAD)
+            for step, out_ref in enumerate(out_refs):
+                out_ref[:, at : at + capacity // 2] = part[step * far : (step + 1) * far]
             at += capacity // 2
-    out_ref[:, at] = ids_ref[:, :2, :].astype(jnp.bfloat16)
-
-
-def pack(pick, ids, kept, got, key_bias, value_bias):
+    for step, out_ref in enumerate(out_refs):
+        out_ref[:, at] = ids_ref[step * far : (step + 1) * far, :2, :].astype(jnp.bfloat16)
+
+
+def pack(pick, ids, kept, got, key_bias, value_bias, near):
     rows, width = kept.shape
     partitions, id_rows, _ = ids.shape
     capacity = pick.shape[0] // partitions
     block = width // HEAD * capacity // 2 + 1
     return pl.pallas_call(
         pack_kernel,
-        out_shape=jax.ShapeDtypeStruct((partitions, block, 2, HEAD), jnp.bfloat16),
+        out_shape=[jax.ShapeDtypeStruct((partitions // near, block, 2, HEAD), jnp.bfloat16)] * near,
         in_specs=[VMEM] * 6,
-        out_specs=VMEM,
+        out_specs=[VMEM] * near,
         compiler_params=params(8),
         cost_estimate=cost(2 * rows * width * partitions * capacity, 8 * rows * width),
         name="pack",
     )(pick, ids, kept, got, key_bias, value_bias)
 
 
-def attend_kernel(capacity, got_ref, queries_ref, score_ref, cache_ref, out_ref):
+def regroup_kernel(*refs):
+    far = refs[0].shape[0]
+    got_refs, out_refs = refs[:-far], refs[-far:]
+    for step, out_ref in enumerate(out_refs):
+        for near, got_ref in enumerate(got_refs):
+            out_ref[near] = got_ref[step]
+
+
+def regroup(blocks):
+    far, *block = blocks[0].shape
+    return pl.pallas_call(
+        regroup_kernel,
+        out_shape=[jax.ShapeDtypeStruct((len(blocks), *block), jnp.bfloat16)] * far,
+        in_specs=[VMEM] * len(blocks),
+        out_specs=[VMEM] * far,
+        compiler_params=params(8),
+        cost_estimate=cost(0, 4 * len(blocks) * blocks[0].size),
+        name="regroup",
+    )(*blocks)
+
+
+def attend_kernel(capacity, queries_ref, score_ref, cache_ref, *refs):
+    *got_refs, out_ref = refs
     heads, rows, window = score_ref.shape
     sessions = cache_ref.shape[0]
-    partitions = got_ref.shape[0]
+    partitions = len(got_refs) * got_refs[0].shape[0]
     slots = partitions * capacity
     at = heads * capacity
     ids = jnp.concatenate(
         [
-            jnp.sum(got_ref[:, at, j : j + 1, :].astype(jnp.float32), axis=0)
+            sum(jnp.sum(ref[:, at, j : j + 1, :].astype(jnp.float32), axis=0) for ref in got_refs)
             for j in range(slots // HEAD)
         ],
         axis=1,
     ).astype(jnp.int32)
     own = lax.broadcasted_iota(jnp.int32, (rows, slots), 0) % sessions + 1 == ids
+
+    def rows_of(vector):
+        part = slice(vector * capacity // 2, (vector + 1) * capacity // 2)
+        return jnp.concatenate([ref[:, part].reshape(-1, HEAD) for ref in got_refs], axis=0)
+
     row_session = lax.broadcasted_iota(jnp.int32, (rows, window), 0) % sessions
     for head in range(heads):
         query = queries_ref[head]
-        key = got_ref[:, head * capacity // 2 : (head + 1) * capacity // 2].reshape(slots, HEAD)
-        first = (heads + head) * capacity // 2
-        value = got_ref[:, first : first + capacity // 2].reshape(slots, HEAD)
+        key, value = rows_of(head), rows_of(heads + head)
         cached = score_ref[head]
         fresh = jnp.where(own, nt_dot(query, key) * (HEAD**-0.5), -jnp.inf)
         largest = jnp.maximum(
@@ -344,12 +394,12 @@
         out_shape=jax.ShapeDtypeStruct(
             (cache_value.shape[0], queries.shape[0] * GROUP * HEAD), jnp.bfloat16
         ),
-        in_specs=[VMEM] * 4,
+        in_specs=[VMEM] * (3 + len(got)),
         out_specs=VMEM,
         compiler_params=params(8),
         cost_estimate=cost(4 * queries.shape[1] * cache_value.size, 2 * cache_value.size),
         name="attend",
-    )(got, queries, scores, cache_value)
+    )(queries, scores, cache_value, *got)
 
 
 def project(frame_rows, ln_gain, w_key, w_value, k_bias, v_bias):
@@ -477,7 +527,8 @@
     per_shard = queries.shape[0]
     rows = frames.shape[0]
     capacity = max(2, 5 * rows // (2 * partitions) + 1)
-    if shares != 2 or per_shard % 8 or capacity % 16 or partitions * capacity % HEAD:
+    stages = stage_masks(lax.axis_size("grp"), lax.axis_size("seq"))
+    if stages is None or shares != 2 or per_shard % 8 or capacity % 16 or partitions * capacity % HEAD:
         return general(
             frames, token_session, ln_gain, w_key, w_value, k_bias, v_bias, queries, cache_key, cache_value,
             cache_start, cache_len,
@@ -489,15 +540,21 @@
     other = lax.ppermute(own, "mp", swap)
     held_key, held_value, pick, ids, scores, laid = beside(
         here, token_session[None, :], cache_start[None, :], cache_len[None, :], queries, cache_key, w_key,
-        w_value, (partitions, per_shard, capacity),
+        w_value, (partitions, per_shard, capacity, stages),
     )
     normed, sent = send_products(
         index, held, own, other, ln_gain[None, :], held_key, held_value, frames.shape[1] * shares
     )
     arrived = lax.ppermute(sent, "mp", swap)
     kept = keep_products(index, normed, held_key, held_value)
-    blocks = pack(pick, ids, kept, arrived, k_bias[None, :], v_bias[None, :])
-    got = lax.all_to_all(blocks, ("grp", "seq"), split_axis=0, concat_axis=0, tiled=True)
+    blocks = pack(pick, ids, kept, arrived, k_bias[None, :], v_bias[None, :], len(stages[0]))
+
+    def step(arrays, masks):
+        pairs = [[(i, i ^ mask) for i in range(partitions)] for mask in masks]
+        sent = [lax.ppermute(a, ("grp", "seq"), p) for a, p in zip(arrays[1:], pairs[1:])]
+        return [arrays[0], *sent]
+
+    got = step(regroup(step(blocks, stages[0])), stages[1])
     return attend(got, laid, scores, cache_value, capacity)
 
 

time: 28.1 us -> 27.3 us (0.972)
  blocking collectives: 18.4 us -> 0 us
  waiting for transfers between devices: 0.56 us -> 9.36 us
  starting transfers between devices: 0.67 us -> 9.45 us
    all_to_all x1 -> x0, blocking collectives: 18.4 us -> none  [local(): lax.all_to_all(blocks, ('grp', 'seq'), split_axis=0, concat_axis=0, tiled...]
    ppermute x0 -> x6, waiting for transfers between devices: none -> 8.8 us  [step(): lax.ppermute(a, ('grp', 'seq'), p)]
    ppermute x0 -> x6, starting transfers between devices: none -> 8.78 us  [step(): lax.ppermute(a, ('grp', 'seq'), p)]
    pallas_call x2 -> x3, Pallas kernels: 4.06 us -> 4.08 us  [the longest x1 3.75 us: beside(): pl.pallas_call(functools.partial(beside_kernel, per_shard, capacity, stag...]
  transfers between devices with their start and end apart: 2 -> 8, of which waited for: 1 -> 6; matrix products, arithmetic and copies ran while one was open for 0% -> 0% of each run, Pallas kernels for 16% -> 17%
where the time goes in v5:
time: 27.3 us; the launch traced here: 27.1 us
  starting transfers between devices  9.45 us (35%)
  waiting for transfers between devices  9.36 us (34%)
  Pallas kernels  8.24 us (30%)
    ppermute x6, waiting for transfers between devices, step(): lax.ppermute(a, ('grp', 'seq'), p)  8.8 us
    ppermute x6, starting transfers between devices, step(): lax.ppermute(a, ('grp', 'seq'), p)  8.78 us
    pallas_call x1, Pallas kernels, beside(): pl.pallas_call(functools.partial(beside_kernel, per_shard, capacity, stag...  3.75 us
    pallas_call x1, Pallas kernels, attend(): pl.pallas_call(functools.partial(attend_kernel, capacity), out_shape=jax....  1.27 us
    pallas_call x1, Pallas kernels, partial_squares(): pl.pallas_call(squares_kernel, out_shape=(jax.ShapeDtypeStruct((rows, HEA...  1.21 us
    pallas_call x1, Pallas kernels, send_products(): pl.pallas_call(functools.partial(send_kernel, features), out_shape=(jax.S...  0.88 us
    pallas_call x1, Pallas kernels, keep_products(): pl.pallas_call(keep_kernel, out_shape=jax.ShapeDtypeStruct((rows, width),...  0.8 us
    ppermute x1, waiting for transfers between devices, local(): arrived = lax.ppermute(sent, 'mp', swap)  0.55 us
  transfers between devices with their start and end apart: 8, of which 6 were waited for; matrix products, arithmetic and copies ran while one was open for 0% of the time, Pallas kernels for 17%

profile of v5, /device:TPU:0, one launch (start us, length us, event | category | flops | bytes accessed | tf_op | source)
XLA Modules:
  0.0 27.1 jit_solution(2541961317298770513)
XLA Ops:
  0.0 1.2 %partial_squares.1 = (f32[96,128]{1,0:T(8,128)S(1)}, bf16[96,4096]{1,0:T(8,128)(2,1)S(1)}) custom-call(bf16[96,4096]{1,0:T(8,128)(2,1)} %frames_ref.1), custom_call_target="tpu_custom_call" | custom-call | flops 786432 | bytes 786432 | tf_op jit(solution)/shard_map/partial_squares/pallas_call | solution.py:64
  1.2 0.5 %collective-permute-start = (f32[96,128]{1,0:T(8,128)S(1)}, f32[96,128]{1,0:T(8,128)S(1)}, u32[]{:S(2)}, u32[]{:S(2)}) collective-permute-start(f32[96,128]{1,0:T(8,128)S(1)} %get-tuple-element.28.own_ref), channel_id=1, source_target_pairs={{0,1},{1,0},{2,3},{3,2},{4,5},{5,4},{6,7},{7,6},{8,9},{9,8},{10,11... | collective-permute-start | bytes 147464 | tf_op jit(solution)/shard_map/ppermute | solution.py:540
  1.7 0.0 copy-start.1
  1.7 3.8 %beside.1 = (bf16[4096,512]{1,0:T(8,128)(2,1)S(1)}, bf16[4096,512]{1,0:T(8,128)(2,1)S(1)}, bf16[256,96]{1,0:T(8,128)(2,1)S(1)}, f32[16,8,128]{2,1,0:T(8,128)S(1)...) custom-call(s32[1]{0:T(128)} %bitcast.here_ref, s32[1,96]{1,0:T(1,128)} %bitcast.11, s32[1,8]{1,0:T(1,128)} %bitcast.12, ...), custom_call_target="tpu_custom_call" | custom-call | flops 33554432 | bytes 8388608 | tf_op jit(solution)/shard_map/beside/pallas_call | solution.py:260
  5.5 0.0 collective-permute-done.other_ref
  5.5 0.0 copy-done.1
  5.5 0.9 %send_products.1 = (bf16[96,4096]{1,0:T(8,128)(2,1)S(1)}, f32[96,512]{1,0:T(8,128)S(1)}) custom-call(s32[1]{0:T(128)} %bitcast.4.index_ref, bf16[96,4096]{1,0:T(8,128)(2,1)S(1)} %get-tuple-element.27.frames_ref, f32[96,128]{1,0:T(8,128)S(1)} %get-tuple-element.28.own_ref, f32[96,128]{1,0:T(8,128)S(1)} %collective-permute-done.other_ref, ...), custom_call_target="tpu_custom_call" | custom-call | flops 402653184 | bytes 4194304 | tf_op jit(solution)/shard_map/send_products/pallas_call | solution.py:97
  6.4 0.1 collective-permute-start.1
  6.6 0.0 copy-start.2
  6.6 0.0 copy-start.3
  6.6 0.0 copy-start
  6.6 0.8 %keep_products.1.kept_ref = f32[96,512]{1,0:T(8,128)S(1)} custom-call(s32[1]{0:T(128)} %bitcast.4.index_ref, bf16[96,4096]{1,0:T(8,128)(2,1)S(1)} %get-tuple-element.31.normed_ref, bf16[4096,512]{1,0:T(8,128)(2,1)S(1)} %get-tuple-element.29.key_ref, bf16[4096,512]{1,0:T(8,128)(2,1)S(1)} %get-tuple-element.30.value_ref), custom_call_target="tpu_custom_call" | custom-call | flops 402653184 | bytes 4194304 | tf_op jit(solution)/shard_map/keep_products/pallas_call | solution.py:118
  7.4 0.6 %collective-permute-done.1.got_ref = f32[96,512]{1,0:T(8,128)S(1)} collective-permute-done((f32[96,512]{1,0:T(8,128)S(1)}, f32[96,512]{1,0:T(8,128)S(1)}, u32[]{:S(2)}, u32[]{:S(2)}) %collective-permute-start.1) | collective-permute-done | bytes 196640 | tf_op jit(solution)/shard_map/ppermute | solution.py:548
  7.9 0.0 copy-done.2
  7.9 0.0 copy-done.3
  7.9 0.3 %pack.1 = (bf16[4,33,2,128]{3,2,1,0:T(2,128)(2,1)S(1)}, bf16[4,33,2,128]{3,2,1,0:T(2,128)(2,1)S(1)}, bf16[4,33,2,128]{3,2,1,0:T(2,128)(2,1)S(1)}, bf16[4,33,2,128]{3,2,1,0:T(2,128)(2,1)S(1)}) custom-call(bf16[256,96]{1,0:T(8,128)(2,1)S(1)} %get-tuple-element.25.pick_ref, f32[16,8,128]{2,1,0:T(8,128)S(1)} %get-tuple-element.26.ids_ref, ...), custom_call_target="tpu_custom_call" | custom-call | flops 25165824 | bytes 393216 | tf_op jit(solution)/shard_map/pack/pallas_call | solution.py:315
  8.2 3.7 %collective-permute-start.2 = (bf16[4,33,2,128]{3,2,1,0:T(2,128)(2,1)S(1)}, bf16[4,33,2,128]{3,2,1,0:T(2,128)(2,1)S(1)}, u32[]{:S(2)}, u32[]{:S(2)}) collective-permute-start(bf16[4,33,2,128]{3,2,1,0:T(2,128)(2,1)S(1)} %get-tuple-element.34), channel_id=1, source_target_pairs={{0,18},{2,16},{4,22},{6,20},{8,26},{10,24},{12,30},{14,28},{16,2},... | collective-permute-start | bytes 202760 | tf_op jit(solution)/shard_map/ppermute | solution.py:554
  11.9 0.5 %collective-permute-start.3 = (bf16[4,33,2,128]{3,2,1,0:T(2,128)(2,1)S(1)}, bf16[4,33,2,128]{3,2,1,0:T(2,128)(2,1)S(1)}, u32[]{:S(2)}, u32[]{:S(2)}) collective-permute-start(bf16[4,33,2,128]{3,2,1,0:T(2,128)(2,1)S(1)} %get-tuple-element.35), channel_id=1, source_target_pairs={{0,16},{2,18},{4,20},{6,22},{8,24},{10,26},{12,28},{14,30},{16,0},... | collective-permute-start | bytes 202760 | tf_op jit(solution)/shard_map/ppermute | solution.py:554
  12.5 0.1 collective-permute-start.4
  12.6 2.0 %collective-permute-done.2.refs_1_ = bf16[4,33,2,128]{3,2,1,0:T(2,128)(2,1)S(1)} collective-permute-done((bf16[4,33,2,128]{3,2,1,0:T(2,128)(2,1)S(1)}, bf16[4,33,2,128]{3,2,1,0:T(2,128)(2,1)S(1)}, u32[]{:S(2)}, u32[]{:S(2)}) %collective-permute-start.2) | collective-permute-done | bytes 67616 | tf_op jit(solution)/shard_map/ppermute | solution.py:554
  14.6 1.7 %collective-permute-done.3.refs_2_ = bf16[4,33,2,128]{3,2,1,0:T(2,128)(2,1)S(1)} collective-permute-done((bf16[4,33,2,128]{3,2,1,0:T(2,128)(2,1)S(1)}, bf16[4,33,2,128]{3,2,1,0:T(2,128)(2,1)S(1)}, u32[]{:S(2)}, u32[]{:S(2)}) %collective-permute-start.3) | collective-permute-done | bytes 67616 | tf_op jit(solution)/shard_map/ppermute | solution.py:554
  16.3 0.5 %collective-permute-done.4.refs_3_ = bf16[4,33,2,128]{3,2,1,0:T(2,128)(2,1)S(1)} collective-permute-done((bf16[4,33,2,128]{3,2,1,0:T(2,128)(2,1)S(1)}, bf16[4,33,2,128]{3,2,1,0:T(2,128)(2,1)S(1)}, u32[]{:S(2)}, u32[]{:S(2)}) %collective-permute-start.4) | collective-permute-done | bytes 67616 | tf_op jit(solution)/shard_map/ppermute | solution.py:554
  16.8 3.7 %collective-permute-start.5 = (bf16[4,33,2,128]{3,2,1,0:T(2,128)(2,1)S(1)}, bf16[4,33,2,128]{3,2,1,0:T(2,128)(2,1)S(1)}, u32[]{:S(2)}, u32[]{:S(2)}) collective-permute-start(bf16[4,33,2,128]{3,2,1,0:T(2,128)(2,1)S(1)} %get-tuple-element.38), channel_id=1, source_target_pairs={{0,12},{2,14},{4,8},{6,10},{8,4},{10,6},{12,0},{14,2},{16,28},{18,... | collective-permute-start | bytes 202760 | tf_op jit(solution)/shard_map/ppermute | solution.py:554
  20.4 0.0 collective-permute-start.6
  20.4 0.8 %collective-permute-start.7 = (bf16[4,33,2,128]{3,2,1,0:T(2,128)(2,1)S(1)}, bf16[4,33,2,128]{3,2,1,0:T(2,128)(2,1)S(1)}, u32[]{:S(2)}, u32[]{:S(2)}) collective-permute-start(bf16[4,33,2,128]{3,2,1,0:T(2,128)(2,1)S(1)} %get-tuple-element.40), channel_id=1, source_target_pairs={{0,4},{2,6},{4,0},{6,2},{8,12},{10,14},{12,8},{14,10},{16,20},{18,... | collective-permute-start | bytes 202760 | tf_op jit(solution)/shard_map/ppermute | solution.py:554
  21.2 2.0 %collective-permute-done.5.refs_1_ = bf16[4,33,2,128]{3,2,1,0:T(2,128)(2,1)S(1)} collective-permute-done((bf16[4,33,2,128]{3,2,1,0:T(2,128)(2,1)S(1)}, bf16[4,33,2,128]{3,2,1,0:T(2,128)(2,1)S(1)}, u32[]{:S(2)}, u32[]{:S(2)}) %collective-permute-start.5) | collective-permute-done | bytes 67616 | tf_op jit(solution)/shard_map/ppermute | solution.py:554
  23.3 2.6 %collective-permute-done.6.refs_2_ = bf16[4,33,2,128]{3,2,1,0:T(2,128)(2,1)S(1)} collective-permute-done((bf16[4,33,2,128]{3,2,1,0:T(2,128)(2,1)S(1)}, bf16[4,33,2,128]{3,2,1,0:T(2,128)(2,1)S(1)}, u32[]{:S(2)}, u32[]{:S(2)}) %collective-permute-start.6) | collective-permute-done | bytes 67616 | tf_op jit(solution)/shard_map/ppermute | solution.py:554
  25.8 0.0 collective-permute-done.7.refs_3_
  25.8 0.0 copy-done
  25.8 1.3 %attend.1 = bf16[8,2048]{1,0:T(8,128)(2,1)} custom-call(bf16[2,64,128]{2,1,0:T(8,128)(2,1)S(1)} %get-tuple-element.23.queries_ref, f32[2,64,128]{2,1,0:T(8,128)S(1)} %get-tuple-element.24.score_ref, bf16[8,128,256]{2,1,0:T(8,128)(2,1)S(1)} %copy-done, bf16[4,33,2,128]{3,2,1,0:T(2,128)(2,1)S(1)} %get-tuple-element.37.refs_0_, ...), custom_call_target="tpu_custom_call" | custom-call | flops 67108864 | bytes 524288 | tf_op jit(solution)/shard_map/attend/pallas_call | solution.py:392
  (1 shorter events, 0.0 us)
Async XLA Ops:
  1.2 4.3 %collective-permute-start = (f32[96,128]{1,0:T(8,128)S(1)}, f32[96,128]{1,0:T(8,128)S(1)}, u32[]{:S(2)}, u32[]{:S(2)}) collective-permute-start(f32[96,128]{1,0:T(8,128)S(1)} %get-tuple-element.28.own_ref), channel_id=1, source_target_pairs={{0,1},{1,0},{2,3},{3,2},{4,5},{5,4},{6,7},{7,6},{8,9},{9,8},{10,11... | collective-permute-start | bytes 147464 | tf_op jit(solution)/shard_map/ppermute | solution.py:540
  1.7 3.8 %copy-start.1 = (f32[4096]{0:T(1024)S(1)}, f32[4096]{0:T(1024)}, u32[]{:S(2)}) copy-start(f32[4096]{0:T(1024)} %param.14) | copy-start | bytes 49156
  6.4 1.5 %collective-permute-start.1 = (f32[96,512]{1,0:T(8,128)S(1)}, f32[96,512]{1,0:T(8,128)S(1)}, u32[]{:S(2)}, u32[]{:S(2)}) collective-permute-start(f32[96,512]{1,0:T(8,128)S(1)} %get-tuple-element.32), channel_id=1, source_target_pairs={{0,1},{1,0},{2,3},{3,2},{4,5},{5,4},{6,7},{7,6},{8,9},{9,8},{10,11... | collective-permute-start | bytes 589832 | tf_op jit(solution)/shard_map/ppermute | solution.py:548
  6.6 1.4 %copy-start.2 = (f32[256]{0:T(256)S(1)}, f32[256]{0:T(256)}, u32[]{:S(2)}) copy-start(f32[256]{0:T(256)} %param.17) | copy-start | bytes 3076
  6.6 1.4 %copy-start.3 = (f32[256]{0:T(256)S(1)}, f32[256]{0:T(256)}, u32[]{:S(2)}) copy-start(f32[256]{0:T(256)} %param.18) | copy-start | bytes 3076
  6.6 19.3 %copy-start = (bf16[8,128,256]{2,1,0:T(8,128)(2,1)S(1)}, bf16[8,128,256]{2,1,0:T(8,128)(2,1)}, u32[]{:S(2)}) copy-start(bf16[8,128,256]{2,1,0:T(8,128)(2,1)} %cache_ref.3) | copy-start | bytes 1572868
  8.2 6.4 %collective-permute-start.2 = (bf16[4,33,2,128]{3,2,1,0:T(2,128)(2,1)S(1)}, bf16[4,33,2,128]{3,2,1,0:T(2,128)(2,1)S(1)}, u32[]{:S(2)}, u32[]{:S(2)}) collective-permute-start(bf16[4,33,2,128]{3,2,1,0:T(2,128)(2,1)S(1)} %get-tuple-element.34), channel_id=1, source_target_pairs={{0,18},{2,16},{4,22},{6,20},{8,26},{10,24},{12,30},{14,28},{16,2},... | collective-permute-start | bytes 202760 | tf_op jit(solution)/shard_map/ppermute | solution.py:554
  11.9 4.4 %collective-permute-start.3 = (bf16[4,33,2,128]{3,2,1,0:T(2,128)(2,1)S(1)}, bf16[4,33,2,128]{3,2,1,0:T(2,128)(2,1)S(1)}, u32[]{:S(2)}, u32[]{:S(2)}) collective-permute-start(bf16[4,33,2,128]{3,2,1,0:T(2,128)(2,1)S(1)} %get-tuple-element.35), channel_id=1, source_target_pairs={{0,16},{2,18},{4,20},{6,22},{8,24},{10,26},{12,28},{14,30},{16,0},... | collective-permute-start | bytes 202760 | tf_op jit(solution)/shard_map/ppermute | solution.py:554
  12.5 4.3 %collective-permute-start.4 = (bf16[4,33,2,128]{3,2,1,0:T(2,128)(2,1)S(1)}, bf16[4,33,2,128]{3,2,1,0:T(2,128)(2,1)S(1)}, u32[]{:S(2)}, u32[]{:S(2)}) collective-permute-start(bf16[4,33,2,128]{3,2,1,0:T(2,128)(2,1)S(1)} %get-tuple-element.36), channel_id=1, source_target_pairs={{0,2},{2,0},{4,6},{6,4},{8,10},{10,8},{12,14},{14,12},{16,18},{18,... | collective-permute-start | bytes 202760 | tf_op jit(solution)/shard_map/ppermute | solution.py:554
  16.8 6.5 %collective-permute-start.5 = (bf16[4,33,2,128]{3,2,1,0:T(2,128)(2,1)S(1)}, bf16[4,33,2,128]{3,2,1,0:T(2,128)(2,1)S(1)}, u32[]{:S(2)}, u32[]{:S(2)}) collective-permute-start(bf16[4,33,2,128]{3,2,1,0:T(2,128)(2,1)S(1)} %get-tuple-element.38), channel_id=1, source_target_pairs={{0,12},{2,14},{4,8},{6,10},{8,4},{10,6},{12,0},{14,2},{16,28},{18,... | collective-permute-start | bytes 202760 | tf_op jit(solution)/shard_map/ppermute | solution.py:554
  20.4 5.4 %collective-permute-start.6 = (bf16[4,33,2,128]{3,2,1,0:T(2,128)(2,1)S(1)}, bf16[4,33,2,128]{3,2,1,0:T(2,128)(2,1)S(1)}, u32[]{:S(2)}, u32[]{:S(2)}) collective-permute-start(bf16[4,33,2,128]{3,2,1,0:T(2,128)(2,1)S(1)} %get-tuple-element.39), channel_id=1, source_target_pairs={{0,8},{2,10},{4,12},{6,14},{8,0},{10,2},{12,4},{14,6},{16,24},{18,... | collective-permute-start | bytes 202760 | tf_op jit(solution)/shard_map/ppermute | solution.py:554
  20.4 5.4 %collective-permute-start.7 = (bf16[4,33,2,128]{3,2,1,0:T(2,128)(2,1)S(1)}, bf16[4,33,2,128]{3,2,1,0:T(2,128)(2,1)S(1)}, u32[]{:S(2)}, u32[]{:S(2)}) collective-permute-start(bf16[4,33,2,128]{3,2,1,0:T(2,128)(2,1)S(1)} %get-tuple-element.40), channel_id=1, source_target_pairs={{0,4},{2,6},{4,0},{6,2},{8,12},{10,14},{12,8},{14,10},{16,20},{18,... | collective-permute-start | bytes 202760 | tf_op jit(solution)/shard_map/ppermute | solution.py:554

commit v6 on v5

--- a/solution.py
+++ b/solution.py
@@ -135,7 +135,7 @@
         return None
     near = sorted((g * members + m for g in range(groups) for m in range(2)), reverse=True)
     far = sorted(range(0, members, 2), reverse=True)
-    return tuple(tuple([0] + masks[:-1]) for masks in (near, far))
+    return (0, *near[:-1]), (0, far[0], *far[-2:0:-1])
 
 
 def route(per_shard, capacity, stages, here, session, pick_ref, ids_ref):
@@ -179,8 +179,8 @@
 
 
 def score_cache(start_ref, len_ref, queries_ref, key_ref, out_ref, laid_ref):
-    heads, rows, window = out_ref.shape
-    sessions = queries_ref.shape[0]
+    sessions, window, width = key_ref.shape
+    heads, rows = width // HEAD, GROUP * sessions
 
     def by_row(ref):
         mine = lax.broadcasted_iota(jnp.int32, (rows, sessions), 0) % sessions
@@ -192,14 +192,16 @@
     since = jnp.where(since < 0, since + window, since)
     live = since < by_row(len_ref)
     row_session = lax.broadcasted_iota(jnp.int32, (rows, window), 0) % sessions
+    laid_ref[...] = jnp.zeros_like(laid_ref)
     for head in range(heads):
         query = queries_of(queries_ref, head)
-        laid_ref[head] = query
+        laid_ref[head * rows : (head + 1) * rows, head * HEAD : (head + 1) * HEAD] = query
         total = jnp.zeros((rows, window), jnp.float32)
         for session in range(sessions):
             key = key_ref[session, :, head * HEAD : (head + 1) * HEAD]
             total = jnp.where(row_session == session, nt_dot(query, key), total)
-        out_ref[head] = jnp.where(live, total * (HEAD**-0.5), -jnp.inf)
+        total = jnp.where(live, total * (HEAD**-0.5), -jnp.inf)
+        out_ref[head * rows : (head + 1) * rows] = total
 
 
 def beside_kernel(
@@ -264,8 +266,8 @@
             jax.ShapeDtypeStruct(w_value.shape, w_value.dtype),
             jax.ShapeDtypeStruct((slots, rows), jnp.bfloat16),
             jax.ShapeDtypeStruct((partitions, id_rows, HEAD), jnp.float32),
-            jax.ShapeDtypeStruct((heads, GROUP * sessions, window), jnp.float32),
-            jax.ShapeDtypeStruct((heads, GROUP * sessions, HEAD), jnp.bfloat16),
+            jax.ShapeDtypeStruct((heads * GROUP * sessions, window), jnp.float32),
+            jax.ShapeDtypeStruct((heads * GROUP * sessions, width), jnp.bfloat16),
         ),
         in_specs=[SMEM] + [HBM] * 7,
         out_specs=(VMEM,) * 6,
@@ -346,10 +348,10 @@
 
 def attend_kernel(capacity, queries_ref, score_ref, cache_ref, *refs):
     *got_refs, out_ref = refs
-    heads, rows, window = score_ref.shape
-    sessions = cache_ref.shape[0]
-    partitions = len(got_refs) * got_refs[0].shape[0]
-    slots = partitions * capacity
+    rows, window = score_ref.shape
+    sessions, _, width = cache_ref.shape
+    heads = width // HEAD
+    slots = len(got_refs) * got_refs[0].shape[0] * capacity
     at = heads * capacity
     ids = jnp.concatenate(
         [
@@ -360,31 +362,38 @@
     ).astype(jnp.int32)
     own = lax.broadcasted_iota(jnp.int32, (rows, slots), 0) % sessions + 1 == ids
 
-    def rows_of(vector):
-        part = slice(vector * capacity // 2, (vector + 1) * capacity // 2)
-        return jnp.concatenate([ref[:, part].reshape(-1, HEAD) for ref in got_refs], axis=0)
-
+    def rows_of(vectors):
+        columns = []
+        for vector in vectors:
+            part = slice(vector * capacity // 2, (vector + 1) * capacity // 2)
+            columns.append(
+                jnp.concatenate([ref[:, part].reshape(-1, HEAD) for ref in got_refs], axis=0)
+            )
+        return jnp.concatenate(columns, axis=1)
+
+    cached = score_ref[...]
+    fresh = nt_dot(queries_ref[...], rows_of(range(heads))) * (HEAD**-0.5)
+    fresh = jnp.where(own, fresh, -jnp.inf)
+    largest = jnp.maximum(
+        jnp.max(cached, axis=1, keepdims=True), jnp.max(fresh, axis=1, keepdims=True)
+    )
+    cached = jnp.exp(cached - largest)
+    fresh = jnp.exp(fresh - largest)
+    total = jnp.sum(cached, axis=1, keepdims=True) + jnp.sum(fresh, axis=1, keepdims=True)
+    cached = cached / total
+    attended = dot((fresh / total).astype(jnp.bfloat16), rows_of(range(heads, 2 * heads)))
     row_session = lax.broadcasted_iota(jnp.int32, (rows, window), 0) % sessions
+    for session in range(0, sessions, 2):
+        weights = jnp.concatenate(
+            [jnp.where(row_session == session + more, cached, 0.0) for more in range(2)], axis=1
+        )
+        values = cache_ref[session : session + 2].reshape(2 * window, width)
+        attended += dot(weights.astype(jnp.bfloat16), values)
     for head in range(heads):
-        query = queries_ref[head]
-        key, value = rows_of(head), rows_of(heads + head)
-        cached = score_ref[head]
-        fresh = jnp.where(own, nt_dot(query, key) * (HEAD**-0.5), -jnp.inf)
-        largest = jnp.maximum(
-            jnp.max(cached, axis=1, keepdims=True), jnp.max(fresh, axis=1, keepdims=True)
-        )
-        cached = jnp.exp(cached - largest)
-        fresh = jnp.exp(fresh - largest)
-        total = jnp.sum(cached, axis=1, keepdims=True) + jnp.sum(fresh, axis=1, keepdims=True)
-        cached = cached / total
-        attended = dot((fresh / total).astype(jnp.bfloat16), value)
-        for session in range(sessions):
-            weights = jnp.where(row_session == session, cached, 0.0).astype(jnp.bfloat16)
-            attended += dot(weights, cache_ref[session, :, head * HEAD : (head + 1) * HEAD])
         for q in range(GROUP):
-            column = (head * GROUP + q) * HEAD
+            row, column = (head * GROUP + q) * sessions, (head * GROUP + q) * HEAD
             out_ref[:, column : column + HEAD] = attended[
-                q * sessions : (q + 1) * sessions
+                row : row + sessions, head * HEAD : (head + 1) * HEAD
             ].astype(jnp.bfloat16)
 
 
@@ -392,12 +401,12 @@
     return pl.pallas_call(
         functools.partial(attend_kernel, capacity),
         out_shape=jax.ShapeDtypeStruct(
-            (cache_value.shape[0], queries.shape[0] * GROUP * HEAD), jnp.bfloat16
+            (cache_value.shape[0], queries.shape[1] * GROUP), jnp.bfloat16
         ),
         in_specs=[VMEM] * (3 + len(got)),
         out_specs=VMEM,
         compiler_params=params(8),
-        cost_estimate=cost(4 * queries.shape[1] * cache_value.size, 2 * cache_value.size),
+        cost_estimate=cost(4 * queries.shape[0] * cache_value.size, 2 * cache_value.size),
         name="attend",
     )(queries, scores, cache_value, *got)
 

time: 27.3 us -> 27 us (0.989)
  transfers between devices with their start and end apart: 8 -> 8, of which waited for: 6 -> 7; matrix products, arithmetic and copies ran while one was open for 0% -> 0% of each run, Pallas kernels for 17% -> 17%
where the time goes in v6:
time: 27 us; the launch traced here: 26.9 us
  starting transfers between devices  9.45 us (35%)
  waiting for transfers between devices  9.14 us (34%)
  Pallas kernels  8.21 us (30%)
    ppermute x6, starting transfers between devices, step(): lax.ppermute(a, ('grp', 'seq'), p)  8.78 us
    ppermute x6, waiting for transfers between devices, step(): lax.ppermute(a, ('grp', 'seq'), p)  8.58 us
    pallas_call x1, Pallas kernels, beside(): pl.pallas_call(functools.partial(beside_kernel, per_shard, capacity, stag...  3.75 us
    pallas_call x1, Pallas kernels, attend(): pl.pallas_call(functools.partial(attend_kernel, capacity), out_shape=jax....  1.24 us
    pallas_call x1, Pallas kernels, partial_squares(): pl.pallas_call(squares_kernel, out_shape=(jax.ShapeDtypeStruct((rows, HEA...  1.21 us
    pallas_call x1, Pallas kernels, send_products(): pl.pallas_call(functools.partial(send_kernel, features), out_shape=(jax.S...  0.88 us
    pallas_call x1, Pallas kernels, keep_products(): pl.pallas_call(keep_kernel, out_shape=jax.ShapeDtypeStruct((rows, width),...  0.8 us
    ppermute x1, waiting for transfers between devices, local(): arrived = lax.ppermute(sent, 'mp', swap)  0.55 us
  transfers between devices with their start and end apart: 8, of which 7 were waited for; matrix products, arithmetic and copies ran while one was open for 0% of the time, Pallas kernels for 17%

profile of v6, /device:TPU:0, one launch (start us, length us, event | category | flops | bytes accessed | tf_op | source)
XLA Modules:
  0.0 26.9 jit_solution(17745595985716929296)
XLA Ops:
  0.0 1.2 %partial_squares.1 = (f32[96,128]{1,0:T(8,128)S(1)}, bf16[96,4096]{1,0:T(8,128)(2,1)S(1)}) custom-call(bf16[96,4096]{1,0:T(8,128)(2,1)} %frames_ref.1), custom_call_target="tpu_custom_call" | custom-call | flops 786432 | bytes 786432 | tf_op jit(solution)/shard_map/partial_squares/pallas_call | solution.py:64
  1.2 0.5 %collective-permute-start = (f32[96,128]{1,0:T(8,128)S(1)}, f32[96,128]{1,0:T(8,128)S(1)}, u32[]{:S(2)}, u32[]{:S(2)}) collective-permute-start(f32[96,128]{1,0:T(8,128)S(1)} %get-tuple-element.28.own_ref), channel_id=1, source_target_pairs={{0,1},{1,0},{2,3},{3,2},{4,5},{5,4},{6,7},{7,6},{8,9},{9,8},{10,11... | collective-permute-start | bytes 147464 | tf_op jit(solution)/shard_map/ppermute | solution.py:549
  1.7 0.0 copy-start.1
  1.7 3.8 %beside.1 = (bf16[4096,512]{1,0:T(8,128)(2,1)S(1)}, bf16[4096,512]{1,0:T(8,128)(2,1)S(1)}, bf16[256,96]{1,0:T(8,128)(2,1)S(1)}, f32[16,8,128]{2,1,0:T(8,128)S(1)...) custom-call(s32[1]{0:T(128)} %bitcast.here_ref, s32[1,96]{1,0:T(1,128)} %bitcast.11, s32[1,8]{1,0:T(1,128)} %bitcast.12, ...), custom_call_target="tpu_custom_call" | custom-call | flops 33554432 | bytes 8388608 | tf_op jit(solution)/shard_map/beside/pallas_call | solution.py:262
  5.5 0.0 collective-permute-done.other_ref
  5.5 0.0 copy-done.1
  5.5 0.9 %send_products.1 = (bf16[96,4096]{1,0:T(8,128)(2,1)S(1)}, f32[96,512]{1,0:T(8,128)S(1)}) custom-call(s32[1]{0:T(128)} %bitcast.4.index_ref, bf16[96,4096]{1,0:T(8,128)(2,1)S(1)} %get-tuple-element.27.frames_ref, f32[96,128]{1,0:T(8,128)S(1)} %get-tuple-element.28.own_ref, f32[96,128]{1,0:T(8,128)S(1)} %collective-permute-done.other_ref, ...), custom_call_target="tpu_custom_call" | custom-call | flops 402653184 | bytes 4194304 | tf_op jit(solution)/shard_map/send_products/pallas_call | solution.py:97
  6.4 0.1 collective-permute-start.1
  6.6 0.0 copy-start.2
  6.6 0.0 copy-start.3
  6.6 0.0 copy-start
  6.6 0.8 %keep_products.1.kept_ref = f32[96,512]{1,0:T(8,128)S(1)} custom-call(s32[1]{0:T(128)} %bitcast.4.index_ref, bf16[96,4096]{1,0:T(8,128)(2,1)S(1)} %get-tuple-element.31.normed_ref, bf16[4096,512]{1,0:T(8,128)(2,1)S(1)} %get-tuple-element.29.key_ref, bf16[4096,512]{1,0:T(8,128)(2,1)S(1)} %get-tuple-element.30.value_ref), custom_call_target="tpu_custom_call" | custom-call | flops 402653184 | bytes 4194304 | tf_op jit(solution)/shard_map/keep_products/pallas_call | solution.py:118
  7.4 0.6 %collective-permute-done.1.got_ref = f32[96,512]{1,0:T(8,128)S(1)} collective-permute-done((f32[96,512]{1,0:T(8,128)S(1)}, f32[96,512]{1,0:T(8,128)S(1)}, u32[]{:S(2)}, u32[]{:S(2)}) %collective-permute-start.1) | collective-permute-done | bytes 196640 | tf_op jit(solution)/shard_map/ppermute | solution.py:557
  7.9 0.0 copy-done.2
  7.9 0.0 copy-done.3
  7.9 0.3 %pack.1 = (bf16[4,33,2,128]{3,2,1,0:T(2,128)(2,1)S(1)}, bf16[4,33,2,128]{3,2,1,0:T(2,128)(2,1)S(1)}, bf16[4,33,2,128]{3,2,1,0:T(2,128)(2,1)S(1)}, bf16[4,33,2,128]{3,2,1,0:T(2,128)(2,1)S(1)}) custom-call(bf16[256,96]{1,0:T(8,128)(2,1)S(1)} %get-tuple-element.25.pick_ref, f32[16,8,128]{2,1,0:T(8,128)S(1)} %get-tuple-element.26.ids_ref, ...), custom_call_target="tpu_custom_call" | custom-call | flops 25165824 | bytes 393216 | tf_op jit(solution)/shard_map/pack/pallas_call | solution.py:317
  8.2 3.7 %collective-permute-start.2 = (bf16[4,33,2,128]{3,2,1,0:T(2,128)(2,1)S(1)}, bf16[4,33,2,128]{3,2,1,0:T(2,128)(2,1)S(1)}, u32[]{:S(2)}, u32[]{:S(2)}) collective-permute-start(bf16[4,33,2,128]{3,2,1,0:T(2,128)(2,1)S(1)} %get-tuple-element.34), channel_id=1, source_target_pairs={{0,18},{2,16},{4,22},{6,20},{8,26},{10,24},{12,30},{14,28},{16,2},... | collective-permute-start | bytes 202760 | tf_op jit(solution)/shard_map/ppermute | solution.py:563
  11.9 0.5 %collective-permute-start.3 = (bf16[4,33,2,128]{3,2,1,0:T(2,128)(2,1)S(1)}, bf16[4,33,2,128]{3,2,1,0:T(2,128)(2,1)S(1)}, u32[]{:S(2)}, u32[]{:S(2)}) collective-permute-start(bf16[4,33,2,128]{3,2,1,0:T(2,128)(2,1)S(1)} %get-tuple-element.35), channel_id=1, source_target_pairs={{0,16},{2,18},{4,20},{6,22},{8,24},{10,26},{12,28},{14,30},{16,0},... | collective-permute-start | bytes 202760 | tf_op jit(solution)/shard_map/ppermute | solution.py:563
  12.5 0.1 collective-permute-start.4
  12.6 2.0 %collective-permute-done.2.refs_1_ = bf16[4,33,2,128]{3,2,1,0:T(2,128)(2,1)S(1)} collective-permute-done((bf16[4,33,2,128]{3,2,1,0:T(2,128)(2,1)S(1)}, bf16[4,33,2,128]{3,2,1,0:T(2,128)(2,1)S(1)}, u32[]{:S(2)}, u32[]{:S(2)}) %collective-permute-start.2) | collective-permute-done | bytes 67616 | tf_op jit(solution)/shard_map/ppermute | solution.py:563
  14.6 1.7 %collective-permute-done.3.refs_2_ = bf16[4,33,2,128]{3,2,1,0:T(2,128)(2,1)S(1)} collective-permute-done((bf16[4,33,2,128]{3,2,1,0:T(2,128)(2,1)S(1)}, bf16[4,33,2,128]{3,2,1,0:T(2,128)(2,1)S(1)}, u32[]{:S(2)}, u32[]{:S(2)}) %collective-permute-start.3) | collective-permute-done | bytes 67616 | tf_op jit(solution)/shard_map/ppermute | solution.py:563
  16.3 0.5 %collective-permute-done.4.refs_3_ = bf16[4,33,2,128]{3,2,1,0:T(2,128)(2,1)S(1)} collective-permute-done((bf16[4,33,2,128]{3,2,1,0:T(2,128)(2,1)S(1)}, bf16[4,33,2,128]{3,2,1,0:T(2,128)(2,1)S(1)}, u32[]{:S(2)}, u32[]{:S(2)}) %collective-permute-start.4) | collective-permute-done | bytes 67616 | tf_op jit(solution)/shard_map/ppermute | solution.py:563
  16.8 3.7 %collective-permute-start.5 = (bf16[4,33,2,128]{3,2,1,0:T(2,128)(2,1)S(1)}, bf16[4,33,2,128]{3,2,1,0:T(2,128)(2,1)S(1)}, u32[]{:S(2)}, u32[]{:S(2)}) collective-permute-start(bf16[4,33,2,128]{3,2,1,0:T(2,128)(2,1)S(1)} %get-tuple-element.38), channel_id=1, source_target_pairs={{0,12},{2,14},{4,8},{6,10},{8,4},{10,6},{12,0},{14,2},{16,28},{18,... | collective-permute-start | bytes 202760 | tf_op jit(solution)/shard_map/ppermute | solution.py:563
  20.4 0.0 collective-permute-start.6
  20.4 0.8 %collective-permute-start.7 = (bf16[4,33,2,128]{3,2,1,0:T(2,128)(2,1)S(1)}, bf16[4,33,2,128]{3,2,1,0:T(2,128)(2,1)S(1)}, u32[]{:S(2)}, u32[]{:S(2)}) collective-permute-start(bf16[4,33,2,128]{3,2,1,0:T(2,128)(2,1)S(1)} %get-tuple-element.40), channel_id=1, source_target_pairs={{0,8},{2,10},{4,12},{6,14},{8,0},{10,2},{12,4},{14,6},{16,24},{18,... | collective-permute-start | bytes 202760 | tf_op jit(solution)/shard_map/ppermute | solution.py:563
  21.2 1.8 %collective-permute-done.5.refs_1_ = bf16[4,33,2,128]{3,2,1,0:T(2,128)(2,1)S(1)} collective-permute-done((bf16[4,33,2,128]{3,2,1,0:T(2,128)(2,1)S(1)}, bf16[4,33,2,128]{3,2,1,0:T(2,128)(2,1)S(1)}, u32[]{:S(2)}, u32[]{:S(2)}) %collective-permute-start.5) | collective-permute-done | bytes 67616 | tf_op jit(solution)/shard_map/ppermute | solution.py:563
  23.0 1.7 %collective-permute-done.6.refs_2_ = bf16[4,33,2,128]{3,2,1,0:T(2,128)(2,1)S(1)} collective-permute-done((bf16[4,33,2,128]{3,2,1,0:T(2,128)(2,1)S(1)}, bf16[4,33,2,128]{3,2,1,0:T(2,128)(2,1)S(1)}, u32[]{:S(2)}, u32[]{:S(2)}) %collective-permute-start.6) | collective-permute-done | bytes 67616 | tf_op jit(solution)/shard_map/ppermute | solution.py:563
  24.7 0.9 %collective-permute-done.7.refs_3_ = bf16[4,33,2,128]{3,2,1,0:T(2,128)(2,1)S(1)} collective-permute-done((bf16[4,33,2,128]{3,2,1,0:T(2,128)(2,1)S(1)}, bf16[4,33,2,128]{3,2,1,0:T(2,128)(2,1)S(1)}, u32[]{:S(2)}, u32[]{:S(2)}) %collective-permute-start.7) | collective-permute-done | bytes 67616 | tf_op jit(solution)/shard_map/ppermute | solution.py:563
  25.6 0.0 copy-done
  25.6 1.2 %attend.1 = bf16[8,2048]{1,0:T(8,128)(2,1)} custom-call(bf16[128,256]{1,0:T(8,128)(2,1)S(1)} %get-tuple-element.23.queries_ref, f32[128,128]{1,0:T(8,128)S(1)} %get-tuple-element.24.score_ref, bf16[8,128,256]{2,1,0:T(8,128)(2,1)S(1)} %copy-done, bf16[4,33,2,128]{3,2,1,0:T(2,128)(2,1)S(1)} %get-tuple-element.37.refs_0_, ...), custom_call_target="tpu_custom_call" | custom-call | flops 134217728 | bytes 524288 | tf_op jit(solution)/shard_map/attend/pallas_call | solution.py:401
  (1 shorter events, 0.0 us)
Async XLA Ops:
  1.2 4.3 %collective-permute-start = (f32[96,128]{1,0:T(8,128)S(1)}, f32[96,128]{1,0:T(8,128)S(1)}, u32[]{:S(2)}, u32[]{:S(2)}) collective-permute-start(f32[96,128]{1,0:T(8,128)S(1)} %get-tuple-element.28.own_ref), channel_id=1, source_target_pairs={{0,1},{1,0},{2,3},{3,2},{4,5},{5,4},{6,7},{7,6},{8,9},{9,8},{10,11... | collective-permute-start | bytes 147464 | tf_op jit(solution)/shard_map/ppermute | solution.py:549
  1.7 3.8 %copy-start.1 = (f32[4096]{0:T(1024)S(1)}, f32[4096]{0:T(1024)}, u32[]{:S(2)}) copy-start(f32[4096]{0:T(1024)} %param.14) | copy-start | bytes 49156
  6.4 1.5 %collective-permute-start.1 = (f32[96,512]{1,0:T(8,128)S(1)}, f32[96,512]{1,0:T(8,128)S(1)}, u32[]{:S(2)}, u32[]{:S(2)}) collective-permute-start(f32[96,512]{1,0:T(8,128)S(1)} %get-tuple-element.32), channel_id=1, source_target_pairs={{0,1},{1,0},{2,3},{3,2},{4,5},{5,4},{6,7},{7,6},{8,9},{9,8},{10,11... | collective-permute-start | bytes 589832 | tf_op jit(solution)/shard_map/ppermute | solution.py:557
  6.6 1.4 %copy-start.2 = (f32[256]{0:T(256)S(1)}, f32[256]{0:T(256)}, u32[]{:S(2)}) copy-start(f32[256]{0:T(256)} %param.17) | copy-start | bytes 3076
  6.6 1.4 %copy-start.3 = (f32[256]{0:T(256)S(1)}, f32[256]{0:T(256)}, u32[]{:S(2)}) copy-start(f32[256]{0:T(256)} %param.18) | copy-start | bytes 3076
  6.6 19.1 %copy-start = (bf16[8,128,256]{2,1,0:T(8,128)(2,1)S(1)}, bf16[8,128,256]{2,1,0:T(8,128)(2,1)}, u32[]{:S(2)}) copy-start(bf16[8,128,256]{2,1,0:T(8,128)(2,1)} %cache_ref.3) | copy-start | bytes 1572868
  8.2 6.4 %collective-permute-start.2 = (bf16[4,33,2,128]{3,2,1,0:T(2,128)(2,1)S(1)}, bf16[4,33,2,128]{3,2,1,0:T(2,128)(2,1)S(1)}, u32[]{:S(2)}, u32[]{:S(2)}) collective-permute-start(bf16[4,33,2,128]{3,2,1,0:T(2,128)(2,1)S(1)} %get-tuple-element.34), channel_id=1, source_target_pairs={{0,18},{2,16},{4,22},{6,20},{8,26},{10,24},{12,30},{14,28},{16,2},... | collective-permute-start | bytes 202760 | tf_op jit(solution)/shard_map/ppermute | solution.py:563
  11.9 4.4 %collective-permute-start.3 = (bf16[4,33,2,128]{3,2,1,0:T(2,128)(2,1)S(1)}, bf16[4,33,2,128]{3,2,1,0:T(2,128)(2,1)S(1)}, u32[]{:S(2)}, u32[]{:S(2)}) collective-permute-start(bf16[4,33,2,128]{3,2,1,0:T(2,128)(2,1)S(1)} %get-tuple-element.35), channel_id=1, source_target_pairs={{0,16},{2,18},{4,20},{6,22},{8,24},{10,26},{12,28},{14,30},{16,0},... | collective-permute-start | bytes 202760 | tf_op jit(solution)/shard_map/ppermute | solution.py:563
  12.5 4.3 %collective-permute-start.4 = (bf16[4,33,2,128]{3,2,1,0:T(2,128)(2,1)S(1)}, bf16[4,33,2,128]{3,2,1,0:T(2,128)(2,1)S(1)}, u32[]{:S(2)}, u32[]{:S(2)}) collective-permute-start(bf16[4,33,2,128]{3,2,1,0:T(2,128)(2,1)S(1)} %get-tuple-element.36), channel_id=1, source_target_pairs={{0,2},{2,0},{4,6},{6,4},{8,10},{10,8},{12,14},{14,12},{16,18},{18,... | collective-permute-start | bytes 202760 | tf_op jit(solution)/shard_map/ppermute | solution.py:563
  16.8 6.3 %collective-permute-start.5 = (bf16[4,33,2,128]{3,2,1,0:T(2,128)(2,1)S(1)}, bf16[4,33,2,128]{3,2,1,0:T(2,128)(2,1)S(1)}, u32[]{:S(2)}, u32[]{:S(2)}) collective-permute-start(bf16[4,33,2,128]{3,2,1,0:T(2,128)(2,1)S(1)} %get-tuple-element.38), channel_id=1, source_target_pairs={{0,12},{2,14},{4,8},{6,10},{8,4},{10,6},{12,0},{14,2},{16,28},{18,... | collective-permute-start | bytes 202760 | tf_op jit(solution)/shard_map/ppermute | solution.py:563
  20.4 4.3 %collective-permute-start.6 = (bf16[4,33,2,128]{3,2,1,0:T(2,128)(2,1)S(1)}, bf16[4,33,2,128]{3,2,1,0:T(2,128)(2,1)S(1)}, u32[]{:S(2)}, u32[]{:S(2)}) collective-permute-start(bf16[4,33,2,128]{3,2,1,0:T(2,128)(2,1)S(1)} %get-tuple-element.39), channel_id=1, source_target_pairs={{0,4},{2,6},{4,0},{6,2},{8,12},{10,14},{12,8},{14,10},{16,20},{18,... | collective-permute-start | bytes 202760 | tf_op jit(solution)/shard_map/ppermute | solution.py:563
  20.4 5.2 %collective-permute-start.7 = (bf16[4,33,2,128]{3,2,1,0:T(2,128)(2,1)S(1)}, bf16[4,33,2,128]{3,2,1,0:T(2,128)(2,1)S(1)}, u32[]{:S(2)}, u32[]{:S(2)}) collective-permute-start(bf16[4,33,2,128]{3,2,1,0:T(2,128)(2,1)S(1)} %get-tuple-element.40), channel_id=1, source_target_pairs={{0,8},{2,10},{4,12},{6,14},{8,0},{10,2},{12,4},{14,6},{16,24},{18,... | collective-permute-start | bytes 202760 | tf_op jit(solution)/shard_map/ppermute | solution.py:563

commit v7 on v6

--- a/solution.py
+++ b/solution.py
@@ -160,14 +160,13 @@
     order = jnp.sum(to * ahead, axis=0, keepdims=True).astype(jnp.int32)
     place = lax.broadcasted_iota(jnp.int32, (slots, rows), 0)
     pick_ref[...] = (place == leaves * capacity + order).astype(jnp.bfloat16)
-    lane = (place == lands * capacity + order).astype(jnp.bfloat16)
-    ids = nt_dot((to * (local + 1).astype(jnp.float32)).astype(jnp.bfloat16), lane)
-    row = lax.broadcasted_iota(jnp.int32, ids_ref.shape, 1)
-    block = jnp.zeros(ids_ref.shape, jnp.float32)
-    for j in range(slots // HEAD):
-        part = ids[:, j * HEAD : (j + 1) * HEAD]
-        block = jnp.where(row == j, part[:, None, :], block)
-    ids_ref[...] = block
+    lane = lands * capacity + order
+    parts = slots // HEAD
+    block = lax.broadcasted_iota(jnp.int32, (partitions * parts, rows), 0)
+    named = block == leaves * parts + lane // HEAD
+    named = jnp.where(named, (local + 1).astype(jnp.float32), 0.0).astype(jnp.bfloat16)
+    spot = lax.broadcasted_iota(jnp.int32, (HEAD, rows), 0) == lane % HEAD
+    ids_ref[...] = nt_dot(named, spot.astype(jnp.bfloat16))
 
 
 def queries_of(queries_ref, head):
@@ -257,7 +256,6 @@
     slots, rows = partitions * capacity, session.shape[1]
     sessions, window, width = cache_key.shape
     heads = width // HEAD
-    id_rows = -(-slots // (8 * HEAD)) * 8
     copied = (session, start, length, queries, cache_key)
     return pl.pallas_call(
         functools.partial(beside_kernel, per_shard, capacity, stages),
@@ -265,7 +263,7 @@
             jax.ShapeDtypeStruct(w_key.shape, w_key.dtype),
             jax.ShapeDtypeStruct(w_value.shape, w_value.dtype),
             jax.ShapeDtypeStruct((slots, rows), jnp.bfloat16),
-            jax.ShapeDtypeStruct((partitions, id_rows, HEAD), jnp.float32),
+            jax.ShapeDtypeStruct((partitions * slots // HEAD, HEAD), jnp.float32),
             jax.ShapeDtypeStruct((heads * GROUP * sessions, window), jnp.float32),
             jax.ShapeDtypeStruct((heads * GROUP * sessions, width), jnp.bfloat16),
         ),
@@ -279,96 +277,91 @@
     )(here, *map(in_hbm, copied), in_hbm(w_key), in_hbm(w_value))
 
 
-def pack_kernel(
-    pick_ref,
-    ids_ref,
-    kept_ref,
-    got_ref,
-    key_bias_ref,
-    value_bias_ref,
-    *out_refs,
-):
-    partitions = ids_ref.shape[0]
-    far = partitions // len(out_refs)
-    slots = pick_ref.shape[0]
-    capacity = slots // partitions
+def pack_kernel(pick_ref, ids_ref, kept_ref, got_ref, key_bias_ref, value_bias_ref, *out_refs):
     width = key_bias_ref.shape[1]
     sums = kept_ref[...] + got_ref[...]
     key = (sums[:, :width] + key_bias_ref[...]).astype(jnp.bfloat16)
     value = (sums[:, width:] + value_bias_ref[...]).astype(jnp.bfloat16)
+    tall = pick_ref.shape[0] // len(out_refs)
     at = 0
     for source in (key, value):
-        laid = dot(pick_ref[...], source).astype(jnp.bfloat16).reshape(partitions, capacity, width)
+        laid = dot(pick_ref[...], source).astype(jnp.bfloat16)
         for column in range(0, width, HEAD):
-            part = laid[:, :, column : column + HEAD]
-            part = part.reshape(partitions, capacity // 2, 2, HEAD)
             for step, out_ref in enumerate(out_refs):
-                out_ref[:, at : at + capacity // 2] = part[step * far : (step + 1) * far]
-            at += capacity // 2
+                out_ref[at : at + tall, :] = laid[
+                    step * tall : (step + 1) * tall, column : column + HEAD
+                ]
+            at += tall
+    named = ids_ref.shape[0] // len(out_refs)
     for step, out_ref in enumerate(out_refs):
-        out_ref[:, at] = ids_ref[step * far : (step + 1) * far, :2, :].astype(jnp.bfloat16)
+        out_ref[at:, :] = ids_ref[step * named : (step + 1) * named, :].astype(jnp.bfloat16)
 
 
 def pack(pick, ids, kept, got, key_bias, value_bias, near):
     rows, width = kept.shape
-    partitions, id_rows, _ = ids.shape
-    capacity = pick.shape[0] // partitions
-    block = width // HEAD * capacity // 2 + 1
+    slots = pick.shape[0]
+    tall = (width // HEAD * slots + ids.shape[0]) // near
     return pl.pallas_call(
         pack_kernel,
-        out_shape=[jax.ShapeDtypeStruct((partitions // near, block, 2, HEAD), jnp.bfloat16)] * near,
+        out_shape=[jax.ShapeDtypeStruct((tall, HEAD), jnp.bfloat16)] * near,
         in_specs=[VMEM] * 6,
         out_specs=[VMEM] * near,
         compiler_params=params(8),
-        cost_estimate=cost(2 * rows * width * partitions * capacity, 8 * rows * width),
+        cost_estimate=cost(2 * rows * width * slots, 8 * rows * width),
         name="pack",
     )(pick, ids, kept, got, key_bias, value_bias)
 
 
-def regroup_kernel(*refs):
-    far = refs[0].shape[0]
-    got_refs, out_refs = refs[:-far], refs[-far:]
-    for step, out_ref in enumerate(out_refs):
-        for near, got_ref in enumerate(got_refs):
-            out_ref[near] = got_ref[step]
-
-
-def regroup(blocks):
-    far, *block = blocks[0].shape
-    return pl.pallas_call(
-        regroup_kernel,
-        out_shape=[jax.ShapeDtypeStruct((len(blocks), *block), jnp.bfloat16)] * far,
-        in_specs=[VMEM] * len(blocks),
+def regroup_kernel(near, vectors, capacity, *refs):
+    got_refs, out_refs = refs[:near], refs[near:]
+    far = len(out_refs)
+    for vector in range(vectors):
+        for step, out_ref in enumerate(out_refs):
+            for first, got_ref in enumerate(got_refs):
+                to, at = (vector * near + first) * capacity, (vector * far + step) * capacity
+                out_ref[to : to + capacity, :] = got_ref[at : at + capacity, :]
+    ids = sum(ref[vectors * far * capacity :, :].astype(jnp.float32) for ref in got_refs)
+    for out_ref in out_refs:
+        out_ref[vectors * near * capacity :, :] = ids.astype(jnp.bfloat16)
+
+
+def regroup(blocks, far, vectors, capacity):
+    near = len(blocks)
+    tall = blocks[0].shape[0] + vectors * capacity * (near - far)
+    return pl.pallas_call(
+        functools.partial(regroup_kernel, near, vectors, capacity),
+        out_shape=[jax.ShapeDtypeStruct((tall, HEAD), jnp.bfloat16)] * far,
+        in_specs=[VMEM] * near,
         out_specs=[VMEM] * far,
         compiler_params=params(8),
-        cost_estimate=cost(0, 4 * len(blocks) * blocks[0].size),
+        cost_estimate=cost(0, 4 * near * blocks[0].size),
         name="regroup",
     )(*blocks)
 
 
-def attend_kernel(capacity, queries_ref, score_ref, cache_ref, *refs):
+def attend_kernel(near, capacity, queries_ref, score_ref, cache_ref, *refs):
     *got_refs, out_ref = refs
     rows, window = score_ref.shape
     sessions, _, width = cache_ref.shape
     heads = width // HEAD
-    slots = len(got_refs) * got_refs[0].shape[0] * capacity
-    at = heads * capacity
-    ids = jnp.concatenate(
-        [
-            sum(jnp.sum(ref[:, at, j : j + 1, :].astype(jnp.float32), axis=0) for ref in got_refs)
-            for j in range(slots // HEAD)
-        ],
-        axis=1,
-    ).astype(jnp.int32)
+    tall = near * capacity
+    slots = len(got_refs) * tall
+    parts = slots // HEAD
+    ids = [
+        sum(
+            ref[2 * heads * tall :, :].astype(jnp.float32)[step * parts + part : step * parts + part + 1]
+            for step, ref in enumerate(got_refs)
+        )
+        for part in range(parts)
+    ]
+    ids = jnp.concatenate(ids, axis=1).astype(jnp.int32)
     own = lax.broadcasted_iota(jnp.int32, (rows, slots), 0) % sessions + 1 == ids
 
     def rows_of(vectors):
         columns = []
         for vector in vectors:
-            part = slice(vector * capacity // 2, (vector + 1) * capacity // 2)
-            columns.append(
-                jnp.concatenate([ref[:, part].reshape(-1, HEAD) for ref in got_refs], axis=0)
-            )
+            part = slice(vector * tall, (vector + 1) * tall)
+            columns.append(jnp.concatenate([ref[part, :] for ref in got_refs], axis=0))
         return jnp.concatenate(columns, axis=1)
 
     cached = score_ref[...]
@@ -397,9 +390,9 @@
             ].astype(jnp.bfloat16)
 
 
-def attend(got, queries, scores, cache_value, capacity):
-    return pl.pallas_call(
-        functools.partial(attend_kernel, capacity),
+def attend(got, queries, scores, cache_value, near, capacity):
+    return pl.pallas_call(
+        functools.partial(attend_kernel, near, capacity),
         out_shape=jax.ShapeDtypeStruct(
             (cache_value.shape[0], queries.shape[1] * GROUP), jnp.bfloat16
         ),
@@ -563,8 +556,10 @@
         sent = [lax.ppermute(a, ("grp", "seq"), p) for a, p in zip(arrays[1:], pairs[1:])]
         return [arrays[0], *sent]
 
-    got = step(regroup(step(blocks, stages[0])), stages[1])
-    return attend(got, laid, scores, cache_value, capacity)
+    near, far = stages
+    vectors = 2 * cache_key.shape[2] // HEAD
+    mid = regroup(step(blocks, near), len(far), vectors, capacity)
+    return attend(step(mid, far), laid, scores, cache_value, len(near), capacity)
 
 
 def solution(mesh):

time: 27 us -> 26.9 us (level)
  no operation moved by 1% of the time
where the time goes in v7:
time: 26.9 us; the launch traced here: 26.8 us
  starting transfers between devices  9.45 us (35%)
  waiting for transfers between devices  9.14 us (34%)
  Pallas kernels  8.12 us (30%)
    ppermute x6, starting transfers between devices, step(): lax.ppermute(a, ('grp', 'seq'), p)  8.78 us
    ppermute x6, waiting for transfers between devices, step(): lax.ppermute(a, ('grp', 'seq'), p)  8.58 us
    pallas_call x1, Pallas kernels, beside(): pl.pallas_call(functools.partial(beside_kernel, per_shard, capacity, stag...  3.75 us
    pallas_call x1, Pallas kernels, attend(): pl.pallas_call(functools.partial(attend_kernel, near, capacity), out_shap...  1.22 us
    pallas_call x1, Pallas kernels, partial_squares(): pl.pallas_call(squares_kernel, out_shape=(jax.ShapeDtypeStruct((rows, HEA...  1.21 us
    pallas_call x1, Pallas kernels, send_products(): pl.pallas_call(functools.partial(send_kernel, features), out_shape=(jax.S...  0.88 us
    pallas_call x1, Pallas kernels, keep_products(): pl.pallas_call(keep_kernel, out_shape=jax.ShapeDtypeStruct((rows, width),...  0.8 us
    ppermute x1, waiting for transfers between devices, local(): arrived = lax.ppermute(sent, 'mp', swap)  0.55 us
  transfers between devices with their start and end apart: 8, of which 7 were waited for; matrix products, arithmetic and copies ran while one was open for 0% of the time, Pallas kernels for 17%

profile of v7, /device:TPU:0, one launch (start us, length us, event | category | flops | bytes accessed | tf_op | source)
XLA Modules:
  0.0 26.8 jit_solution(16898767009610755609)
XLA Ops:
  0.0 1.2 %partial_squares.1 = (f32[96,128]{1,0:T(8,128)S(1)}, bf16[96,4096]{1,0:T(8,128)(2,1)S(1)}) custom-call(bf16[96,4096]{1,0:T(8,128)(2,1)} %frames_ref.1), custom_call_target="tpu_custom_call" | custom-call | flops 786432 | bytes 786432 | tf_op jit(solution)/shard_map/partial_squares/pallas_call | solution.py:64
  1.2 0.5 %collective-permute-start = (f32[96,128]{1,0:T(8,128)S(1)}, f32[96,128]{1,0:T(8,128)S(1)}, u32[]{:S(2)}, u32[]{:S(2)}) collective-permute-start(f32[96,128]{1,0:T(8,128)S(1)} %get-tuple-element.28.own_ref), channel_id=1, source_target_pairs={{0,1},{1,0},{2,3},{3,2},{4,5},{5,4},{6,7},{7,6},{8,9},{9,8},{10,11... | collective-permute-start | bytes 147464 | tf_op jit(solution)/shard_map/ppermute | solution.py:542
  1.7 0.0 copy-start.1
  1.7 3.8 %beside.1 = (bf16[4096,512]{1,0:T(8,128)(2,1)S(1)}, bf16[4096,512]{1,0:T(8,128)(2,1)S(1)}, bf16[256,96]{1,0:T(8,128)(2,1)S(1)}, f32[32,128]{1,0:T(8,128)S(1)}, f...) custom-call(s32[1]{0:T(128)} %bitcast.here_ref, s32[1,96]{1,0:T(1,128)} %bitcast.11, s32[1,8]{1,0:T(1,128)} %bitcast.12, ...), custom_call_target="tpu_custom_call" | custom-call | flops 33554432 | bytes 8388608 | tf_op jit(solution)/shard_map/beside/pallas_call | solution.py:260
  5.5 0.0 collective-permute-done.other_ref
  5.5 0.0 copy-done.1
  5.5 0.9 %send_products.1 = (bf16[96,4096]{1,0:T(8,128)(2,1)S(1)}, f32[96,512]{1,0:T(8,128)S(1)}) custom-call(s32[1]{0:T(128)} %bitcast.4.index_ref, bf16[96,4096]{1,0:T(8,128)(2,1)S(1)} %get-tuple-element.27.frames_ref, f32[96,128]{1,0:T(8,128)S(1)} %get-tuple-element.28.own_ref, f32[96,128]{1,0:T(8,128)S(1)} %collective-permute-done.other_ref, ...), custom_call_target="tpu_custom_call" | custom-call | flops 402653184 | bytes 4194304 | tf_op jit(solution)/shard_map/send_products/pallas_call | solution.py:97
  6.4 0.1 collective-permute-start.1
  6.6 0.0 copy-start.2
  6.6 0.0 copy-start.3
  6.6 0.0 copy-start
  6.6 0.8 %keep_products.1.kept_ref = f32[96,512]{1,0:T(8,128)S(1)} custom-call(s32[1]{0:T(128)} %bitcast.4.index_ref, bf16[96,4096]{1,0:T(8,128)(2,1)S(1)} %get-tuple-element.31.normed_ref, bf16[4096,512]{1,0:T(8,128)(2,1)S(1)} %get-tuple-element.29.key_ref, bf16[4096,512]{1,0:T(8,128)(2,1)S(1)} %get-tuple-element.30.value_ref), custom_call_target="tpu_custom_call" | custom-call | flops 402653184 | bytes 4194304 | tf_op jit(solution)/shard_map/keep_products/pallas_call | solution.py:118
  7.4 0.6 %collective-permute-done.1.got_ref = f32[96,512]{1,0:T(8,128)S(1)} collective-permute-done((f32[96,512]{1,0:T(8,128)S(1)}, f32[96,512]{1,0:T(8,128)S(1)}, u32[]{:S(2)}, u32[]{:S(2)}) %collective-permute-start.1) | collective-permute-done | bytes 196640 | tf_op jit(solution)/shard_map/ppermute | solution.py:550
  7.9 0.0 copy-done.2
  7.9 0.0 copy-done.3
  7.9 0.2 pack.1
  8.1 3.7 %collective-permute-start.2 = (bf16[264,128]{1,0:T(8,128)(2,1)S(1)}, bf16[264,128]{1,0:T(8,128)(2,1)S(1)}, u32[]{:S(2)}, u32[]{:S(2)}) collective-permute-start(bf16[264,128]{1,0:T(8,128)(2,1)S(1)} %get-tuple-element.34), channel_id=1, source_target_pairs={{0,18},{2,16},{4,22},{6,20},{8,26},{10,24},{12,30},{14,28},{16,2},... | collective-permute-start | bytes 202760 | tf_op jit(solution)/shard_map/ppermute | solution.py:556
  11.8 0.5 %collective-permute-start.3 = (bf16[264,128]{1,0:T(8,128)(2,1)S(1)}, bf16[264,128]{1,0:T(8,128)(2,1)S(1)}, u32[]{:S(2)}, u32[]{:S(2)}) collective-permute-start(bf16[264,128]{1,0:T(8,128)(2,1)S(1)} %get-tuple-element.35), channel_id=1, source_target_pairs={{0,16},{2,18},{4,20},{6,22},{8,24},{10,26},{12,28},{14,30},{16,0},... | collective-permute-start | bytes 202760 | tf_op jit(solution)/shard_map/ppermute | solution.py:556
  12.4 0.1 collective-permute-start.4
  12.5 2.0 %collective-permute-done.2.refs_1_ = bf16[264,128]{1,0:T(8,128)(2,1)S(1)} collective-permute-done((bf16[264,128]{1,0:T(8,128)(2,1)S(1)}, bf16[264,128]{1,0:T(8,128)(2,1)S(1)}, u32[]{:S(2)}, u32[]{:S(2)}) %collective-permute-start.2) | collective-permute-done | bytes 67616 | tf_op jit(solution)/shard_map/ppermute | solution.py:556
  14.5 1.7 %collective-permute-done.3.refs_2_ = bf16[264,128]{1,0:T(8,128)(2,1)S(1)} collective-permute-done((bf16[264,128]{1,0:T(8,128)(2,1)S(1)}, bf16[264,128]{1,0:T(8,128)(2,1)S(1)}, u32[]{:S(2)}, u32[]{:S(2)}) %collective-permute-start.3) | collective-permute-done | bytes 67616 | tf_op jit(solution)/shard_map/ppermute | solution.py:556
  16.2 0.5 %collective-permute-done.4.refs_3_ = bf16[264,128]{1,0:T(8,128)(2,1)S(1)} collective-permute-done((bf16[264,128]{1,0:T(8,128)(2,1)S(1)}, bf16[264,128]{1,0:T(8,128)(2,1)S(1)}, u32[]{:S(2)}, u32[]{:S(2)}) %collective-permute-start.4) | collective-permute-done | bytes 67616 | tf_op jit(solution)/shard_map/ppermute | solution.py:556
  16.7 3.7 %collective-permute-start.5 = (bf16[264,128]{1,0:T(8,128)(2,1)S(1)}, bf16[264,128]{1,0:T(8,128)(2,1)S(1)}, u32[]{:S(2)}, u32[]{:S(2)}) collective-permute-start(bf16[264,128]{1,0:T(8,128)(2,1)S(1)} %get-tuple-element.38), channel_id=1, source_target_pairs={{0,12},{2,14},{4,8},{6,10},{8,4},{10,6},{12,0},{14,2},{16,28},{18,... | collective-permute-start | bytes 202760 | tf_op jit(solution)/shard_map/ppermute | solution.py:556
  20.4 0.0 collective-permute-start.6
  20.4 0.8 %collective-permute-start.7 = (bf16[264,128]{1,0:T(8,128)(2,1)S(1)}, bf16[264,128]{1,0:T(8,128)(2,1)S(1)}, u32[]{:S(2)}, u32[]{:S(2)}) collective-permute-start(bf16[264,128]{1,0:T(8,128)(2,1)S(1)} %get-tuple-element.40), channel_id=1, source_target_pairs={{0,8},{2,10},{4,12},{6,14},{8,0},{10,2},{12,4},{14,6},{16,24},{18,... | collective-permute-start | bytes 202760 | tf_op jit(solution)/shard_map/ppermute | solution.py:556
  21.1 1.8 %collective-permute-done.5.refs_1_ = bf16[264,128]{1,0:T(8,128)(2,1)S(1)} collective-permute-done((bf16[264,128]{1,0:T(8,128)(2,1)S(1)}, bf16[264,128]{1,0:T(8,128)(2,1)S(1)}, u32[]{:S(2)}, u32[]{:S(2)}) %collective-permute-start.5) | collective-permute-done | bytes 67616 | tf_op jit(solution)/shard_map/ppermute | solution.py:556
  23.0 1.7 %collective-permute-done.6.refs_2_ = bf16[264,128]{1,0:T(8,128)(2,1)S(1)} collective-permute-done((bf16[264,128]{1,0:T(8,128)(2,1)S(1)}, bf16[264,128]{1,0:T(8,128)(2,1)S(1)}, u32[]{:S(2)}, u32[]{:S(2)}) %collective-permute-start.6) | collective-permute-done | bytes 67616 | tf_op jit(solution)/shard_map/ppermute | solution.py:556
  24.6 0.9 %collective-permute-done.7.refs_3_ = bf16[264,128]{1,0:T(8,128)(2,1)S(1)} collective-permute-done((bf16[264,128]{1,0:T(8,128)(2,1)S(1)}, bf16[264,128]{1,0:T(8,128)(2,1)S(1)}, u32[]{:S(2)}, u32[]{:S(2)}) %collective-permute-start.7) | collective-permute-done | bytes 67616 | tf_op jit(solution)/shard_map/ppermute | solution.py:556
  25.5 0.0 copy-done
  25.5 1.2 %attend.1 = bf16[8,2048]{1,0:T(8,128)(2,1)} custom-call(bf16[128,256]{1,0:T(8,128)(2,1)S(1)} %get-tuple-element.23.queries_ref, f32[128,128]{1,0:T(8,128)S(1)} %get-tuple-element.24.score_ref, bf16[8,128,256]{2,1,0:T(8,128)(2,1)S(1)} %copy-done, bf16[264,128]{1,0:T(8,128)(2,1)S(1)} %get-tuple-element.37.refs_0_, ...), custom_call_target="tpu_custom_call" | custom-call | flops 134217728 | bytes 524288 | tf_op jit(solution)/shard_map/attend/pallas_call | solution.py:394
  (1 shorter events, 0.0 us)
Async XLA Ops:
  1.2 4.3 %collective-permute-start = (f32[96,128]{1,0:T(8,128)S(1)}, f32[96,128]{1,0:T(8,128)S(1)}, u32[]{:S(2)}, u32[]{:S(2)}) collective-permute-start(f32[96,128]{1,0:T(8,128)S(1)} %get-tuple-element.28.own_ref), channel_id=1, source_target_pairs={{0,1},{1,0},{2,3},{3,2},{4,5},{5,4},{6,7},{7,6},{8,9},{9,8},{10,11... | collective-permute-start | bytes 147464 | tf_op jit(solution)/shard_map/ppermute | solution.py:542
  1.7 3.8 %copy-start.1 = (f32[4096]{0:T(1024)S(1)}, f32[4096]{0:T(1024)}, u32[]{:S(2)}) copy-start(f32[4096]{0:T(1024)} %param.14) | copy-start | bytes 49156
  6.4 1.5 %collective-permute-start.1 = (f32[96,512]{1,0:T(8,128)S(1)}, f32[96,512]{1,0:T(8,128)S(1)}, u32[]{:S(2)}, u32[]{:S(2)}) collective-permute-start(f32[96,512]{1,0:T(8,128)S(1)} %get-tuple-element.32), channel_id=1, source_target_pairs={{0,1},{1,0},{2,3},{3,2},{4,5},{5,4},{6,7},{7,6},{8,9},{9,8},{10,11... | collective-permute-start | bytes 589832 | tf_op jit(solution)/shard_map/ppermute | solution.py:550
  6.6 1.4 %copy-start.2 = (f32[256]{0:T(256)S(1)}, f32[256]{0:T(256)}, u32[]{:S(2)}) copy-start(f32[256]{0:T(256)} %param.17) | copy-start | bytes 3076
  6.6 1.4 %copy-start.3 = (f32[256]{0:T(256)S(1)}, f32[256]{0:T(256)}, u32[]{:S(2)}) copy-start(f32[256]{0:T(256)} %param.18) | copy-start | bytes 3076
  6.6 19.0 %copy-start = (bf16[8,128,256]{2,1,0:T(8,128)(2,1)S(1)}, bf16[8,128,256]{2,1,0:T(8,128)(2,1)}, u32[]{:S(2)}) copy-start(bf16[8,128,256]{2,1,0:T(8,128)(2,1)} %cache_ref.3) | copy-start | bytes 1572868
  8.1 6.4 %collective-permute-start.2 = (bf16[264,128]{1,0:T(8,128)(2,1)S(1)}, bf16[264,128]{1,0:T(8,128)(2,1)S(1)}, u32[]{:S(2)}, u32[]{:S(2)}) collective-permute-start(bf16[264,128]{1,0:T(8,128)(2,1)S(1)} %get-tuple-element.34), channel_id=1, source_target_pairs={{0,18},{2,16},{4,22},{6,20},{8,26},{10,24},{12,30},{14,28},{16,2},... | collective-permute-start | bytes 202760 | tf_op jit(solution)/shard_map/ppermute | solution.py:556
  11.8 4.4 %collective-permute-start.3 = (bf16[264,128]{1,0:T(8,128)(2,1)S(1)}, bf16[264,128]{1,0:T(8,128)(2,1)S(1)}, u32[]{:S(2)}, u32[]{:S(2)}) collective-permute-start(bf16[264,128]{1,0:T(8,128)(2,1)S(1)} %get-tuple-element.35), channel_id=1, source_target_pairs={{0,16},{2,18},{4,20},{6,22},{8,24},{10,26},{12,28},{14,30},{16,0},... | collective-permute-start | bytes 202760 | tf_op jit(solution)/shard_map/ppermute | solution.py:556
  12.4 4.3 %collective-permute-start.4 = (bf16[264,128]{1,0:T(8,128)(2,1)S(1)}, bf16[264,128]{1,0:T(8,128)(2,1)S(1)}, u32[]{:S(2)}, u32[]{:S(2)}) collective-permute-start(bf16[264,128]{1,0:T(8,128)(2,1)S(1)} %get-tuple-element.36), channel_id=1, source_target_pairs={{0,2},{2,0},{4,6},{6,4},{8,10},{10,8},{12,14},{14,12},{16,18},{18,... | collective-permute-start | bytes 202760 | tf_op jit(solution)/shard_map/ppermute | solution.py:556
  16.7 6.3 %collective-permute-start.5 = (bf16[264,128]{1,0:T(8,128)(2,1)S(1)}, bf16[264,128]{1,0:T(8,128)(2,1)S(1)}, u32[]{:S(2)}, u32[]{:S(2)}) collective-permute-start(bf16[264,128]{1,0:T(8,128)(2,1)S(1)} %get-tuple-element.38), channel_id=1, source_target_pairs={{0,12},{2,14},{4,8},{6,10},{8,4},{10,6},{12,0},{14,2},{16,28},{18,... | collective-permute-start | bytes 202760 | tf_op jit(solution)/shard_map/ppermute | solution.py:556
  20.4 4.3 %collective-permute-start.6 = (bf16[264,128]{1,0:T(8,128)(2,1)S(1)}, bf16[264,128]{1,0:T(8,128)(2,1)S(1)}, u32[]{:S(2)}, u32[]{:S(2)}) collective-permute-start(bf16[264,128]{1,0:T(8,128)(2,1)S(1)} %get-tuple-element.39), channel_id=1, source_target_pairs={{0,4},{2,6},{4,0},{6,2},{8,12},{10,14},{12,8},{14,10},{16,20},{18,... | collective-permute-start | bytes 202760 | tf_op jit(solution)/shard_map/ppermute | solution.py:556
  20.4 5.2 %collective-permute-start.7 = (bf16[264,128]{1,0:T(8,128)(2,1)S(1)}, bf16[264,128]{1,0:T(8,128)(2,1)S(1)}, u32[]{:S(2)}, u32[]{:S(2)}) collective-permute-start(bf16[264,128]{1,0:T(8,128)(2,1)S(1)} %get-tuple-element.40), channel_id=1, source_target_pairs={{0,8},{2,10},{4,12},{6,14},{8,0},{10,2},{12,4},{14,6},{16,24},{18,... | collective-permute-start | bytes 202760 | tf_op jit(solution)/shard_map/ppermute | solution.py:556

commit v8 on v7

--- a/solution.py
+++ b/solution.py
@@ -209,33 +209,19 @@
     stages,
     here_ref,
     session_ref,
-    start_ref,
-    len_ref,
-    queries_ref,
-    cache_ref,
     w_key_ref,
     w_value_ref,
     held_key_ref,
     held_value_ref,
     pick_ref,
     ids_ref,
-    score_ref,
-    laid_ref,
     session,
-    start,
-    length,
-    queries,
-    cache,
     arrived,
 ):
     copies = []
     for at, (source, held) in enumerate(
         (
             (session_ref, session),
-            (start_ref, start),
-            (len_ref, length),
-            (queries_ref, queries),
-            (cache_ref, cache),
             (w_key_ref, held_key_ref),
             (w_value_ref, held_value_ref),
         )
@@ -244,19 +230,13 @@
         copies[-1].start()
     copies[0].wait()
     route(per_shard, capacity, stages, here_ref[0], session[...], pick_ref, ids_ref)
-    for copy in copies[1:5]:
+    for copy in copies[1:]:
         copy.wait()
-    score_cache(start, length, queries, cache, score_ref, laid_ref)
-    for copy in copies[5:]:
-        copy.wait()
-
-
-def beside(here, session, start, length, queries, cache_key, w_key, w_value, sizes):
+
+
+def beside(here, session, w_key, w_value, sizes):
     partitions, per_shard, capacity, stages = sizes
     slots, rows = partitions * capacity, session.shape[1]
-    sessions, window, width = cache_key.shape
-    heads = width // HEAD
-    copied = (session, start, length, queries, cache_key)
     return pl.pallas_call(
         functools.partial(beside_kernel, per_shard, capacity, stages),
         out_shape=(
@@ -264,17 +244,31 @@
             jax.ShapeDtypeStruct(w_value.shape, w_value.dtype),
             jax.ShapeDtypeStruct((slots, rows), jnp.bfloat16),
             jax.ShapeDtypeStruct((partitions * slots // HEAD, HEAD), jnp.float32),
-            jax.ShapeDtypeStruct((heads * GROUP * sessions, window), jnp.float32),
-            jax.ShapeDtypeStruct((heads * GROUP * sessions, width), jnp.bfloat16),
         ),
-        in_specs=[SMEM] + [HBM] * 7,
-        out_specs=(VMEM,) * 6,
-        scratch_shapes=[pltpu.VMEM(array.shape, array.dtype) for array in copied]
-        + [pltpu.SemaphoreType.DMA((7,))],
+        in_specs=[SMEM] + [HBM] * 3,
+        out_specs=(VMEM,) * 4,
+        scratch_shapes=[pltpu.VMEM(session.shape, session.dtype), pltpu.SemaphoreType.DMA((3,))],
         compiler_params=params(24),
-        cost_estimate=cost(2 * GROUP * sessions * cache_key.size, 4 * w_key.size),
+        cost_estimate=cost(4 * rows * rows * slots, 4 * w_key.size),
         name="beside",
-    )(here, *map(in_hbm, copied), in_hbm(w_key), in_hbm(w_value))
+    )(here, in_hbm(session), in_hbm(w_key), in_hbm(w_value))
+
+
+def cached_scores(start, length, queries, cache_key):
+    sessions, window, width = cache_key.shape
+    rows = width // HEAD * GROUP * sessions
+    return pl.pallas_call(
+        score_cache,
+        out_shape=(
+            jax.ShapeDtypeStruct((rows, window), jnp.float32),
+            jax.ShapeDtypeStruct((rows, width), jnp.bfloat16),
+        ),
+        in_specs=[VMEM] * 4,
+        out_specs=(VMEM, VMEM),
+        compiler_params=params(8),
+        cost_estimate=cost(2 * GROUP * sessions * cache_key.size, 2 * cache_key.size),
+        name="cached_scores",
+    )(start, length, queries, cache_key)
 
 
 def pack_kernel(pick_ref, ids_ref, kept_ref, got_ref, key_bias_ref, value_bias_ref, *out_refs):
@@ -540,9 +534,8 @@
     here = lax.axis_index(("grp", "seq")).astype(jnp.int32).reshape(1)
     own, held = partial_squares(frames)
     other = lax.ppermute(own, "mp", swap)
-    held_key, held_value, pick, ids, scores, laid = beside(
-        here, token_session[None, :], cache_start[None, :], cache_len[None, :], queries, cache_key, w_key,
-        w_value, (partitions, per_shard, capacity, stages),
+    held_key, held_value, pick, ids = beside(
+        here, token_session[None, :], w_key, w_value, (partitions, per_shard, capacity, stages)
     )
     normed, sent = send_products(
         index, held, own, other, ln_gain[None, :], held_key, held_value, frames.shape[1] * shares
@@ -558,6 +551,8 @@
 
     near, far = stages
     vectors = 2 * cache_key.shape[2] // HEAD
+    queries, *blocks = lax.optimization_barrier((queries, *blocks))
+    scores, laid = cached_scores(cache_start[None, :], cache_len[None, :], queries, cache_key)
     mid = regroup(step(blocks, near), len(far), vectors, capacity)
     return attend(step(mid, far), laid, scores, cache_value, len(near), capacity)
 

time: 26.9 us -> 26.7 us (level)
  waiting for transfers between devices: 9.14 us -> 8.61 us
    ppermute x6, waiting for transfers between devices: 8.58 us -> 8.1 us  [step(): lax.ppermute(a, ('grp', 'seq'), p)]
    pallas_call x0 -> x1, Pallas kernels: none -> 0.45 us  [cached_scores(): pl.pallas_call(score_cache, out_shape=(jax.ShapeDtypeStruct((rows, window...]
  transfers between devices with their start and end apart: 8 -> 8, of which waited for: 7 -> 7; matrix products, arithmetic and copies ran while one was open for 0% -> 0% of each run, Pallas kernels for 17% -> 18%
where the time goes in v8:
time: 26.7 us; the launch traced here: 26.5 us
  starting transfers between devices  9.45 us (35%)
  waiting for transfers between devices  8.61 us (32%)
  Pallas kernels  8.34 us (31%)
    ppermute x6, starting transfers between devices, step(): lax.ppermute(a, ('grp', 'seq'), p)  8.78 us
    ppermute x6, waiting for transfers between devices, step(): lax.ppermute(a, ('grp', 'seq'), p)  8.1 us
    pallas_call x1, Pallas kernels, beside(): pl.pallas_call(functools.partial(beside_kernel, per_shard, capacity, stag...  3.51 us
    pallas_call x1, Pallas kernels, attend(): pl.pallas_call(functools.partial(attend_kernel, near, capacity), out_shap...  1.23 us
    pallas_call x1, Pallas kernels, partial_squares(): pl.pallas_call(squares_kernel, out_shape=(jax.ShapeDtypeStruct((rows, HEA...  1.21 us
    pallas_call x1, Pallas kernels, send_products(): pl.pallas_call(functools.partial(send_kernel, features), out_shape=(jax.S...  0.88 us
    pallas_call x1, Pallas kernels, keep_products(): pl.pallas_call(keep_kernel, out_shape=jax.ShapeDtypeStruct((rows, width),...  0.8 us
  transfers between devices with their start and end apart: 8, of which 7 were waited for; matrix products, arithmetic and copies ran while one was open for 0% of the time, Pallas kernels for 18%

profile of v8, /device:TPU:0, one launch (start us, length us, event | category | flops | bytes accessed | tf_op | source)
XLA Modules:
  0.0 26.5 jit_solution(15653629349360508008)
XLA Ops:
  0.0 1.2 %partial_squares.1 = (f32[96,128]{1,0:T(8,128)S(1)}, bf16[96,4096]{1,0:T(8,128)(2,1)S(1)}) custom-call(bf16[96,4096]{1,0:T(8,128)(2,1)} %frames_ref.1), custom_call_target="tpu_custom_call" | custom-call | flops 786432 | bytes 786432 | tf_op jit(solution)/shard_map/partial_squares/pallas_call | solution.py:64
  1.2 0.5 %collective-permute-start = (f32[96,128]{1,0:T(8,128)S(1)}, f32[96,128]{1,0:T(8,128)S(1)}, u32[]{:S(2)}, u32[]{:S(2)}) collective-permute-start(f32[96,128]{1,0:T(8,128)S(1)} %get-tuple-element.31.own_ref), channel_id=1, source_target_pairs={{0,1},{1,0},{2,3},{3,2},{4,5},{5,4},{6,7},{7,6},{8,9},{9,8},{10,11... | collective-permute-start | bytes 147464 | tf_op jit(solution)/shard_map/ppermute | solution.py:536
  1.7 0.0 copy-start.3
  1.7 3.5 %beside.1 = (bf16[4096,512]{1,0:T(8,128)(2,1)S(1)}, bf16[4096,512]{1,0:T(8,128)(2,1)S(1)}, bf16[256,96]{1,0:T(8,128)(2,1)S(1)}, f32[32,128]{1,0:T(8,128)S(1)}) custom-call(s32[1]{0:T(128)} %bitcast.2.here_ref, s32[1,96]{1,0:T(1,128)} %bitcast.13, bf16[4096,512]{1,0:T(8,128)(2,1)} %w_key_ref.1, bf16[4096,512]{1,0:T(8,128)(2,1)} %w_value_ref.1), custom_call_target="tpu_custom_call" | custom-call | flops 9437184 | bytes 8388608 | tf_op jit(solution)/shard_map/beside/pallas_call | solution.py:240
  5.3 0.0 collective-permute-done.other_ref
  5.3 0.0 copy-done.3
  5.3 0.9 %send_products.1 = (bf16[96,4096]{1,0:T(8,128)(2,1)S(1)}, f32[96,512]{1,0:T(8,128)S(1)}) custom-call(s32[1]{0:T(128)} %bitcast.4.index_ref, bf16[96,4096]{1,0:T(8,128)(2,1)S(1)} %get-tuple-element.30.frames_ref, f32[96,128]{1,0:T(8,128)S(1)} %get-tuple-element.31.own_ref, f32[96,128]{1,0:T(8,128)S(1)} %collective-permute-done.other_ref, ...), custom_call_target="tpu_custom_call" | custom-call | flops 402653184 | bytes 4194304 | tf_op jit(solution)/shard_map/send_products/pallas_call | solution.py:97
  6.2 0.2 collective-permute-start.1
  6.3 0.0 copy-start.4
  6.3 0.0 copy-start.5
  6.3 0.0 copy-start
  6.3 0.0 copy-start.2
  6.3 0.0 copy-start.6
  6.3 0.0 copy-start.7
  6.4 0.0 copy-start.1
  6.4 0.8 %keep_products.1.kept_ref = f32[96,512]{1,0:T(8,128)S(1)} custom-call(s32[1]{0:T(128)} %bitcast.4.index_ref, bf16[96,4096]{1,0:T(8,128)(2,1)S(1)} %get-tuple-element.34.normed_ref, bf16[4096,512]{1,0:T(8,128)(2,1)S(1)} %get-tuple-element.32.key_ref, bf16[4096,512]{1,0:T(8,128)(2,1)S(1)} %get-tuple-element.33.value_ref), custom_call_target="tpu_custom_call" | custom-call | flops 402653184 | bytes 4194304 | tf_op jit(solution)/shard_map/keep_products/pallas_call | solution.py:118
  7.2 0.5 %collective-permute-done.1.got_ref = f32[96,512]{1,0:T(8,128)S(1)} collective-permute-done((f32[96,512]{1,0:T(8,128)S(1)}, f32[96,512]{1,0:T(8,128)S(1)}, u32[]{:S(2)}, u32[]{:S(2)}) %collective-permute-start.1) | collective-permute-done | bytes 196640 | tf_op jit(solution)/shard_map/ppermute | solution.py:543
  7.7 0.0 copy-done.4
  7.7 0.0 copy-done.5
  7.7 0.2 pack.1
  7.9 3.7 %collective-permute-start.2 = (bf16[264,128]{1,0:T(8,128)(2,1)S(1)}, bf16[264,128]{1,0:T(8,128)(2,1)S(1)}, u32[]{:S(2)}, u32[]{:S(2)}) collective-permute-start(bf16[264,128]{1,0:T(8,128)(2,1)S(1)} %get-tuple-element.44), channel_id=1, source_target_pairs={{0,18},{2,16},{4,22},{6,20},{8,26},{10,24},{12,30},{14,28},{16,2},... | collective-permute-start | bytes 202760 | tf_op jit(solution)/shard_map/ppermute | solution.py:549
  11.6 0.5 %collective-permute-start.3 = (bf16[264,128]{1,0:T(8,128)(2,1)S(1)}, bf16[264,128]{1,0:T(8,128)(2,1)S(1)}, u32[]{:S(2)}, u32[]{:S(2)}) collective-permute-start(bf16[264,128]{1,0:T(8,128)(2,1)S(1)} %get-tuple-element.45), channel_id=1, source_target_pairs={{0,16},{2,18},{4,20},{6,22},{8,24},{10,26},{12,28},{14,30},{16,0},... | collective-permute-start | bytes 202760 | tf_op jit(solution)/shard_map/ppermute | solution.py:549
  12.1 0.1 collective-permute-start.4
  12.2 2.0 %collective-permute-done.2.refs_1_ = bf16[264,128]{1,0:T(8,128)(2,1)S(1)} collective-permute-done((bf16[264,128]{1,0:T(8,128)(2,1)S(1)}, bf16[264,128]{1,0:T(8,128)(2,1)S(1)}, u32[]{:S(2)}, u32[]{:S(2)}) %collective-permute-start.2) | collective-permute-done | bytes 67616 | tf_op jit(solution)/shard_map/ppermute | solution.py:549
  14.3 1.7 %collective-permute-done.3.refs_2_ = bf16[264,128]{1,0:T(8,128)(2,1)S(1)} collective-permute-done((bf16[264,128]{1,0:T(8,128)(2,1)S(1)}, bf16[264,128]{1,0:T(8,128)(2,1)S(1)}, u32[]{:S(2)}, u32[]{:S(2)}) %collective-permute-start.3) | collective-permute-done | bytes 67616 | tf_op jit(solution)/shard_map/ppermute | solution.py:549
  15.9 0.5 %collective-permute-done.4.refs_3_ = bf16[264,128]{1,0:T(8,128)(2,1)S(1)} collective-permute-done((bf16[264,128]{1,0:T(8,128)(2,1)S(1)}, bf16[264,128]{1,0:T(8,128)(2,1)S(1)}, u32[]{:S(2)}, u32[]{:S(2)}) %collective-permute-start.4) | collective-permute-done | bytes 67616 | tf_op jit(solution)/shard_map/ppermute | solution.py:549
  16.4 3.7 %collective-permute-start.5 = (bf16[264,128]{1,0:T(8,128)(2,1)S(1)}, bf16[264,128]{1,0:T(8,128)(2,1)S(1)}, u32[]{:S(2)}, u32[]{:S(2)}) collective-permute-start(bf16[264,128]{1,0:T(8,128)(2,1)S(1)} %get-tuple-element.48), channel_id=1, source_target_pairs={{0,12},{2,14},{4,8},{6,10},{8,4},{10,6},{12,0},{14,2},{16,28},{18,... | collective-permute-start | bytes 202760 | tf_op jit(solution)/shard_map/ppermute | solution.py:549
  20.1 0.0 collective-permute-start.6
  20.1 0.8 %collective-permute-start.7 = (bf16[264,128]{1,0:T(8,128)(2,1)S(1)}, bf16[264,128]{1,0:T(8,128)(2,1)S(1)}, u32[]{:S(2)}, u32[]{:S(2)}) collective-permute-start(bf16[264,128]{1,0:T(8,128)(2,1)S(1)} %get-tuple-element.50), channel_id=1, source_target_pairs={{0,8},{2,10},{4,12},{6,14},{8,0},{10,2},{12,4},{14,6},{16,24},{18,... | collective-permute-start | bytes 202760 | tf_op jit(solution)/shard_map/ppermute | solution.py:549
  20.9 0.0 copy-done
  20.9 0.0 copy-done.2
  20.9 0.0 copy-done.6
  20.9 0.0 copy-done.7
  20.9 0.5 %cached_scores.1 = (f32[128,128]{1,0:T(8,128)S(1)}, bf16[128,256]{1,0:T(8,128)(2,1)S(1)}) custom-call(s32[1,8]{1,0:T(1,128)S(1)} %bitcast.11, s32[1,8]{1,0:T(1,128)S(1)} %bitcast.12, bf16[8,2048]{1,0:T(8,128)(2,1)S(1)} %copy-done.2, bf16[8,128,256]{2,1,0:T(8,128)(2,1)S(1)} %copy-done), custom_call_target="tpu_custom_call" | custom-call | flops 33554432 | bytes 524288 | tf_op jit(solution)/shard_map/cached_scores/pallas_call | solution.py:260
  21.4 1.3 %collective-permute-done.5.refs_1_ = bf16[264,128]{1,0:T(8,128)(2,1)S(1)} collective-permute-done((bf16[264,128]{1,0:T(8,128)(2,1)S(1)}, bf16[264,128]{1,0:T(8,128)(2,1)S(1)}, u32[]{:S(2)}, u32[]{:S(2)}) %collective-permute-start.5) | collective-permute-done | bytes 67616 | tf_op jit(solution)/shard_map/ppermute | solution.py:549
  22.7 1.7 %collective-permute-done.6.refs_2_ = bf16[264,128]{1,0:T(8,128)(2,1)S(1)} collective-permute-done((bf16[264,128]{1,0:T(8,128)(2,1)S(1)}, bf16[264,128]{1,0:T(8,128)(2,1)S(1)}, u32[]{:S(2)}, u32[]{:S(2)}) %collective-permute-start.6) | collective-permute-done | bytes 67616 | tf_op jit(solution)/shard_map/ppermute | solution.py:549
  24.4 0.9 %collective-permute-done.7.refs_3_ = bf16[264,128]{1,0:T(8,128)(2,1)S(1)} collective-permute-done((bf16[264,128]{1,0:T(8,128)(2,1)S(1)}, bf16[264,128]{1,0:T(8,128)(2,1)S(1)}, u32[]{:S(2)}, u32[]{:S(2)}) %collective-permute-start.7) | collective-permute-done | bytes 67616 | tf_op jit(solution)/shard_map/ppermute | solution.py:549
  25.3 0.0 copy-done.1
  25.3 1.2 %attend.1 = bf16[8,2048]{1,0:T(8,128)(2,1)} custom-call(bf16[128,256]{1,0:T(8,128)(2,1)S(1)} %get-tuple-element.41.queries_ref, f32[128,128]{1,0:T(8,128)S(1)} %get-tuple-element.42.score_ref, bf16[8,128,256]{2,1,0:T(8,128)(2,1)S(1)} %copy-done.1, bf16[264,128]{1,0:T(8,128)(2,1)S(1)} %get-tuple-element.47.refs_0_, ...), custom_call_target="tpu_custom_call" | custom-call | flops 134217728 | bytes 524288 | tf_op jit(solution)/shard_map/attend/pallas_call | solution.py:388
  (1 shorter events, 0.0 us)
Async XLA Ops:
  1.2 4.0 %collective-permute-start = (f32[96,128]{1,0:T(8,128)S(1)}, f32[96,128]{1,0:T(8,128)S(1)}, u32[]{:S(2)}, u32[]{:S(2)}) collective-permute-start(f32[96,128]{1,0:T(8,128)S(1)} %get-tuple-element.31.own_ref), channel_id=1, source_target_pairs={{0,1},{1,0},{2,3},{3,2},{4,5},{5,4},{6,7},{7,6},{8,9},{9,8},{10,11... | collective-permute-start | bytes 147464 | tf_op jit(solution)/shard_map/ppermute | solution.py:536
  1.7 3.5 %copy-start.3 = (f32[4096]{0:T(1024)S(1)}, f32[4096]{0:T(1024)}, u32[]{:S(2)}) copy-start(f32[4096]{0:T(1024)} %param.14) | copy-start | bytes 49156
  6.2 1.5 %collective-permute-start.1 = (f32[96,512]{1,0:T(8,128)S(1)}, f32[96,512]{1,0:T(8,128)S(1)}, u32[]{:S(2)}, u32[]{:S(2)}) collective-permute-start(f32[96,512]{1,0:T(8,128)S(1)} %get-tuple-element.35), channel_id=1, source_target_pairs={{0,1},{1,0},{2,3},{3,2},{4,5},{5,4},{6,7},{7,6},{8,9},{9,8},{10,11... | collective-permute-start | bytes 589832 | tf_op jit(solution)/shard_map/ppermute | solution.py:543
  6.3 1.4 %copy-start.4 = (f32[256]{0:T(256)S(1)}, f32[256]{0:T(256)}, u32[]{:S(2)}) copy-start(f32[256]{0:T(256)} %param.17) | copy-start | bytes 3076
  6.3 1.4 %copy-start.5 = (f32[256]{0:T(256)S(1)}, f32[256]{0:T(256)}, u32[]{:S(2)}) copy-start(f32[256]{0:T(256)} %param.18) | copy-start | bytes 3076
  6.3 14.6 %copy-start = (bf16[8,128,256]{2,1,0:T(8,128)(2,1)S(1)}, bf16[8,128,256]{2,1,0:T(8,128)(2,1)}, u32[]{:S(2)}) copy-start(bf16[8,128,256]{2,1,0:T(8,128)(2,1)} %key_ref.1) | copy-start | bytes 1572868
  6.3 14.6 %copy-start.2 = (bf16[8,2048]{1,0:T(8,128)(2,1)S(1)}, bf16[8,2048]{1,0:T(8,128)(2,1)}, u32[]{:S(2)}) copy-start(bf16[8,2048]{1,0:T(8,128)(2,1)} %queries_ref) | copy-start | bytes 98308
  6.3 14.6 %copy-start.6 = (s32[8]{0:T(128)S(1)}, s32[8]{0:T(128)}, u32[]{:S(2)}) copy-start(s32[8]{0:T(128)} %param.22) | copy-start | bytes 100
  6.3 14.6 %copy-start.7 = (s32[8]{0:T(128)S(1)}, s32[8]{0:T(128)}, u32[]{:S(2)}) copy-start(s32[8]{0:T(128)} %param.23) | copy-start | bytes 100
  6.4 19.0 %copy-start.1 = (bf16[8,128,256]{2,1,0:T(8,128)(2,1)S(1)}, bf16[8,128,256]{2,1,0:T(8,128)(2,1)}, u32[]{:S(2)}) copy-start(bf16[8,128,256]{2,1,0:T(8,128)(2,1)} %cache_ref.1) | copy-start | bytes 1572868
  7.9 6.4 %collective-permute-start.2 = (bf16[264,128]{1,0:T(8,128)(2,1)S(1)}, bf16[264,128]{1,0:T(8,128)(2,1)S(1)}, u32[]{:S(2)}, u32[]{:S(2)}) collective-permute-start(bf16[264,128]{1,0:T(8,128)(2,1)S(1)} %get-tuple-element.44), channel_id=1, source_target_pairs={{0,18},{2,16},{4,22},{6,20},{8,26},{10,24},{12,30},{14,28},{16,2},... | collective-permute-start | bytes 202760 | tf_op jit(solution)/shard_map/ppermute | solution.py:549
  11.6 4.4 %collective-permute-start.3 = (bf16[264,128]{1,0:T(8,128)(2,1)S(1)}, bf16[264,128]{1,0:T(8,128)(2,1)S(1)}, u32[]{:S(2)}, u32[]{:S(2)}) collective-permute-start(bf16[264,128]{1,0:T(8,128)(2,1)S(1)} %get-tuple-element.45), channel_id=1, source_target_pairs={{0,16},{2,18},{4,20},{6,22},{8,24},{10,26},{12,28},{14,30},{16,0},... | collective-permute-start | bytes 202760 | tf_op jit(solution)/shard_map/ppermute | solution.py:549
  12.1 4.3 %collective-permute-start.4 = (bf16[264,128]{1,0:T(8,128)(2,1)S(1)}, bf16[264,128]{1,0:T(8,128)(2,1)S(1)}, u32[]{:S(2)}, u32[]{:S(2)}) collective-permute-start(bf16[264,128]{1,0:T(8,128)(2,1)S(1)} %get-tuple-element.46), channel_id=1, source_target_pairs={{0,2},{2,0},{4,6},{6,4},{8,10},{10,8},{12,14},{14,12},{16,18},{18,... | collective-permute-start | bytes 202760 | tf_op jit(solution)/shard_map/ppermute | solution.py:549
  16.4 6.3 %collective-permute-start.5 = (bf16[264,128]{1,0:T(8,128)(2,1)S(1)}, bf16[264,128]{1,0:T(8,128)(2,1)S(1)}, u32[]{:S(2)}, u32[]{:S(2)}) collective-permute-start(bf16[264,128]{1,0:T(8,128)(2,1)S(1)} %get-tuple-element.48), channel_id=1, source_target_pairs={{0,12},{2,14},{4,8},{6,10},{8,4},{10,6},{12,0},{14,2},{16,28},{18,... | collective-permute-start | bytes 202760 | tf_op jit(solution)/shard_map/ppermute | solution.py:549
  20.1 4.3 %collective-permute-start.6 = (bf16[264,128]{1,0:T(8,128)(2,1)S(1)}, bf16[264,128]{1,0:T(8,128)(2,1)S(1)}, u32[]{:S(2)}, u32[]{:S(2)}) collective-permute-start(bf16[264,128]{1,0:T(8,128)(2,1)S(1)} %get-tuple-element.49), channel_id=1, source_target_pairs={{0,4},{2,6},{4,0},{6,2},{8,12},{10,14},{12,8},{14,10},{16,20},{18,... | collective-permute-start | bytes 202760 | tf_op jit(solution)/shard_map/ppermute | solution.py:549
  20.1 5.2 %collective-permute-start.7 = (bf16[264,128]{1,0:T(8,128)(2,1)S(1)}, bf16[264,128]{1,0:T(8,128)(2,1)S(1)}, u32[]{:S(2)}, u32[]{:S(2)}) collective-permute-start(bf16[264,128]{1,0:T(8,128)(2,1)S(1)} %get-tuple-element.50), channel_id=1, source_target_pairs={{0,8},{2,10},{4,12},{6,14},{8,0},{10,2},{12,4},{14,6},{16,24},{18,... | collective-permute-start | bytes 202760 | tf_op jit(solution)/shard_map/ppermute | solution.py:549

commit v9 on v8

--- a/solution.py
+++ b/solution.py
@@ -63,7 +63,10 @@
     chunks = 2 if columns % (2 * HEAD) == 0 else 1
     return pl.pallas_call(
         squares_kernel,
-        out_shape=(jax.ShapeDtypeStruct((rows, HEAD), jnp.float32), jax.ShapeDtypeStruct(frames.shape, frames.dtype)),
+        out_shape=(
+            jax.ShapeDtypeStruct((rows, HEAD), jnp.float32),
+            jax.ShapeDtypeStruct(frames.shape, frames.dtype),
+        ),
         in_specs=[HBM],
         out_specs=(VMEM, VMEM),
         scratch_shapes=[pltpu.SemaphoreType.DMA((chunks,))],
@@ -135,7 +138,7 @@
         return None
     near = sorted((g * members + m for g in range(groups) for m in range(2)), reverse=True)
     far = sorted(range(0, members, 2), reverse=True)
-    return (0, *near[:-1]), (0, far[0], *far[-2:0:-1])
+    return tuple((0, masks[0], *masks[-2:0:-1]) for masks in (near, far))
 
 
 def route(per_shard, capacity, stages, here, session, pick_ref, ids_ref):

time: 26.7 us -> 26.7 us (level)
  no operation moved by 1% of the time
where the time goes in v9:
time: 26.7 us; the launch traced here: 26.5 us
  starting transfers between devices  9.45 us (35%)
  waiting for transfers between devices  8.59 us (32%)
  Pallas kernels  8.34 us (31%)
    ppermute x6, starting transfers between devices, step(): lax.ppermute(a, ('grp', 'seq'), p)  8.78 us
    ppermute x6, waiting for transfers between devices, step(): lax.ppermute(a, ('grp', 'seq'), p)  8.08 us
    pallas_call x1, Pallas kernels, beside(): pl.pallas_call(functools.partial(beside_kernel, per_shard, capacity, stag...  3.51 us
    pallas_call x1, Pallas kernels, attend(): pl.pallas_call(functools.partial(attend_kernel, near, capacity), out_shap...  1.23 us
    pallas_call x1, Pallas kernels, partial_squares(): pl.pallas_call(squares_kernel, out_shape=(jax.ShapeDtypeStruct((rows, HEA...  1.21 us
    pallas_call x1, Pallas kernels, send_products(): pl.pallas_call(functools.partial(send_kernel, features), out_shape=(jax.S...  0.88 us
    pallas_call x1, Pallas kernels, keep_products(): pl.pallas_call(keep_kernel, out_shape=jax.ShapeDtypeStruct((rows, width),...  0.8 us
  transfers between devices with their start and end apart: 8, of which 7 were waited for; matrix products, arithmetic and copies ran while one was open for 0% of the time, Pallas kernels for 18%

profile of v9, /device:TPU:0, one launch (start us, length us, event | category | flops | bytes accessed | tf_op | source)
XLA Modules:
  0.0 26.5 jit_solution(2849372385850970804)
XLA Ops:
  0.0 1.2 %partial_squares.1 = (f32[96,128]{1,0:T(8,128)S(1)}, bf16[96,4096]{1,0:T(8,128)(2,1)S(1)}) custom-call(bf16[96,4096]{1,0:T(8,128)(2,1)} %frames_ref.1), custom_call_target="tpu_custom_call" | custom-call | flops 786432 | bytes 786432 | tf_op jit(solution)/shard_map/partial_squares/pallas_call | solution.py:64
  1.2 0.5 %collective-permute-start = (f32[96,128]{1,0:T(8,128)S(1)}, f32[96,128]{1,0:T(8,128)S(1)}, u32[]{:S(2)}, u32[]{:S(2)}) collective-permute-start(f32[96,128]{1,0:T(8,128)S(1)} %get-tuple-element.31.own_ref), channel_id=1, source_target_pairs={{0,1},{1,0},{2,3},{3,2},{4,5},{5,4},{6,7},{7,6},{8,9},{9,8},{10,11... | collective-permute-start | bytes 147464 | tf_op jit(solution)/shard_map/ppermute | solution.py:539
  1.7 0.0 copy-start.3
  1.7 3.5 %beside.1 = (bf16[4096,512]{1,0:T(8,128)(2,1)S(1)}, bf16[4096,512]{1,0:T(8,128)(2,1)S(1)}, bf16[256,96]{1,0:T(8,128)(2,1)S(1)}, f32[32,128]{1,0:T(8,128)S(1)}) custom-call(s32[1]{0:T(128)} %bitcast.2.here_ref, s32[1,96]{1,0:T(1,128)} %bitcast.13, bf16[4096,512]{1,0:T(8,128)(2,1)} %w_key_ref.1, bf16[4096,512]{1,0:T(8,128)(2,1)} %w_value_ref.1), custom_call_target="tpu_custom_call" | custom-call | flops 9437184 | bytes 8388608 | tf_op jit(solution)/shard_map/beside/pallas_call | solution.py:243
  5.3 0.0 collective-permute-done.other_ref
  5.3 0.0 copy-done.3
  5.3 0.9 %send_products.1 = (bf16[96,4096]{1,0:T(8,128)(2,1)S(1)}, f32[96,512]{1,0:T(8,128)S(1)}) custom-call(s32[1]{0:T(128)} %bitcast.4.index_ref, bf16[96,4096]{1,0:T(8,128)(2,1)S(1)} %get-tuple-element.30.frames_ref, f32[96,128]{1,0:T(8,128)S(1)} %get-tuple-element.31.own_ref, f32[96,128]{1,0:T(8,128)S(1)} %collective-permute-done.other_ref, ...), custom_call_target="tpu_custom_call" | custom-call | flops 402653184 | bytes 4194304 | tf_op jit(solution)/shard_map/send_products/pallas_call | solution.py:100
  6.2 0.2 collective-permute-start.1
  6.3 0.0 copy-start.4
  6.3 0.0 copy-start.5
  6.3 0.0 copy-start
  6.3 0.0 copy-start.2
  6.3 0.0 copy-start.6
  6.3 0.0 copy-start.7
  6.4 0.0 copy-start.1
  6.4 0.8 %keep_products.1.kept_ref = f32[96,512]{1,0:T(8,128)S(1)} custom-call(s32[1]{0:T(128)} %bitcast.4.index_ref, bf16[96,4096]{1,0:T(8,128)(2,1)S(1)} %get-tuple-element.34.normed_ref, bf16[4096,512]{1,0:T(8,128)(2,1)S(1)} %get-tuple-element.32.key_ref, bf16[4096,512]{1,0:T(8,128)(2,1)S(1)} %get-tuple-element.33.value_ref), custom_call_target="tpu_custom_call" | custom-call | flops 402653184 | bytes 4194304 | tf_op jit(solution)/shard_map/keep_products/pallas_call | solution.py:121
  7.2 0.5 %collective-permute-done.1.got_ref = f32[96,512]{1,0:T(8,128)S(1)} collective-permute-done((f32[96,512]{1,0:T(8,128)S(1)}, f32[96,512]{1,0:T(8,128)S(1)}, u32[]{:S(2)}, u32[]{:S(2)}) %collective-permute-start.1) | collective-permute-done | bytes 196640 | tf_op jit(solution)/shard_map/ppermute | solution.py:546
  7.7 0.0 copy-done.4
  7.7 0.0 copy-done.5
  7.7 0.2 pack.1
  7.9 3.7 %collective-permute-start.2 = (bf16[264,128]{1,0:T(8,128)(2,1)S(1)}, bf16[264,128]{1,0:T(8,128)(2,1)S(1)}, u32[]{:S(2)}, u32[]{:S(2)}) collective-permute-start(bf16[264,128]{1,0:T(8,128)(2,1)S(1)} %get-tuple-element.44), channel_id=1, source_target_pairs={{0,18},{2,16},{4,22},{6,20},{8,26},{10,24},{12,30},{14,28},{16,2},... | collective-permute-start | bytes 202760 | tf_op jit(solution)/shard_map/ppermute | solution.py:552
  11.6 0.5 %collective-permute-start.3 = (bf16[264,128]{1,0:T(8,128)(2,1)S(1)}, bf16[264,128]{1,0:T(8,128)(2,1)S(1)}, u32[]{:S(2)}, u32[]{:S(2)}) collective-permute-start(bf16[264,128]{1,0:T(8,128)(2,1)S(1)} %get-tuple-element.45), channel_id=1, source_target_pairs={{0,2},{2,0},{4,6},{6,4},{8,10},{10,8},{12,14},{14,12},{16,18},{18,... | collective-permute-start | bytes 202760 | tf_op jit(solution)/shard_map/ppermute | solution.py:552
  12.1 0.1 collective-permute-start.4
  12.2 2.0 %collective-permute-done.2.refs_1_ = bf16[264,128]{1,0:T(8,128)(2,1)S(1)} collective-permute-done((bf16[264,128]{1,0:T(8,128)(2,1)S(1)}, bf16[264,128]{1,0:T(8,128)(2,1)S(1)}, u32[]{:S(2)}, u32[]{:S(2)}) %collective-permute-start.2) | collective-permute-done | bytes 67616 | tf_op jit(solution)/shard_map/ppermute | solution.py:552
  14.2 1.6 %collective-permute-done.3.refs_2_ = bf16[264,128]{1,0:T(8,128)(2,1)S(1)} collective-permute-done((bf16[264,128]{1,0:T(8,128)(2,1)S(1)}, bf16[264,128]{1,0:T(8,128)(2,1)S(1)}, u32[]{:S(2)}, u32[]{:S(2)}) %collective-permute-start.3) | collective-permute-done | bytes 67616 | tf_op jit(solution)/shard_map/ppermute | solution.py:552
  15.9 0.5 %collective-permute-done.4.refs_3_ = bf16[264,128]{1,0:T(8,128)(2,1)S(1)} collective-permute-done((bf16[264,128]{1,0:T(8,128)(2,1)S(1)}, bf16[264,128]{1,0:T(8,128)(2,1)S(1)}, u32[]{:S(2)}, u32[]{:S(2)}) %collective-permute-start.4) | collective-permute-done | bytes 67616 | tf_op jit(solution)/shard_map/ppermute | solution.py:552
  16.4 3.7 %collective-permute-start.5 = (bf16[264,128]{1,0:T(8,128)(2,1)S(1)}, bf16[264,128]{1,0:T(8,128)(2,1)S(1)}, u32[]{:S(2)}, u32[]{:S(2)}) collective-permute-start(bf16[264,128]{1,0:T(8,128)(2,1)S(1)} %get-tuple-element.48), channel_id=1, source_target_pairs={{0,12},{2,14},{4,8},{6,10},{8,4},{10,6},{12,0},{14,2},{16,28},{18,... | collective-permute-start | bytes 202760 | tf_op jit(solution)/shard_map/ppermute | solution.py:552
  20.1 0.0 collective-permute-start.6
  20.1 0.8 %collective-permute-start.7 = (bf16[264,128]{1,0:T(8,128)(2,1)S(1)}, bf16[264,128]{1,0:T(8,128)(2,1)S(1)}, u32[]{:S(2)}, u32[]{:S(2)}) collective-permute-start(bf16[264,128]{1,0:T(8,128)(2,1)S(1)} %get-tuple-element.50), channel_id=1, source_target_pairs={{0,8},{2,10},{4,12},{6,14},{8,0},{10,2},{12,4},{14,6},{16,24},{18,... | collective-permute-start | bytes 202760 | tf_op jit(solution)/shard_map/ppermute | solution.py:552
  20.9 0.0 copy-done
  20.9 0.0 copy-done.2
  20.9 0.0 copy-done.6
  20.9 0.0 copy-done.7
  20.9 0.5 %cached_scores.1 = (f32[128,128]{1,0:T(8,128)S(1)}, bf16[128,256]{1,0:T(8,128)(2,1)S(1)}) custom-call(s32[1,8]{1,0:T(1,128)S(1)} %bitcast.11, s32[1,8]{1,0:T(1,128)S(1)} %bitcast.12, bf16[8,2048]{1,0:T(8,128)(2,1)S(1)} %copy-done.2, bf16[8,128,256]{2,1,0:T(8,128)(2,1)S(1)} %copy-done), custom_call_target="tpu_custom_call" | custom-call | flops 33554432 | bytes 524288 | tf_op jit(solution)/shard_map/cached_scores/pallas_call | solution.py:263
  21.3 1.4 %collective-permute-done.5.refs_1_ = bf16[264,128]{1,0:T(8,128)(2,1)S(1)} collective-permute-done((bf16[264,128]{1,0:T(8,128)(2,1)S(1)}, bf16[264,128]{1,0:T(8,128)(2,1)S(1)}, u32[]{:S(2)}, u32[]{:S(2)}) %collective-permute-start.5) | collective-permute-done | bytes 67616 | tf_op jit(solution)/shard_map/ppermute | solution.py:552
  22.7 1.7 %collective-permute-done.6.refs_2_ = bf16[264,128]{1,0:T(8,128)(2,1)S(1)} collective-permute-done((bf16[264,128]{1,0:T(8,128)(2,1)S(1)}, bf16[264,128]{1,0:T(8,128)(2,1)S(1)}, u32[]{:S(2)}, u32[]{:S(2)}) %collective-permute-start.6) | collective-permute-done | bytes 67616 | tf_op jit(solution)/shard_map/ppermute | solution.py:552
  24.4 0.9 %collective-permute-done.7.refs_3_ = bf16[264,128]{1,0:T(8,128)(2,1)S(1)} collective-permute-done((bf16[264,128]{1,0:T(8,128)(2,1)S(1)}, bf16[264,128]{1,0:T(8,128)(2,1)S(1)}, u32[]{:S(2)}, u32[]{:S(2)}) %collective-permute-start.7) | collective-permute-done | bytes 67616 | tf_op jit(solution)/shard_map/ppermute | solution.py:552
  25.3 0.0 copy-done.1
  25.3 1.2 %attend.1 = bf16[8,2048]{1,0:T(8,128)(2,1)} custom-call(bf16[128,256]{1,0:T(8,128)(2,1)S(1)} %get-tuple-element.41.queries_ref, f32[128,128]{1,0:T(8,128)S(1)} %get-tuple-element.42.score_ref, bf16[8,128,256]{2,1,0:T(8,128)(2,1)S(1)} %copy-done.1, bf16[264,128]{1,0:T(8,128)(2,1)S(1)} %get-tuple-element.47.refs_0_, ...), custom_call_target="tpu_custom_call" | custom-call | flops 134217728 | bytes 524288 | tf_op jit(solution)/shard_map/attend/pallas_call | solution.py:391
  (1 shorter events, 0.0 us)
Async XLA Ops:
  1.2 4.0 %collective-permute-start = (f32[96,128]{1,0:T(8,128)S(1)}, f32[96,128]{1,0:T(8,128)S(1)}, u32[]{:S(2)}, u32[]{:S(2)}) collective-permute-start(f32[96,128]{1,0:T(8,128)S(1)} %get-tuple-element.31.own_ref), channel_id=1, source_target_pairs={{0,1},{1,0},{2,3},{3,2},{4,5},{5,4},{6,7},{7,6},{8,9},{9,8},{10,11... | collective-permute-start | bytes 147464 | tf_op jit(solution)/shard_map/ppermute | solution.py:539
  1.7 3.5 %copy-start.3 = (f32[4096]{0:T(1024)S(1)}, f32[4096]{0:T(1024)}, u32[]{:S(2)}) copy-start(f32[4096]{0:T(1024)} %param.14) | copy-start | bytes 49156
  6.2 1.5 %collective-permute-start.1 = (f32[96,512]{1,0:T(8,128)S(1)}, f32[96,512]{1,0:T(8,128)S(1)}, u32[]{:S(2)}, u32[]{:S(2)}) collective-permute-start(f32[96,512]{1,0:T(8,128)S(1)} %get-tuple-element.35), channel_id=1, source_target_pairs={{0,1},{1,0},{2,3},{3,2},{4,5},{5,4},{6,7},{7,6},{8,9},{9,8},{10,11... | collective-permute-start | bytes 589832 | tf_op jit(solution)/shard_map/ppermute | solution.py:546
  6.3 1.4 %copy-start.4 = (f32[256]{0:T(256)S(1)}, f32[256]{0:T(256)}, u32[]{:S(2)}) copy-start(f32[256]{0:T(256)} %param.17) | copy-start | bytes 3076
  6.3 1.4 %copy-start.5 = (f32[256]{0:T(256)S(1)}, f32[256]{0:T(256)}, u32[]{:S(2)}) copy-start(f32[256]{0:T(256)} %param.18) | copy-start | bytes 3076
  6.3 14.6 %copy-start = (bf16[8,128,256]{2,1,0:T(8,128)(2,1)S(1)}, bf16[8,128,256]{2,1,0:T(8,128)(2,1)}, u32[]{:S(2)}) copy-start(bf16[8,128,256]{2,1,0:T(8,128)(2,1)} %key_ref.1) | copy-start | bytes 1572868
  6.3 14.6 %copy-start.2 = (bf16[8,2048]{1,0:T(8,128)(2,1)S(1)}, bf16[8,2048]{1,0:T(8,128)(2,1)}, u32[]{:S(2)}) copy-start(bf16[8,2048]{1,0:T(8,128)(2,1)} %queries_ref) | copy-start | bytes 98308
  6.3 14.6 %copy-start.6 = (s32[8]{0:T(128)S(1)}, s32[8]{0:T(128)}, u32[]{:S(2)}) copy-start(s32[8]{0:T(128)} %param.22) | copy-start | bytes 100
  6.3 14.5 %copy-start.7 = (s32[8]{0:T(128)S(1)}, s32[8]{0:T(128)}, u32[]{:S(2)}) copy-start(s32[8]{0:T(128)} %param.23) | copy-start | bytes 100
  6.4 18.9 %copy-start.1 = (bf16[8,128,256]{2,1,0:T(8,128)(2,1)S(1)}, bf16[8,128,256]{2,1,0:T(8,128)(2,1)}, u32[]{:S(2)}) copy-start(bf16[8,128,256]{2,1,0:T(8,128)(2,1)} %cache_ref.1) | copy-start | bytes 1572868
  7.9 6.3 %collective-permute-start.2 = (bf16[264,128]{1,0:T(8,128)(2,1)S(1)}, bf16[264,128]{1,0:T(8,128)(2,1)S(1)}, u32[]{:S(2)}, u32[]{:S(2)}) collective-permute-start(bf16[264,128]{1,0:T(8,128)(2,1)S(1)} %get-tuple-element.44), channel_id=1, source_target_pairs={{0,18},{2,16},{4,22},{6,20},{8,26},{10,24},{12,30},{14,28},{16,2},... | collective-permute-start | bytes 202760 | tf_op jit(solution)/shard_map/ppermute | solution.py:552
  11.6 4.3 %collective-permute-start.3 = (bf16[264,128]{1,0:T(8,128)(2,1)S(1)}, bf16[264,128]{1,0:T(8,128)(2,1)S(1)}, u32[]{:S(2)}, u32[]{:S(2)}) collective-permute-start(bf16[264,128]{1,0:T(8,128)(2,1)S(1)} %get-tuple-element.45), channel_id=1, source_target_pairs={{0,2},{2,0},{4,6},{6,4},{8,10},{10,8},{12,14},{14,12},{16,18},{18,... | collective-permute-start | bytes 202760 | tf_op jit(solution)/shard_map/ppermute | solution.py:552
  12.1 4.3 %collective-permute-start.4 = (bf16[264,128]{1,0:T(8,128)(2,1)S(1)}, bf16[264,128]{1,0:T(8,128)(2,1)S(1)}, u32[]{:S(2)}, u32[]{:S(2)}) collective-permute-start(bf16[264,128]{1,0:T(8,128)(2,1)S(1)} %get-tuple-element.46), channel_id=1, source_target_pairs={{0,16},{2,18},{4,20},{6,22},{8,24},{10,26},{12,28},{14,30},{16,0},... | collective-permute-start | bytes 202760 | tf_op jit(solution)/shard_map/ppermute | solution.py:552
  16.4 6.3 %collective-permute-start.5 = (bf16[264,128]{1,0:T(8,128)(2,1)S(1)}, bf16[264,128]{1,0:T(8,128)(2,1)S(1)}, u32[]{:S(2)}, u32[]{:S(2)}) collective-permute-start(bf16[264,128]{1,0:T(8,128)(2,1)S(1)} %get-tuple-element.48), channel_id=1, source_target_pairs={{0,12},{2,14},{4,8},{6,10},{8,4},{10,6},{12,0},{14,2},{16,28},{18,... | collective-permute-start | bytes 202760 | tf_op jit(solution)/shard_map/ppermute | solution.py:552
  20.1 4.3 %collective-permute-start.6 = (bf16[264,128]{1,0:T(8,128)(2,1)S(1)}, bf16[264,128]{1,0:T(8,128)(2,1)S(1)}, u32[]{:S(2)}, u32[]{:S(2)}) collective-permute-start(bf16[264,128]{1,0:T(8,128)(2,1)S(1)} %get-tuple-element.49), channel_id=1, source_target_pairs={{0,4},{2,6},{4,0},{6,2},{8,12},{10,14},{12,8},{14,10},{16,20},{18,... | collective-permute-start | bytes 202760 | tf_op jit(solution)/shard_map/ppermute | solution.py:552
  20.1 5.2 %collective-permute-start.7 = (bf16[264,128]{1,0:T(8,128)(2,1)S(1)}, bf16[264,128]{1,0:T(8,128)(2,1)S(1)}, u32[]{:S(2)}, u32[]{:S(2)}) collective-permute-start(bf16[264,128]{1,0:T(8,128)(2,1)S(1)} %get-tuple-element.50), channel_id=1, source_target_pairs={{0,8},{2,10},{4,12},{6,14},{8,0},{10,2},{12,4},{14,6},{16,24},{18,... | collective-permute-start | bytes 202760 | tf_op jit(solution)/shard_map/ppermute | solution.py:552

commit v10 on v9

--- a/solution.py
+++ b/solution.py
@@ -129,31 +129,41 @@
     )(index, normed, key, value)
 
 
-def max_bits(masks):
-    return functools.reduce(lambda a, b: a | b, masks)
-
-
-def stage_masks(groups, members):
+def first_masks(groups, members):
     if groups & (groups - 1) or members & (members - 1) or members < 4:
         return None
-    near = sorted((g * members + m for g in range(groups) for m in range(2)), reverse=True)
-    far = sorted(range(0, members, 2), reverse=True)
-    return tuple((0, masks[0], *masks[-2:0:-1]) for masks in (near, far))
-
-
-def route(per_shard, capacity, stages, here, session, pick_ref, ids_ref):
+    masks = [group * members + low for group in range(groups) for low in range(2)]
+    return (0, masks[-1], *masks[1:-1])
+
+
+def ring_place(device, members):
+    upper = (device & (members - 1)) >> 1
+    place = upper
+    for shift in range(1, (members // 2).bit_length() - 1):
+        place = place ^ (upper >> shift)
+    return place
+
+
+def second_pairs(partitions, members):
+    line = members // 2
+    devices = range(partitions)
+    at = {(d // members, d & 1, ring_place(d, members)): d for d in devices}
+    return [
+        [(d, at[d // members, d & 1, (ring_place(d, members) + up) % line]) for d in devices]
+        for up in range(line)
+    ]
+
+
+def route(per_shard, capacity, near, members, here, session, pick_ref, ids_ref):
     slots, rows = pick_ref.shape
     partitions = slots // capacity
-    near, far = stages
+    line = members // 2
     target = lax.div(session, per_shard)
     local = session - target * per_shard
-    apart = target ^ here
-    step = [
-        sum(jnp.where((apart & max_bits(masks)) == mask, at, 0) for at, mask in enumerate(masks))
-        for masks in stages
-    ]
-    leaves = step[0] * len(far) + step[1]
-    lands = step[1] * len(near) + step[0]
+    apart = (target ^ here) & functools.reduce(lambda a, b: a | b, near)
+    first = sum(jnp.where(apart == mask, at, 0) for at, mask in enumerate(near))
+    second = (ring_place(target, members) - ring_place(here, members)) & (line - 1)
+    leaves, lands = first * line + second, second * len(near) + first
     to = lax.broadcasted_iota(jnp.int32, (partitions, rows), 0) == leaves
     to = to.astype(jnp.float32)
     earlier = lax.broadcasted_iota(jnp.int32, (rows, rows), 0) < lax.broadcasted_iota(
@@ -209,7 +219,8 @@
 def beside_kernel(
     per_shard,
     capacity,
-    stages,
+    near,
+    members,
     here_ref,
     session_ref,
     w_key_ref,
@@ -232,16 +243,16 @@
         copies.append(pltpu.make_async_copy(source, held, arrived.at[at]))
         copies[-1].start()
     copies[0].wait()
-    route(per_shard, capacity, stages, here_ref[0], session[...], pick_ref, ids_ref)
+    route(per_shard, capacity, near, members, here_ref[0], session[...], pick_ref, ids_ref)
     for copy in copies[1:]:
         copy.wait()
 
 
 def beside(here, session, w_key, w_value, sizes):
-    partitions, per_shard, capacity, stages = sizes
-    slots, rows = partitions * capacity, session.shape[1]
-    return pl.pallas_call(
-        functools.partial(beside_kernel, per_shard, capacity, stages),
+    partitions, *sizes = sizes
+    slots, rows = partitions * sizes[1], session.shape[1]
+    return pl.pallas_call(
+        functools.partial(beside_kernel, *sizes),
         out_shape=(
             jax.ShapeDtypeStruct(w_key.shape, w_key.dtype),
             jax.ShapeDtypeStruct(w_value.shape, w_value.dtype),
@@ -526,8 +537,9 @@
     per_shard = queries.shape[0]
     rows = frames.shape[0]
     capacity = max(2, 5 * rows // (2 * partitions) + 1)
-    stages = stage_masks(lax.axis_size("grp"), lax.axis_size("seq"))
-    if stages is None or shares != 2 or per_shard % 8 or capacity % 16 or partitions * capacity % HEAD:
+    members = lax.axis_size("seq")
+    near = first_masks(lax.axis_size("grp"), members)
+    if near is None or shares != 2 or per_shard % 8 or capacity % 16 or partitions * capacity % HEAD:
         return general(
             frames, token_session, ln_gain, w_key, w_value, k_bias, v_bias, queries, cache_key, cache_value,
             cache_start, cache_len,
@@ -538,26 +550,26 @@
     own, held = partial_squares(frames)
     other = lax.ppermute(own, "mp", swap)
     held_key, held_value, pick, ids = beside(
-        here, token_session[None, :], w_key, w_value, (partitions, per_shard, capacity, stages)
+        here, token_session[None, :], w_key, w_value, (partitions, per_shard, capacity, near, members)
     )
     normed, sent = send_products(
         index, held, own, other, ln_gain[None, :], held_key, held_value, frames.shape[1] * shares
     )
     arrived = lax.ppermute(sent, "mp", swap)
     kept = keep_products(index, normed, held_key, held_value)
-    blocks = pack(pick, ids, kept, arrived, k_bias[None, :], v_bias[None, :], len(stages[0]))
-
-    def step(arrays, masks):
-        pairs = [[(i, i ^ mask) for i in range(partitions)] for mask in masks]
+    blocks = pack(pick, ids, kept, arrived, k_bias[None, :], v_bias[None, :], len(near))
+
+    def step(arrays, pairs):
         sent = [lax.ppermute(a, ("grp", "seq"), p) for a, p in zip(arrays[1:], pairs[1:])]
         return [arrays[0], *sent]
 
-    near, far = stages
-    vectors = 2 * cache_key.shape[2] // HEAD
     queries, *blocks = lax.optimization_barrier((queries, *blocks))
     scores, laid = cached_scores(cache_start[None, :], cache_len[None, :], queries, cache_key)
-    mid = regroup(step(blocks, near), len(far), vectors, capacity)
-    return attend(step(mid, far), laid, scores, cache_value, len(near), capacity)
+    vectors = 2 * cache_key.shape[2] // HEAD
+    blocks = step(blocks, [[(i, i ^ mask) for i in range(partitions)] for mask in near])
+    blocks = regroup(blocks, members // 2, vectors, capacity)
+    blocks = step(blocks, second_pairs(partitions, members))
+    return attend(blocks, laid, scores, cache_value, len(near), capacity)
 
 
 def solution(mesh):

time: 26.7 us -> 26.4 us (0.989)
  waiting for transfers between devices: 8.59 us -> 7.06 us
  starting transfers between devices: 9.45 us -> 10.7 us
    ppermute x6, waiting for transfers between devices: 8.08 us -> 6.55 us  [step(): lax.ppermute(a, ('grp', 'seq'), p)]
    ppermute x6, starting transfers between devices: 8.78 us -> 10 us  [step(): lax.ppermute(a, ('grp', 'seq'), p)]
  transfers between devices with their start and end apart: 8 -> 8, of which waited for: 7 -> 6; matrix products, arithmetic and copies ran while one was open for 0% -> 0% of each run, Pallas kernels for 18% -> 18%
where the time goes in v10:
time: 26.4 us; the launch traced here: 26.2 us
  starting transfers between devices  10.7 us (41%)
  Pallas kernels  8.34 us (32%)
  waiting for transfers between devices  7.06 us (27%)
    ppermute x6, starting transfers between devices, step(): lax.ppermute(a, ('grp', 'seq'), p)  10 us
    ppermute x6, waiting for transfers between devices, step(): lax.ppermute(a, ('grp', 'seq'), p)  6.55 us
    pallas_call x1, Pallas kernels, beside(): pl.pallas_call(functools.partial(beside_kernel, *sizes), out_shape=(jax.S...  3.51 us
    pallas_call x1, Pallas kernels, attend(): pl.pallas_call(functools.partial(attend_kernel, near, capacity), out_shap...  1.23 us
    pallas_call x1, Pallas kernels, partial_squares(): pl.pallas_call(squares_kernel, out_shape=(jax.ShapeDtypeStruct((rows, HEA...  1.21 us
    pallas_call x1, Pallas kernels, send_products(): pl.pallas_call(functools.partial(send_kernel, features), out_shape=(jax.S...  0.88 us
    pallas_call x1, Pallas kernels, keep_products(): pl.pallas_call(keep_kernel, out_shape=jax.ShapeDtypeStruct((rows, width),...  0.8 us
  transfers between devices with their start and end apart: 8, of which 6 were waited for; matrix products, arithmetic and copies ran while one was open for 0% of the time, Pallas kernels for 18%

profile of v10, /device:TPU:0, one launch (start us, length us, event | category | flops | bytes accessed | tf_op | source)
XLA Modules:
  0.0 26.2 jit_solution(9952671781169152504)
XLA Ops:
  0.0 1.2 %partial_squares.1 = (f32[96,128]{1,0:T(8,128)S(1)}, bf16[96,4096]{1,0:T(8,128)(2,1)S(1)}) custom-call(bf16[96,4096]{1,0:T(8,128)(2,1)} %frames_ref.1), custom_call_target="tpu_custom_call" | custom-call | flops 786432 | bytes 786432 | tf_op jit(solution)/shard_map/partial_squares/pallas_call | solution.py:64
  1.2 0.5 %collective-permute-start = (f32[96,128]{1,0:T(8,128)S(1)}, f32[96,128]{1,0:T(8,128)S(1)}, u32[]{:S(2)}, u32[]{:S(2)}) collective-permute-start(f32[96,128]{1,0:T(8,128)S(1)} %get-tuple-element.31.own_ref), channel_id=1, source_target_pairs={{0,1},{1,0},{2,3},{3,2},{4,5},{5,4},{6,7},{7,6},{8,9},{9,8},{10,11... | collective-permute-start | bytes 147464 | tf_op jit(solution)/shard_map/ppermute | solution.py:551
  1.7 0.0 copy-start.3
  1.7 3.5 %beside.1 = (bf16[4096,512]{1,0:T(8,128)(2,1)S(1)}, bf16[4096,512]{1,0:T(8,128)(2,1)S(1)}, bf16[256,96]{1,0:T(8,128)(2,1)S(1)}, f32[32,128]{1,0:T(8,128)S(1)}) custom-call(s32[1]{0:T(128)} %bitcast.2.here_ref, s32[1,96]{1,0:T(1,128)} %bitcast.13, bf16[4096,512]{1,0:T(8,128)(2,1)} %w_key_ref.1, bf16[4096,512]{1,0:T(8,128)(2,1)} %w_value_ref.1), custom_call_target="tpu_custom_call" | custom-call | flops 9437184 | bytes 8388608 | tf_op jit(solution)/shard_map/beside/pallas_call | solution.py:254
  5.3 0.0 collective-permute-done.other_ref
  5.3 0.0 copy-done.3
  5.3 0.9 %send_products.1 = (bf16[96,4096]{1,0:T(8,128)(2,1)S(1)}, f32[96,512]{1,0:T(8,128)S(1)}) custom-call(s32[1]{0:T(128)} %bitcast.4.index_ref, bf16[96,4096]{1,0:T(8,128)(2,1)S(1)} %get-tuple-element.30.frames_ref, f32[96,128]{1,0:T(8,128)S(1)} %get-tuple-element.31.own_ref, f32[96,128]{1,0:T(8,128)S(1)} %collective-permute-done.other_ref, ...), custom_call_target="tpu_custom_call" | custom-call | flops 402653184 | bytes 4194304 | tf_op jit(solution)/shard_map/send_products/pallas_call | solution.py:100
  6.2 0.2 collective-permute-start.1
  6.3 0.0 copy-start.4
  6.3 0.0 copy-start.5
  6.3 0.0 copy-start
  6.3 0.0 copy-start.2
  6.3 0.0 copy-start.6
  6.3 0.0 copy-start.7
  6.4 0.0 copy-start.1
  6.4 0.8 %keep_products.1.kept_ref = f32[96,512]{1,0:T(8,128)S(1)} custom-call(s32[1]{0:T(128)} %bitcast.4.index_ref, bf16[96,4096]{1,0:T(8,128)(2,1)S(1)} %get-tuple-element.34.normed_ref, bf16[4096,512]{1,0:T(8,128)(2,1)S(1)} %get-tuple-element.32.key_ref, bf16[4096,512]{1,0:T(8,128)(2,1)S(1)} %get-tuple-element.33.value_ref), custom_call_target="tpu_custom_call" | custom-call | flops 402653184 | bytes 4194304 | tf_op jit(solution)/shard_map/keep_products/pallas_call | solution.py:121
  7.2 0.5 %collective-permute-done.1.got_ref = f32[96,512]{1,0:T(8,128)S(1)} collective-permute-done((f32[96,512]{1,0:T(8,128)S(1)}, f32[96,512]{1,0:T(8,128)S(1)}, u32[]{:S(2)}, u32[]{:S(2)}) %collective-permute-start.1) | collective-permute-done | bytes 196640 | tf_op jit(solution)/shard_map/ppermute | solution.py:558
  7.7 0.0 copy-done.4
  7.7 0.0 copy-done.5
  7.7 0.2 pack.1
  7.9 3.7 %collective-permute-start.2 = (bf16[264,128]{1,0:T(8,128)(2,1)S(1)}, bf16[264,128]{1,0:T(8,128)(2,1)S(1)}, u32[]{:S(2)}, u32[]{:S(2)}) collective-permute-start(bf16[264,128]{1,0:T(8,128)(2,1)S(1)} %get-tuple-element.44), channel_id=1, source_target_pairs={{0,18},{2,16},{4,22},{6,20},{8,26},{10,24},{12,30},{14,28},{16,2},... | collective-permute-start | bytes 202760 | tf_op jit(solution)/shard_map/ppermute | solution.py:563
  11.6 0.5 %collective-permute-start.3 = (bf16[264,128]{1,0:T(8,128)(2,1)S(1)}, bf16[264,128]{1,0:T(8,128)(2,1)S(1)}, u32[]{:S(2)}, u32[]{:S(2)}) collective-permute-start(bf16[264,128]{1,0:T(8,128)(2,1)S(1)} %get-tuple-element.45), channel_id=1, source_target_pairs={{0,2},{2,0},{4,6},{6,4},{8,10},{10,8},{12,14},{14,12},{16,18},{18,... | collective-permute-start | bytes 202760 | tf_op jit(solution)/shard_map/ppermute | solution.py:563
  12.1 0.1 collective-permute-start.4
  12.2 2.0 %collective-permute-done.2.refs_1_ = bf16[264,128]{1,0:T(8,128)(2,1)S(1)} collective-permute-done((bf16[264,128]{1,0:T(8,128)(2,1)S(1)}, bf16[264,128]{1,0:T(8,128)(2,1)S(1)}, u32[]{:S(2)}, u32[]{:S(2)}) %collective-permute-start.2) | collective-permute-done | bytes 67616 | tf_op jit(solution)/shard_map/ppermute | solution.py:563
  14.2 1.6 %collective-permute-done.3.refs_2_ = bf16[264,128]{1,0:T(8,128)(2,1)S(1)} collective-permute-done((bf16[264,128]{1,0:T(8,128)(2,1)S(1)}, bf16[264,128]{1,0:T(8,128)(2,1)S(1)}, u32[]{:S(2)}, u32[]{:S(2)}) %collective-permute-start.3) | collective-permute-done | bytes 67616 | tf_op jit(solution)/shard_map/ppermute | solution.py:563
  15.9 0.5 %collective-permute-done.4.refs_3_ = bf16[264,128]{1,0:T(8,128)(2,1)S(1)} collective-permute-done((bf16[264,128]{1,0:T(8,128)(2,1)S(1)}, bf16[264,128]{1,0:T(8,128)(2,1)S(1)}, u32[]{:S(2)}, u32[]{:S(2)}) %collective-permute-start.4) | collective-permute-done | bytes 67616 | tf_op jit(solution)/shard_map/ppermute | solution.py:563
  16.4 1.6 %collective-permute-start.5 = (bf16[264,128]{1,0:T(8,128)(2,1)S(1)}, bf16[264,128]{1,0:T(8,128)(2,1)S(1)}, u32[]{:S(2)}, u32[]{:S(2)}) collective-permute-start(bf16[264,128]{1,0:T(8,128)(2,1)S(1)} %get-tuple-element.48), channel_id=1, source_target_pairs={{0,4},{2,6},{4,12},{6,14},{8,0},{10,2},{12,8},{14,10},{16,20},{18,... | collective-permute-start | bytes 202760 | tf_op jit(solution)/shard_map/ppermute | solution.py:563
  18.0 2.5 %collective-permute-start.6 = (bf16[264,128]{1,0:T(8,128)(2,1)S(1)}, bf16[264,128]{1,0:T(8,128)(2,1)S(1)}, u32[]{:S(2)}, u32[]{:S(2)}) collective-permute-start(bf16[264,128]{1,0:T(8,128)(2,1)S(1)} %get-tuple-element.49), channel_id=1, source_target_pairs={{0,12},{2,14},{4,8},{6,10},{8,4},{10,6},{12,0},{14,2},{16,28},{18,... | collective-permute-start | bytes 202760 | tf_op jit(solution)/shard_map/ppermute | solution.py:563
  20.5 1.6 %collective-permute-start.7 = (bf16[264,128]{1,0:T(8,128)(2,1)S(1)}, bf16[264,128]{1,0:T(8,128)(2,1)S(1)}, u32[]{:S(2)}, u32[]{:S(2)}) collective-permute-start(bf16[264,128]{1,0:T(8,128)(2,1)S(1)} %get-tuple-element.50), channel_id=1, source_target_pairs={{0,8},{2,10},{4,0},{6,2},{8,12},{10,14},{12,4},{14,6},{16,24},{18,... | collective-permute-start | bytes 202760 | tf_op jit(solution)/shard_map/ppermute | solution.py:563
  22.1 0.0 copy-done
  22.1 0.0 copy-done.2
  22.1 0.0 copy-done.6
  22.1 0.0 copy-done.7
  22.1 0.5 %cached_scores.1 = (f32[128,128]{1,0:T(8,128)S(1)}, bf16[128,256]{1,0:T(8,128)(2,1)S(1)}) custom-call(s32[1,8]{1,0:T(1,128)S(1)} %bitcast.11, s32[1,8]{1,0:T(1,128)S(1)} %bitcast.12, bf16[8,2048]{1,0:T(8,128)(2,1)S(1)} %copy-done.2, bf16[8,128,256]{2,1,0:T(8,128)(2,1)S(1)} %copy-done), custom_call_target="tpu_custom_call" | custom-call | flops 33554432 | bytes 524288 | tf_op jit(solution)/shard_map/cached_scores/pallas_call | solution.py:274
  22.6 1.7 %collective-permute-done.5.refs_1_ = bf16[264,128]{1,0:T(8,128)(2,1)S(1)} collective-permute-done((bf16[264,128]{1,0:T(8,128)(2,1)S(1)}, bf16[264,128]{1,0:T(8,128)(2,1)S(1)}, u32[]{:S(2)}, u32[]{:S(2)}) %collective-permute-start.5) | collective-permute-done | bytes 67616 | tf_op jit(solution)/shard_map/ppermute | solution.py:563
  24.3 0.0 collective-permute-done.6.refs_2_
  24.3 0.7 %collective-permute-done.7.refs_3_ = bf16[264,128]{1,0:T(8,128)(2,1)S(1)} collective-permute-done((bf16[264,128]{1,0:T(8,128)(2,1)S(1)}, bf16[264,128]{1,0:T(8,128)(2,1)S(1)}, u32[]{:S(2)}, u32[]{:S(2)}) %collective-permute-start.7) | collective-permute-done | bytes 67616 | tf_op jit(solution)/shard_map/ppermute | solution.py:563
  25.0 0.0 copy-done.1
  25.0 1.2 %attend.1 = bf16[8,2048]{1,0:T(8,128)(2,1)} custom-call(bf16[128,256]{1,0:T(8,128)(2,1)S(1)} %get-tuple-element.41.queries_ref, f32[128,128]{1,0:T(8,128)S(1)} %get-tuple-element.42.score_ref, bf16[8,128,256]{2,1,0:T(8,128)(2,1)S(1)} %copy-done.1, bf16[264,128]{1,0:T(8,128)(2,1)S(1)} %get-tuple-element.47.refs_0_, ...), custom_call_target="tpu_custom_call" | custom-call | flops 134217728 | bytes 524288 | tf_op jit(solution)/shard_map/attend/pallas_call | solution.py:402
  (1 shorter events, 0.0 us)
Async XLA Ops:
  1.2 4.0 %collective-permute-start = (f32[96,128]{1,0:T(8,128)S(1)}, f32[96,128]{1,0:T(8,128)S(1)}, u32[]{:S(2)}, u32[]{:S(2)}) collective-permute-start(f32[96,128]{1,0:T(8,128)S(1)} %get-tuple-element.31.own_ref), channel_id=1, source_target_pairs={{0,1},{1,0},{2,3},{3,2},{4,5},{5,4},{6,7},{7,6},{8,9},{9,8},{10,11... | collective-permute-start | bytes 147464 | tf_op jit(solution)/shard_map/ppermute | solution.py:551
  1.7 3.5 %copy-start.3 = (f32[4096]{0:T(1024)S(1)}, f32[4096]{0:T(1024)}, u32[]{:S(2)}) copy-start(f32[4096]{0:T(1024)} %param.14) | copy-start | bytes 49156
  6.2 1.5 %collective-permute-start.1 = (f32[96,512]{1,0:T(8,128)S(1)}, f32[96,512]{1,0:T(8,128)S(1)}, u32[]{:S(2)}, u32[]{:S(2)}) collective-permute-start(f32[96,512]{1,0:T(8,128)S(1)} %get-tuple-element.35), channel_id=1, source_target_pairs={{0,1},{1,0},{2,3},{3,2},{4,5},{5,4},{6,7},{7,6},{8,9},{9,8},{10,11... | collective-permute-start | bytes 589832 | tf_op jit(solution)/shard_map/ppermute | solution.py:558
  6.3 1.4 %copy-start.4 = (f32[256]{0:T(256)S(1)}, f32[256]{0:T(256)}, u32[]{:S(2)}) copy-start(f32[256]{0:T(256)} %param.17) | copy-start | bytes 3076
  6.3 1.4 %copy-start.5 = (f32[256]{0:T(256)S(1)}, f32[256]{0:T(256)}, u32[]{:S(2)}) copy-start(f32[256]{0:T(256)} %param.18) | copy-start | bytes 3076
  6.3 15.8 %copy-start = (bf16[8,128,256]{2,1,0:T(8,128)(2,1)S(1)}, bf16[8,128,256]{2,1,0:T(8,128)(2,1)}, u32[]{:S(2)}) copy-start(bf16[8,128,256]{2,1,0:T(8,128)(2,1)} %key_ref.1) | copy-start | bytes 1572868
  6.3 15.8 %copy-start.2 = (bf16[8,2048]{1,0:T(8,128)(2,1)S(1)}, bf16[8,2048]{1,0:T(8,128)(2,1)}, u32[]{:S(2)}) copy-start(bf16[8,2048]{1,0:T(8,128)(2,1)} %queries_ref) | copy-start | bytes 98308
  6.3 15.8 %copy-start.6 = (s32[8]{0:T(128)S(1)}, s32[8]{0:T(128)}, u32[]{:S(2)}) copy-start(s32[8]{0:T(128)} %param.22) | copy-start | bytes 100
  6.3 15.8 %copy-start.7 = (s32[8]{0:T(128)S(1)}, s32[8]{0:T(128)}, u32[]{:S(2)}) copy-start(s32[8]{0:T(128)} %param.23) | copy-start | bytes 100
  6.4 18.6 %copy-start.1 = (bf16[8,128,256]{2,1,0:T(8,128)(2,1)S(1)}, bf16[8,128,256]{2,1,0:T(8,128)(2,1)}, u32[]{:S(2)}) copy-start(bf16[8,128,256]{2,1,0:T(8,128)(2,1)} %cache_ref.1) | copy-start | bytes 1572868
  7.9 6.3 %collective-permute-start.2 = (bf16[264,128]{1,0:T(8,128)(2,1)S(1)}, bf16[264,128]{1,0:T(8,128)(2,1)S(1)}, u32[]{:S(2)}, u32[]{:S(2)}) collective-permute-start(bf16[264,128]{1,0:T(8,128)(2,1)S(1)} %get-tuple-element.44), channel_id=1, source_target_pairs={{0,18},{2,16},{4,22},{6,20},{8,26},{10,24},{12,30},{14,28},{16,2},... | collective-permute-start | bytes 202760 | tf_op jit(solution)/shard_map/ppermute | solution.py:563
  11.6 4.3 %collective-permute-start.3 = (bf16[264,128]{1,0:T(8,128)(2,1)S(1)}, bf16[264,128]{1,0:T(8,128)(2,1)S(1)}, u32[]{:S(2)}, u32[]{:S(2)}) collective-permute-start(bf16[264,128]{1,0:T(8,128)(2,1)S(1)} %get-tuple-element.45), channel_id=1, source_target_pairs={{0,2},{2,0},{4,6},{6,4},{8,10},{10,8},{12,14},{14,12},{16,18},{18,... | collective-permute-start | bytes 202760 | tf_op jit(solution)/shard_map/ppermute | solution.py:563
  12.1 4.3 %collective-permute-start.4 = (bf16[264,128]{1,0:T(8,128)(2,1)S(1)}, bf16[264,128]{1,0:T(8,128)(2,1)S(1)}, u32[]{:S(2)}, u32[]{:S(2)}) collective-permute-start(bf16[264,128]{1,0:T(8,128)(2,1)S(1)} %get-tuple-element.46), channel_id=1, source_target_pairs={{0,16},{2,18},{4,20},{6,22},{8,24},{10,26},{12,28},{14,30},{16,0},... | collective-permute-start | bytes 202760 | tf_op jit(solution)/shard_map/ppermute | solution.py:563
  16.4 7.9 %collective-permute-start.5 = (bf16[264,128]{1,0:T(8,128)(2,1)S(1)}, bf16[264,128]{1,0:T(8,128)(2,1)S(1)}, u32[]{:S(2)}, u32[]{:S(2)}) collective-permute-start(bf16[264,128]{1,0:T(8,128)(2,1)S(1)} %get-tuple-element.48), channel_id=1, source_target_pairs={{0,4},{2,6},{4,12},{6,14},{8,0},{10,2},{12,8},{14,10},{16,20},{18,... | collective-permute-start | bytes 202760 | tf_op jit(solution)/shard_map/ppermute | solution.py:563
  18.0 6.2 %collective-permute-start.6 = (bf16[264,128]{1,0:T(8,128)(2,1)S(1)}, bf16[264,128]{1,0:T(8,128)(2,1)S(1)}, u32[]{:S(2)}, u32[]{:S(2)}) collective-permute-start(bf16[264,128]{1,0:T(8,128)(2,1)S(1)} %get-tuple-element.49), channel_id=1, source_target_pairs={{0,12},{2,14},{4,8},{6,10},{8,4},{10,6},{12,0},{14,2},{16,28},{18,... | collective-permute-start | bytes 202760 | tf_op jit(solution)/shard_map/ppermute | solution.py:563
  20.5 4.5 %collective-permute-start.7 = (bf16[264,128]{1,0:T(8,128)(2,1)S(1)}, bf16[264,128]{1,0:T(8,128)(2,1)S(1)}, u32[]{:S(2)}, u32[]{:S(2)}) collective-permute-start(bf16[264,128]{1,0:T(8,128)(2,1)S(1)} %get-tuple-element.50), channel_id=1, source_target_pairs={{0,8},{2,10},{4,0},{6,2},{8,12},{10,14},{12,4},{14,6},{16,24},{18,... | collective-permute-start | bytes 202760 | tf_op jit(solution)/shard_map/ppermute | solution.py:563

commit v11 on v10

--- a/solution.py
+++ b/solution.py
@@ -175,8 +175,8 @@
     pick_ref[...] = (place == leaves * capacity + order).astype(jnp.bfloat16)
     lane = lands * capacity + order
     parts = slots // HEAD
-    block = lax.broadcasted_iota(jnp.int32, (partitions * parts, rows), 0)
-    named = block == leaves * parts + lane // HEAD
+    block = lax.broadcasted_iota(jnp.int32, (ids_ref.shape[0], rows), 0)
+    named = block == first * (ids_ref.shape[0] // len(near)) + second * parts + lane // HEAD
     named = jnp.where(named, (local + 1).astype(jnp.float32), 0.0).astype(jnp.bfloat16)
     spot = lax.broadcasted_iota(jnp.int32, (HEAD, rows), 0) == lane % HEAD
     ids_ref[...] = nt_dot(named, spot.astype(jnp.bfloat16))
@@ -249,15 +249,16 @@
 
 
 def beside(here, session, w_key, w_value, sizes):
-    partitions, *sizes = sizes
-    slots, rows = partitions * sizes[1], session.shape[1]
-    return pl.pallas_call(
-        functools.partial(beside_kernel, *sizes),
+    partitions, _, capacity, near, _ = sizes
+    slots, rows = partitions * capacity, session.shape[1]
+    id_rows = -(-partitions // len(near) * slots // (16 * HEAD)) * 16 * len(near)
+    return pl.pallas_call(
+        functools.partial(beside_kernel, *sizes[1:]),
         out_shape=(
             jax.ShapeDtypeStruct(w_key.shape, w_key.dtype),
             jax.ShapeDtypeStruct(w_value.shape, w_value.dtype),
             jax.ShapeDtypeStruct((slots, rows), jnp.bfloat16),
-            jax.ShapeDtypeStruct((partitions * slots // HEAD, HEAD), jnp.float32),
+            jax.ShapeDtypeStruct((id_rows, HEAD), jnp.float32),
         ),
         in_specs=[SMEM] + [HBM] * 3,
         out_specs=(VMEM,) * 4,

time: 26.4 us -> 26.5 us (level)
  no operation moved by 1% of the time
where the time goes in v11:
time: 26.5 us; the launch traced here: 26.3 us
  starting transfers between devices  10.7 us (40%)
  Pallas kernels  8.33 us (31%)
  waiting for transfers between devices  7.2 us (27%)
    ppermute x6, starting transfers between devices, step(): lax.ppermute(a, ('grp', 'seq'), p)  10 us
    ppermute x6, waiting for transfers between devices, step(): lax.ppermute(a, ('grp', 'seq'), p)  6.69 us
    pallas_call x1, Pallas kernels, beside(): pl.pallas_call(functools.partial(beside_kernel, *sizes[1:]), out_shape=(j...  3.51 us
    pallas_call x1, Pallas kernels, attend(): pl.pallas_call(functools.partial(attend_kernel, near, capacity), out_shap...  1.23 us
    pallas_call x1, Pallas kernels, partial_squares(): pl.pallas_call(squares_kernel, out_shape=(jax.ShapeDtypeStruct((rows, HEA...  1.21 us
    pallas_call x1, Pallas kernels, send_products(): pl.pallas_call(functools.partial(send_kernel, features), out_shape=(jax.S...  0.88 us
    pallas_call x1, Pallas kernels, keep_products(): pl.pallas_call(keep_kernel, out_shape=jax.ShapeDtypeStruct((rows, width),...  0.8 us
  transfers between devices with their start and end apart: 8, of which 6 were waited for; matrix products, arithmetic and copies ran while one was open for 0% of the time, Pallas kernels for 18%

profile of v11, /device:TPU:0, one launch (start us, length us, event | category | flops | bytes accessed | tf_op | source)
XLA Modules:
  0.0 26.3 jit_solution(15117224784545592654)
XLA Ops:
  0.0 1.2 %partial_squares.1 = (f32[96,128]{1,0:T(8,128)S(1)}, bf16[96,4096]{1,0:T(8,128)(2,1)S(1)}) custom-call(bf16[96,4096]{1,0:T(8,128)(2,1)} %frames_ref.1), custom_call_target="tpu_custom_call" | custom-call | flops 786432 | bytes 786432 | tf_op jit(solution)/shard_map/partial_squares/pallas_call | solution.py:64
  1.2 0.5 %collective-permute-start = (f32[96,128]{1,0:T(8,128)S(1)}, f32[96,128]{1,0:T(8,128)S(1)}, u32[]{:S(2)}, u32[]{:S(2)}) collective-permute-start(f32[96,128]{1,0:T(8,128)S(1)} %get-tuple-element.31.own_ref), channel_id=1, source_target_pairs={{0,1},{1,0},{2,3},{3,2},{4,5},{5,4},{6,7},{7,6},{8,9},{9,8},{10,11... | collective-permute-start | bytes 147464 | tf_op jit(solution)/shard_map/ppermute | solution.py:552
  1.7 0.0 copy-start.3
  1.7 3.5 %beside.1 = (bf16[4096,512]{1,0:T(8,128)(2,1)S(1)}, bf16[4096,512]{1,0:T(8,128)(2,1)S(1)}, bf16[256,96]{1,0:T(8,128)(2,1)S(1)}, f32[64,128]{1,0:T(8,128)S(1)}) custom-call(s32[1]{0:T(128)} %bitcast.2.here_ref, s32[1,96]{1,0:T(1,128)} %bitcast.13, bf16[4096,512]{1,0:T(8,128)(2,1)} %w_key_ref.1, bf16[4096,512]{1,0:T(8,128)(2,1)} %w_value_ref.1), custom_call_target="tpu_custom_call" | custom-call | flops 9437184 | bytes 8388608 | tf_op jit(solution)/shard_map/beside/pallas_call | solution.py:255
  5.3 0.0 collective-permute-done.other_ref
  5.3 0.0 copy-done.3
  5.3 0.9 %send_products.1 = (bf16[96,4096]{1,0:T(8,128)(2,1)S(1)}, f32[96,512]{1,0:T(8,128)S(1)}) custom-call(s32[1]{0:T(128)} %bitcast.4.index_ref, bf16[96,4096]{1,0:T(8,128)(2,1)S(1)} %get-tuple-element.30.frames_ref, f32[96,128]{1,0:T(8,128)S(1)} %get-tuple-element.31.own_ref, f32[96,128]{1,0:T(8,128)S(1)} %collective-permute-done.other_ref, ...), custom_call_target="tpu_custom_call" | custom-call | flops 402653184 | bytes 4194304 | tf_op jit(solution)/shard_map/send_products/pallas_call | solution.py:100
  6.2 0.2 collective-permute-start.1
  6.3 0.0 copy-start.4
  6.3 0.0 copy-start.5
  6.3 0.0 copy-start
  6.3 0.0 copy-start.2
  6.3 0.0 copy-start.6
  6.3 0.0 copy-start.7
  6.4 0.0 copy-start.1
  6.4 0.8 %keep_products.1.kept_ref = f32[96,512]{1,0:T(8,128)S(1)} custom-call(s32[1]{0:T(128)} %bitcast.4.index_ref, bf16[96,4096]{1,0:T(8,128)(2,1)S(1)} %get-tuple-element.34.normed_ref, bf16[4096,512]{1,0:T(8,128)(2,1)S(1)} %get-tuple-element.32.key_ref, bf16[4096,512]{1,0:T(8,128)(2,1)S(1)} %get-tuple-element.33.value_ref), custom_call_target="tpu_custom_call" | custom-call | flops 402653184 | bytes 4194304 | tf_op jit(solution)/shard_map/keep_products/pallas_call | solution.py:121
  7.2 0.5 %collective-permute-done.1.got_ref = f32[96,512]{1,0:T(8,128)S(1)} collective-permute-done((f32[96,512]{1,0:T(8,128)S(1)}, f32[96,512]{1,0:T(8,128)S(1)}, u32[]{:S(2)}, u32[]{:S(2)}) %collective-permute-start.1) | collective-permute-done | bytes 196640 | tf_op jit(solution)/shard_map/ppermute | solution.py:559
  7.7 0.0 copy-done.4
  7.7 0.0 copy-done.5
  7.7 0.2 pack.1
  7.9 3.7 %collective-permute-start.2 = (bf16[272,128]{1,0:T(8,128)(2,1)S(1)}, bf16[272,128]{1,0:T(8,128)(2,1)S(1)}, u32[]{:S(2)}, u32[]{:S(2)}) collective-permute-start(bf16[272,128]{1,0:T(8,128)(2,1)S(1)} %get-tuple-element.44), channel_id=1, source_target_pairs={{0,18},{2,16},{4,22},{6,20},{8,26},{10,24},{12,30},{14,28},{16,2},... | collective-permute-start | bytes 208904 | tf_op jit(solution)/shard_map/ppermute | solution.py:564
  11.6 0.5 %collective-permute-start.3 = (bf16[272,128]{1,0:T(8,128)(2,1)S(1)}, bf16[272,128]{1,0:T(8,128)(2,1)S(1)}, u32[]{:S(2)}, u32[]{:S(2)}) collective-permute-start(bf16[272,128]{1,0:T(8,128)(2,1)S(1)} %get-tuple-element.45), channel_id=1, source_target_pairs={{0,2},{2,0},{4,6},{6,4},{8,10},{10,8},{12,14},{14,12},{16,18},{18,... | collective-permute-start | bytes 208904 | tf_op jit(solution)/shard_map/ppermute | solution.py:564
  12.1 0.1 collective-permute-start.4
  12.2 2.1 %collective-permute-done.2.refs_1_ = bf16[272,128]{1,0:T(8,128)(2,1)S(1)} collective-permute-done((bf16[272,128]{1,0:T(8,128)(2,1)S(1)}, bf16[272,128]{1,0:T(8,128)(2,1)S(1)}, u32[]{:S(2)}, u32[]{:S(2)}) %collective-permute-start.2) | collective-permute-done | bytes 69664 | tf_op jit(solution)/shard_map/ppermute | solution.py:564
  14.3 1.6 %collective-permute-done.3.refs_2_ = bf16[272,128]{1,0:T(8,128)(2,1)S(1)} collective-permute-done((bf16[272,128]{1,0:T(8,128)(2,1)S(1)}, bf16[272,128]{1,0:T(8,128)(2,1)S(1)}, u32[]{:S(2)}, u32[]{:S(2)}) %collective-permute-start.3) | collective-permute-done | bytes 69664 | tf_op jit(solution)/shard_map/ppermute | solution.py:564
  15.9 0.5 %collective-permute-done.4.refs_3_ = bf16[272,128]{1,0:T(8,128)(2,1)S(1)} collective-permute-done((bf16[272,128]{1,0:T(8,128)(2,1)S(1)}, bf16[272,128]{1,0:T(8,128)(2,1)S(1)}, u32[]{:S(2)}, u32[]{:S(2)}) %collective-permute-start.4) | collective-permute-done | bytes 69664 | tf_op jit(solution)/shard_map/ppermute | solution.py:564
  16.4 1.6 %collective-permute-start.5 = (bf16[272,128]{1,0:T(8,128)(2,1)S(1)}, bf16[272,128]{1,0:T(8,128)(2,1)S(1)}, u32[]{:S(2)}, u32[]{:S(2)}) collective-permute-start(bf16[272,128]{1,0:T(8,128)(2,1)S(1)} %get-tuple-element.48), channel_id=1, source_target_pairs={{0,4},{2,6},{4,12},{6,14},{8,0},{10,2},{12,8},{14,10},{16,20},{18,... | collective-permute-start | bytes 208904 | tf_op jit(solution)/shard_map/ppermute | solution.py:564
  18.1 2.5 %collective-permute-start.6 = (bf16[272,128]{1,0:T(8,128)(2,1)S(1)}, bf16[272,128]{1,0:T(8,128)(2,1)S(1)}, u32[]{:S(2)}, u32[]{:S(2)}) collective-permute-start(bf16[272,128]{1,0:T(8,128)(2,1)S(1)} %get-tuple-element.49), channel_id=1, source_target_pairs={{0,12},{2,14},{4,8},{6,10},{8,4},{10,6},{12,0},{14,2},{16,28},{18,... | collective-permute-start | bytes 208904 | tf_op jit(solution)/shard_map/ppermute | solution.py:564
  20.5 1.6 %collective-permute-start.7 = (bf16[272,128]{1,0:T(8,128)(2,1)S(1)}, bf16[272,128]{1,0:T(8,128)(2,1)S(1)}, u32[]{:S(2)}, u32[]{:S(2)}) collective-permute-start(bf16[272,128]{1,0:T(8,128)(2,1)S(1)} %get-tuple-element.50), channel_id=1, source_target_pairs={{0,8},{2,10},{4,0},{6,2},{8,12},{10,14},{12,4},{14,6},{16,24},{18,... | collective-permute-start | bytes 208904 | tf_op jit(solution)/shard_map/ppermute | solution.py:564
  22.1 0.0 copy-done
  22.1 0.0 copy-done.2
  22.1 0.0 copy-done.6
  22.1 0.0 copy-done.7
  22.1 0.5 %cached_scores.1 = (f32[128,128]{1,0:T(8,128)S(1)}, bf16[128,256]{1,0:T(8,128)(2,1)S(1)}) custom-call(s32[1,8]{1,0:T(1,128)S(1)} %bitcast.11, s32[1,8]{1,0:T(1,128)S(1)} %bitcast.12, bf16[8,2048]{1,0:T(8,128)(2,1)S(1)} %copy-done.2, bf16[8,128,256]{2,1,0:T(8,128)(2,1)S(1)} %copy-done), custom_call_target="tpu_custom_call" | custom-call | flops 33554432 | bytes 524288 | tf_op jit(solution)/shard_map/cached_scores/pallas_call | solution.py:275
  22.6 1.8 %collective-permute-done.5.refs_1_ = bf16[272,128]{1,0:T(8,128)(2,1)S(1)} collective-permute-done((bf16[272,128]{1,0:T(8,128)(2,1)S(1)}, bf16[272,128]{1,0:T(8,128)(2,1)S(1)}, u32[]{:S(2)}, u32[]{:S(2)}) %collective-permute-start.5) | collective-permute-done | bytes 69664 | tf_op jit(solution)/shard_map/ppermute | solution.py:564
  24.4 0.0 collective-permute-done.6.refs_2_
  24.4 0.7 %collective-permute-done.7.refs_3_ = bf16[272,128]{1,0:T(8,128)(2,1)S(1)} collective-permute-done((bf16[272,128]{1,0:T(8,128)(2,1)S(1)}, bf16[272,128]{1,0:T(8,128)(2,1)S(1)}, u32[]{:S(2)}, u32[]{:S(2)}) %collective-permute-start.7) | collective-permute-done | bytes 69664 | tf_op jit(solution)/shard_map/ppermute | solution.py:564
  25.1 0.0 copy-done.1
  25.1 1.2 %attend.1 = bf16[8,2048]{1,0:T(8,128)(2,1)} custom-call(bf16[128,256]{1,0:T(8,128)(2,1)S(1)} %get-tuple-element.41.queries_ref, f32[128,128]{1,0:T(8,128)S(1)} %get-tuple-element.42.score_ref, bf16[8,128,256]{2,1,0:T(8,128)(2,1)S(1)} %copy-done.1, bf16[272,128]{1,0:T(8,128)(2,1)S(1)} %get-tuple-element.47.refs_0_, ...), custom_call_target="tpu_custom_call" | custom-call | flops 134217728 | bytes 524288 | tf_op jit(solution)/shard_map/attend/pallas_call | solution.py:403
  (1 shorter events, 0.0 us)
Async XLA Ops:
  1.2 4.0 %collective-permute-start = (f32[96,128]{1,0:T(8,128)S(1)}, f32[96,128]{1,0:T(8,128)S(1)}, u32[]{:S(2)}, u32[]{:S(2)}) collective-permute-start(f32[96,128]{1,0:T(8,128)S(1)} %get-tuple-element.31.own_ref), channel_id=1, source_target_pairs={{0,1},{1,0},{2,3},{3,2},{4,5},{5,4},{6,7},{7,6},{8,9},{9,8},{10,11... | collective-permute-start | bytes 147464 | tf_op jit(solution)/shard_map/ppermute | solution.py:552
  1.7 3.5 %copy-start.3 = (f32[4096]{0:T(1024)S(1)}, f32[4096]{0:T(1024)}, u32[]{:S(2)}) copy-start(f32[4096]{0:T(1024)} %param.14) | copy-start | bytes 49156
  6.2 1.5 %collective-permute-start.1 = (f32[96,512]{1,0:T(8,128)S(1)}, f32[96,512]{1,0:T(8,128)S(1)}, u32[]{:S(2)}, u32[]{:S(2)}) collective-permute-start(f32[96,512]{1,0:T(8,128)S(1)} %get-tuple-element.35), channel_id=1, source_target_pairs={{0,1},{1,0},{2,3},{3,2},{4,5},{5,4},{6,7},{7,6},{8,9},{9,8},{10,11... | collective-permute-start | bytes 589832 | tf_op jit(solution)/shard_map/ppermute | solution.py:559
  6.3 1.4 %copy-start.4 = (f32[256]{0:T(256)S(1)}, f32[256]{0:T(256)}, u32[]{:S(2)}) copy-start(f32[256]{0:T(256)} %param.17) | copy-start | bytes 3076
  6.3 1.4 %copy-start.5 = (f32[256]{0:T(256)S(1)}, f32[256]{0:T(256)}, u32[]{:S(2)}) copy-start(f32[256]{0:T(256)} %param.18) | copy-start | bytes 3076
  6.3 15.8 %copy-start = (bf16[8,128,256]{2,1,0:T(8,128)(2,1)S(1)}, bf16[8,128,256]{2,1,0:T(8,128)(2,1)}, u32[]{:S(2)}) copy-start(bf16[8,128,256]{2,1,0:T(8,128)(2,1)} %key_ref.1) | copy-start | bytes 1572868
  6.3 15.8 %copy-start.2 = (bf16[8,2048]{1,0:T(8,128)(2,1)S(1)}, bf16[8,2048]{1,0:T(8,128)(2,1)}, u32[]{:S(2)}) copy-start(bf16[8,2048]{1,0:T(8,128)(2,1)} %queries_ref) | copy-start | bytes 98308
  6.3 15.8 %copy-start.6 = (s32[8]{0:T(128)S(1)}, s32[8]{0:T(128)}, u32[]{:S(2)}) copy-start(s32[8]{0:T(128)} %param.22) | copy-start | bytes 100
  6.3 15.8 %copy-start.7 = (s32[8]{0:T(128)S(1)}, s32[8]{0:T(128)}, u32[]{:S(2)}) copy-start(s32[8]{0:T(128)} %param.23) | copy-start | bytes 100
  6.4 18.8 %copy-start.1 = (bf16[8,128,256]{2,1,0:T(8,128)(2,1)S(1)}, bf16[8,128,256]{2,1,0:T(8,128)(2,1)}, u32[]{:S(2)}) copy-start(bf16[8,128,256]{2,1,0:T(8,128)(2,1)} %cache_ref.1) | copy-start | bytes 1572868
  7.9 6.4 %collective-permute-start.2 = (bf16[272,128]{1,0:T(8,128)(2,1)S(1)}, bf16[272,128]{1,0:T(8,128)(2,1)S(1)}, u32[]{:S(2)}, u32[]{:S(2)}) collective-permute-start(bf16[272,128]{1,0:T(8,128)(2,1)S(1)} %get-tuple-element.44), channel_id=1, source_target_pairs={{0,18},{2,16},{4,22},{6,20},{8,26},{10,24},{12,30},{14,28},{16,2},... | collective-permute-start | bytes 208904 | tf_op jit(solution)/shard_map/ppermute | solution.py:564
  11.6 4.3 %collective-permute-start.3 = (bf16[272,128]{1,0:T(8,128)(2,1)S(1)}, bf16[272,128]{1,0:T(8,128)(2,1)S(1)}, u32[]{:S(2)}, u32[]{:S(2)}) collective-permute-start(bf16[272,128]{1,0:T(8,128)(2,1)S(1)} %get-tuple-element.45), channel_id=1, source_target_pairs={{0,2},{2,0},{4,6},{6,4},{8,10},{10,8},{12,14},{14,12},{16,18},{18,... | collective-permute-start | bytes 208904 | tf_op jit(solution)/shard_map/ppermute | solution.py:564
  12.1 4.3 %collective-permute-start.4 = (bf16[272,128]{1,0:T(8,128)(2,1)S(1)}, bf16[272,128]{1,0:T(8,128)(2,1)S(1)}, u32[]{:S(2)}, u32[]{:S(2)}) collective-permute-start(bf16[272,128]{1,0:T(8,128)(2,1)S(1)} %get-tuple-element.46), channel_id=1, source_target_pairs={{0,16},{2,18},{4,20},{6,22},{8,24},{10,26},{12,28},{14,30},{16,0},... | collective-permute-start | bytes 208904 | tf_op jit(solution)/shard_map/ppermute | solution.py:564
  16.4 8.0 %collective-permute-start.5 = (bf16[272,128]{1,0:T(8,128)(2,1)S(1)}, bf16[272,128]{1,0:T(8,128)(2,1)S(1)}, u32[]{:S(2)}, u32[]{:S(2)}) collective-permute-start(bf16[272,128]{1,0:T(8,128)(2,1)S(1)} %get-tuple-element.48), channel_id=1, source_target_pairs={{0,4},{2,6},{4,12},{6,14},{8,0},{10,2},{12,8},{14,10},{16,20},{18,... | collective-permute-start | bytes 208904 | tf_op jit(solution)/shard_map/ppermute | solution.py:564
  18.1 6.3 %collective-permute-start.6 = (bf16[272,128]{1,0:T(8,128)(2,1)S(1)}, bf16[272,128]{1,0:T(8,128)(2,1)S(1)}, u32[]{:S(2)}, u32[]{:S(2)}) collective-permute-start(bf16[272,128]{1,0:T(8,128)(2,1)S(1)} %get-tuple-element.49), channel_id=1, source_target_pairs={{0,12},{2,14},{4,8},{6,10},{8,4},{10,6},{12,0},{14,2},{16,28},{18,... | collective-permute-start | bytes 208904 | tf_op jit(solution)/shard_map/ppermute | solution.py:564
  20.5 4.6 %collective-permute-start.7 = (bf16[272,128]{1,0:T(8,128)(2,1)S(1)}, bf16[272,128]{1,0:T(8,128)(2,1)S(1)}, u32[]{:S(2)}, u32[]{:S(2)}) collective-permute-start(bf16[272,128]{1,0:T(8,128)(2,1)S(1)} %get-tuple-element.50), channel_id=1, source_target_pairs={{0,8},{2,10},{4,0},{6,2},{8,12},{10,14},{12,4},{14,6},{16,24},{18,... | collective-permute-start | bytes 208904 | tf_op jit(solution)/shard_map/ppermute | solution.py:564

commit v12 on v11

--- a/solution.py
+++ b/solution.py
@@ -348,34 +348,60 @@
     )(*blocks)
 
 
-def attend_kernel(near, capacity, queries_ref, score_ref, cache_ref, *refs):
+def rows_of(refs, vectors, tall):
+    columns = []
+    for vector in vectors:
+        part = slice(vector * tall, (vector + 1) * tall)
+        columns.append(jnp.concatenate([ref[part, :] for ref in refs], axis=0))
+    return jnp.concatenate(columns, axis=1)
+
+
+def score_fresh(refs, begin, parts, tall, heads, sessions, queries):
+    rows, slots = queries.shape[0], len(refs) * tall
+    first = begin * tall // HEAD
+    ids = [
+        sum(
+            ref[2 * heads * tall :, :].astype(jnp.float32)[at : at + 1]
+            for ref, at in ((ref, (begin + k) * parts + part) for k, ref in enumerate(refs))
+        )
+        for part in range(first, first + slots // HEAD)
+    ]
+    ids = jnp.concatenate(ids, axis=1).astype(jnp.int32)
+    own = lax.broadcasted_iota(jnp.int32, (rows, slots), 0) % sessions + 1 == ids
+    fresh = nt_dot(queries, rows_of(refs, range(heads), tall)) * (HEAD**-0.5)
+    return jnp.where(own, fresh, -jnp.inf)
+
+
+def early_kernel(tall, parts, sessions, queries_ref, *refs):
+    *got_refs, out_ref = refs
+    heads = queries_ref.shape[1] // HEAD
+    out_ref[...] = score_fresh(got_refs, 0, parts, tall, heads, sessions, queries_ref[...])
+
+
+def early_scores(got, queries, tall, parts, sessions):
+    rows = queries.shape[0]
+    return pl.pallas_call(
+        functools.partial(early_kernel, tall, parts, sessions),
+        out_shape=jax.ShapeDtypeStruct((rows, len(got) * tall), jnp.float32),
+        in_specs=[VMEM] * (1 + len(got)),
+        out_specs=VMEM,
+        compiler_params=params(8),
+        cost_estimate=cost(2 * rows * len(got) * tall * queries.shape[1], 2 * queries.size),
+        name="early_scores",
+    )(queries, *got)
+
+
+def attend_kernel(near, capacity, queries_ref, score_ref, early_ref, cache_ref, *refs):
     *got_refs, out_ref = refs
     rows, window = score_ref.shape
     sessions, _, width = cache_ref.shape
     heads = width // HEAD
     tall = near * capacity
-    slots = len(got_refs) * tall
-    parts = slots // HEAD
-    ids = [
-        sum(
-            ref[2 * heads * tall :, :].astype(jnp.float32)[step * parts + part : step * parts + part + 1]
-            for step, ref in enumerate(got_refs)
-        )
-        for part in range(parts)
-    ]
-    ids = jnp.concatenate(ids, axis=1).astype(jnp.int32)
-    own = lax.broadcasted_iota(jnp.int32, (rows, slots), 0) % sessions + 1 == ids
-
-    def rows_of(vectors):
-        columns = []
-        for vector in vectors:
-            part = slice(vector * tall, (vector + 1) * tall)
-            columns.append(jnp.concatenate([ref[part, :] for ref in got_refs], axis=0))
-        return jnp.concatenate(columns, axis=1)
-
+    parts = len(got_refs) * tall // HEAD
+    begin = early_ref.shape[1] // tall
     cached = score_ref[...]
-    fresh = nt_dot(queries_ref[...], rows_of(range(heads))) * (HEAD**-0.5)
-    fresh = jnp.where(own, fresh, -jnp.inf)
+    late = score_fresh(got_refs[begin:], begin, parts, tall, heads, sessions, queries_ref[...])
+    fresh = jnp.concatenate([early_ref[...], late], axis=1)
     largest = jnp.maximum(
         jnp.max(cached, axis=1, keepdims=True), jnp.max(fresh, axis=1, keepdims=True)
     )
@@ -383,7 +409,7 @@
     fresh = jnp.exp(fresh - largest)
     total = jnp.sum(cached, axis=1, keepdims=True) + jnp.sum(fresh, axis=1, keepdims=True)
     cached = cached / total
-    attended = dot((fresh / total).astype(jnp.bfloat16), rows_of(range(heads, 2 * heads)))
+    attended = dot((fresh / total).astype(jnp.bfloat16), rows_of(got_refs, range(heads, 2 * heads), tall))
     row_session = lax.broadcasted_iota(jnp.int32, (rows, window), 0) % sessions
     for session in range(0, sessions, 2):
         weights = jnp.concatenate(
@@ -399,18 +425,18 @@
             ].astype(jnp.bfloat16)
 
 
-def attend(got, queries, scores, cache_value, near, capacity):
+def attend(got, queries, scores, early, cache_value, near, capacity):
     return pl.pallas_call(
         functools.partial(attend_kernel, near, capacity),
         out_shape=jax.ShapeDtypeStruct(
             (cache_value.shape[0], queries.shape[1] * GROUP), jnp.bfloat16
         ),
-        in_specs=[VMEM] * (3 + len(got)),
+        in_specs=[VMEM] * (4 + len(got)),
         out_specs=VMEM,
         compiler_params=params(8),
         cost_estimate=cost(4 * queries.shape[0] * cache_value.size, 2 * cache_value.size),
         name="attend",
-    )(queries, scores, cache_value, *got)
+    )(queries, scores, early, cache_value, *got)
 
 
 def project(frame_rows, ln_gain, w_key, w_value, k_bias, v_bias):
@@ -540,7 +566,7 @@
     capacity = max(2, 5 * rows // (2 * partitions) + 1)
     members = lax.axis_size("seq")
     near = first_masks(lax.axis_size("grp"), members)
-    if near is None or shares != 2 or per_shard % 8 or capacity % 16 or partitions * capacity % HEAD:
+    if near is None or shares != 2 or per_shard % 8 or capacity % 16 or partitions * capacity % (2 * HEAD):
         return general(
             frames, token_session, ln_gain, w_key, w_value, k_bias, v_bias, queries, cache_key, cache_value,
             cache_start, cache_len,
@@ -570,7 +596,9 @@
     blocks = step(blocks, [[(i, i ^ mask) for i in range(partitions)] for mask in near])
     blocks = regroup(blocks, members // 2, vectors, capacity)
     blocks = step(blocks, second_pairs(partitions, members))
-    return attend(blocks, laid, scores, cache_value, len(near), capacity)
+    tall, line = len(near) * capacity, members // 2
+    early = early_scores(blocks[: line // 2], laid, tall, line * tall // HEAD, per_shard)
+    return attend(blocks, laid, scores, early, cache_value, len(near), capacity)
 
 
 def solution(mesh):

time: 26.5 us -> 26.4 us (level)
  transfers between devices with their start and end apart: 8 -> 8, of which waited for: 6 -> 6; matrix products, arithmetic and copies ran while one was open for 0% -> 0% of each run, Pallas kernels for 18% -> 19%
where the time goes in v12:
time: 26.4 us; the launch traced here: 26.3 us
  starting transfers between devices  10.7 us (41%)
  Pallas kernels  8.47 us (32%)
  waiting for transfers between devices  7.02 us (27%)
    ppermute x6, starting transfers between devices, step(): lax.ppermute(a, ('grp', 'seq'), p)  10 us
    ppermute x6, waiting for transfers between devices, step(): lax.ppermute(a, ('grp', 'seq'), p)  6.51 us
    pallas_call x1, Pallas kernels, beside(): pl.pallas_call(functools.partial(beside_kernel, *sizes[1:]), out_shape=(j...  3.51 us
    pallas_call x1, Pallas kernels, partial_squares(): pl.pallas_call(squares_kernel, out_shape=(jax.ShapeDtypeStruct((rows, HEA...  1.21 us
    pallas_call x1, Pallas kernels, attend(): pl.pallas_call(functools.partial(attend_kernel, near, capacity), out_shap...  1.19 us
    pallas_call x1, Pallas kernels, send_products(): pl.pallas_call(functools.partial(send_kernel, features), out_shape=(jax.S...  0.88 us
    pallas_call x1, Pallas kernels, keep_products(): pl.pallas_call(keep_kernel, out_shape=jax.ShapeDtypeStruct((rows, width),...  0.8 us
  transfers between devices with their start and end apart: 8, of which 6 were waited for; matrix products, arithmetic and copies ran while one was open for 0% of the time, Pallas kernels for 19%

profile of v12, /device:TPU:0, one launch (start us, length us, event | category | flops | bytes accessed | tf_op | source)
XLA Modules:
  0.0 26.3 jit_solution(8833661762000819433)
XLA Ops:
  0.0 1.2 %partial_squares.1 = (f32[96,128]{1,0:T(8,128)S(1)}, bf16[96,4096]{1,0:T(8,128)(2,1)S(1)}) custom-call(bf16[96,4096]{1,0:T(8,128)(2,1)} %frames_ref.1), custom_call_target="tpu_custom_call" | custom-call | flops 786432 | bytes 786432 | tf_op jit(solution)/shard_map/partial_squares/pallas_call | solution.py:64
  1.2 0.5 %collective-permute-start = (f32[96,128]{1,0:T(8,128)S(1)}, f32[96,128]{1,0:T(8,128)S(1)}, u32[]{:S(2)}, u32[]{:S(2)}) collective-permute-start(f32[96,128]{1,0:T(8,128)S(1)} %get-tuple-element.31.own_ref), channel_id=1, source_target_pairs={{0,1},{1,0},{2,3},{3,2},{4,5},{5,4},{6,7},{7,6},{8,9},{9,8},{10,11... | collective-permute-start | bytes 147464 | tf_op jit(solution)/shard_map/ppermute | solution.py:578
  1.7 0.0 copy-start.3
  1.7 3.5 %beside.1 = (bf16[4096,512]{1,0:T(8,128)(2,1)S(1)}, bf16[4096,512]{1,0:T(8,128)(2,1)S(1)}, bf16[256,96]{1,0:T(8,128)(2,1)S(1)}, f32[64,128]{1,0:T(8,128)S(1)}) custom-call(s32[1]{0:T(128)} %bitcast.2.here_ref, s32[1,96]{1,0:T(1,128)} %bitcast.13, bf16[4096,512]{1,0:T(8,128)(2,1)} %w_key_ref.1, bf16[4096,512]{1,0:T(8,128)(2,1)} %w_value_ref.1), custom_call_target="tpu_custom_call" | custom-call | flops 9437184 | bytes 8388608 | tf_op jit(solution)/shard_map/beside/pallas_call | solution.py:255
  5.3 0.0 collective-permute-done.other_ref
  5.3 0.0 copy-done.3
  5.3 0.9 %send_products.1 = (bf16[96,4096]{1,0:T(8,128)(2,1)S(1)}, f32[96,512]{1,0:T(8,128)S(1)}) custom-call(s32[1]{0:T(128)} %bitcast.4.index_ref, bf16[96,4096]{1,0:T(8,128)(2,1)S(1)} %get-tuple-element.30.frames_ref, f32[96,128]{1,0:T(8,128)S(1)} %get-tuple-element.31.own_ref, f32[96,128]{1,0:T(8,128)S(1)} %collective-permute-done.other_ref, ...), custom_call_target="tpu_custom_call" | custom-call | flops 402653184 | bytes 4194304 | tf_op jit(solution)/shard_map/send_products/pallas_call | solution.py:100
  6.2 0.2 collective-permute-start.1
  6.3 0.0 copy-start.4
  6.3 0.0 copy-start.5
  6.3 0.0 copy-start
  6.3 0.0 copy-start.2
  6.3 0.0 copy-start.6
  6.3 0.0 copy-start.7
  6.4 0.0 copy-start.1
  6.4 0.8 %keep_products.1.kept_ref = f32[96,512]{1,0:T(8,128)S(1)} custom-call(s32[1]{0:T(128)} %bitcast.4.index_ref, bf16[96,4096]{1,0:T(8,128)(2,1)S(1)} %get-tuple-element.34.normed_ref, bf16[4096,512]{1,0:T(8,128)(2,1)S(1)} %get-tuple-element.32.key_ref, bf16[4096,512]{1,0:T(8,128)(2,1)S(1)} %get-tuple-element.33.value_ref), custom_call_target="tpu_custom_call" | custom-call | flops 402653184 | bytes 4194304 | tf_op jit(solution)/shard_map/keep_products/pallas_call | solution.py:121
  7.2 0.5 %collective-permute-done.1.got_ref = f32[96,512]{1,0:T(8,128)S(1)} collective-permute-done((f32[96,512]{1,0:T(8,128)S(1)}, f32[96,512]{1,0:T(8,128)S(1)}, u32[]{:S(2)}, u32[]{:S(2)}) %collective-permute-start.1) | collective-permute-done | bytes 196640 | tf_op jit(solution)/shard_map/ppermute | solution.py:585
  7.7 0.0 copy-done.4
  7.7 0.0 copy-done.5
  7.7 0.2 pack.1
  7.9 3.7 %collective-permute-start.2 = (bf16[272,128]{1,0:T(8,128)(2,1)S(1)}, bf16[272,128]{1,0:T(8,128)(2,1)S(1)}, u32[]{:S(2)}, u32[]{:S(2)}) collective-permute-start(bf16[272,128]{1,0:T(8,128)(2,1)S(1)} %get-tuple-element.44), channel_id=1, source_target_pairs={{0,18},{2,16},{4,22},{6,20},{8,26},{10,24},{12,30},{14,28},{16,2},... | collective-permute-start | bytes 208904 | tf_op jit(solution)/shard_map/ppermute | solution.py:590
  11.6 0.5 %collective-permute-start.3 = (bf16[272,128]{1,0:T(8,128)(2,1)S(1)}, bf16[272,128]{1,0:T(8,128)(2,1)S(1)}, u32[]{:S(2)}, u32[]{:S(2)}) collective-permute-start(bf16[272,128]{1,0:T(8,128)(2,1)S(1)} %get-tuple-element.45), channel_id=1, source_target_pairs={{0,2},{2,0},{4,6},{6,4},{8,10},{10,8},{12,14},{14,12},{16,18},{18,... | collective-permute-start | bytes 208904 | tf_op jit(solution)/shard_map/ppermute | solution.py:590
  12.1 0.1 collective-permute-start.4
  12.2 2.1 %collective-permute-done.2.refs_1_ = bf16[272,128]{1,0:T(8,128)(2,1)S(1)} collective-permute-done((bf16[272,128]{1,0:T(8,128)(2,1)S(1)}, bf16[272,128]{1,0:T(8,128)(2,1)S(1)}, u32[]{:S(2)}, u32[]{:S(2)}) %collective-permute-start.2) | collective-permute-done | bytes 69664 | tf_op jit(solution)/shard_map/ppermute | solution.py:590
  14.3 1.6 %collective-permute-done.3.refs_2_ = bf16[272,128]{1,0:T(8,128)(2,1)S(1)} collective-permute-done((bf16[272,128]{1,0:T(8,128)(2,1)S(1)}, bf16[272,128]{1,0:T(8,128)(2,1)S(1)}, u32[]{:S(2)}, u32[]{:S(2)}) %collective-permute-start.3) | collective-permute-done | bytes 69664 | tf_op jit(solution)/shard_map/ppermute | solution.py:590
  15.9 0.5 %collective-permute-done.4.refs_3_ = bf16[272,128]{1,0:T(8,128)(2,1)S(1)} collective-permute-done((bf16[272,128]{1,0:T(8,128)(2,1)S(1)}, bf16[272,128]{1,0:T(8,128)(2,1)S(1)}, u32[]{:S(2)}, u32[]{:S(2)}) %collective-permute-start.4) | collective-permute-done | bytes 69664 | tf_op jit(solution)/shard_map/ppermute | solution.py:590
  16.4 1.6 %collective-permute-start.5 = (bf16[272,128]{1,0:T(8,128)(2,1)S(1)}, bf16[272,128]{1,0:T(8,128)(2,1)S(1)}, u32[]{:S(2)}, u32[]{:S(2)}) collective-permute-start(bf16[272,128]{1,0:T(8,128)(2,1)S(1)} %get-tuple-element.48), channel_id=1, source_target_pairs={{0,4},{2,6},{4,12},{6,14},{8,0},{10,2},{12,8},{14,10},{16,20},{18,... | collective-permute-start | bytes 208904 | tf_op jit(solution)/shard_map/ppermute | solution.py:590
  18.1 2.5 %collective-permute-start.6 = (bf16[272,128]{1,0:T(8,128)(2,1)S(1)}, bf16[272,128]{1,0:T(8,128)(2,1)S(1)}, u32[]{:S(2)}, u32[]{:S(2)}) collective-permute-start(bf16[272,128]{1,0:T(8,128)(2,1)S(1)} %get-tuple-element.49), channel_id=1, source_target_pairs={{0,12},{2,14},{4,8},{6,10},{8,4},{10,6},{12,0},{14,2},{16,28},{18,... | collective-permute-start | bytes 208904 | tf_op jit(solution)/shard_map/ppermute | solution.py:590
  20.5 1.6 %collective-permute-start.7 = (bf16[272,128]{1,0:T(8,128)(2,1)S(1)}, bf16[272,128]{1,0:T(8,128)(2,1)S(1)}, u32[]{:S(2)}, u32[]{:S(2)}) collective-permute-start(bf16[272,128]{1,0:T(8,128)(2,1)S(1)} %get-tuple-element.50), channel_id=1, source_target_pairs={{0,8},{2,10},{4,0},{6,2},{8,12},{10,14},{12,4},{14,6},{16,24},{18,... | collective-permute-start | bytes 208904 | tf_op jit(solution)/shard_map/ppermute | solution.py:590
  22.1 0.0 copy-done
  22.1 0.0 copy-done.2
  22.1 0.0 copy-done.6
  22.1 0.0 copy-done.7
  22.1 0.5 %cached_scores.1 = (f32[128,128]{1,0:T(8,128)S(1)}, bf16[128,256]{1,0:T(8,128)(2,1)S(1)}) custom-call(s32[1,8]{1,0:T(1,128)S(1)} %bitcast.11, s32[1,8]{1,0:T(1,128)S(1)} %bitcast.12, bf16[8,2048]{1,0:T(8,128)(2,1)S(1)} %copy-done.2, bf16[8,128,256]{2,1,0:T(8,128)(2,1)S(1)} %copy-done), custom_call_target="tpu_custom_call" | custom-call | flops 33554432 | bytes 524288 | tf_op jit(solution)/shard_map/cached_scores/pallas_call | solution.py:275
  22.6 1.8 %collective-permute-done.5.refs_1_ = bf16[272,128]{1,0:T(8,128)(2,1)S(1)} collective-permute-done((bf16[272,128]{1,0:T(8,128)(2,1)S(1)}, bf16[272,128]{1,0:T(8,128)(2,1)S(1)}, u32[]{:S(2)}, u32[]{:S(2)}) %collective-permute-start.5) | collective-permute-done | bytes 69664 | tf_op jit(solution)/shard_map/ppermute | solution.py:590
  24.4 0.2 early_scores.1.early_ref
  24.6 0.0 collective-permute-done.6.refs_2_
  24.6 0.5 %collective-permute-done.7.refs_3_ = bf16[272,128]{1,0:T(8,128)(2,1)S(1)} collective-permute-done((bf16[272,128]{1,0:T(8,128)(2,1)S(1)}, bf16[272,128]{1,0:T(8,128)(2,1)S(1)}, u32[]{:S(2)}, u32[]{:S(2)}) %collective-permute-start.7) | collective-permute-done | bytes 69664 | tf_op jit(solution)/shard_map/ppermute | solution.py:590
  25.1 0.0 copy-done.1
  25.1 1.2 %attend.1 = bf16[8,2048]{1,0:T(8,128)(2,1)} custom-call(bf16[128,256]{1,0:T(8,128)(2,1)S(1)} %get-tuple-element.41.queries_ref, f32[128,128]{1,0:T(8,128)S(1)} %get-tuple-element.42.score_ref, f32[128,128]{1,0:T(8,128)S(1)} %early_scores.1.early_ref, bf16[8,128,256]{2,1,0:T(8,128)(2,1)S(1)} %copy-done.1, bf16[272,128]{1,0:T(8,128)(2,1)S(1)} %get-tuple-element.47.refs_0_, ...), custom_call_target="tpu_custom_call" | custom-call | flops 134217728 | bytes 524288 | tf_op jit(solution)/shard_map/attend/pallas_call | solution.py:429
  (1 shorter events, 0.0 us)
Async XLA Ops:
  1.2 4.0 %collective-permute-start = (f32[96,128]{1,0:T(8,128)S(1)}, f32[96,128]{1,0:T(8,128)S(1)}, u32[]{:S(2)}, u32[]{:S(2)}) collective-permute-start(f32[96,128]{1,0:T(8,128)S(1)} %get-tuple-element.31.own_ref), channel_id=1, source_target_pairs={{0,1},{1,0},{2,3},{3,2},{4,5},{5,4},{6,7},{7,6},{8,9},{9,8},{10,11... | collective-permute-start | bytes 147464 | tf_op jit(solution)/shard_map/ppermute | solution.py:578
  1.7 3.5 %copy-start.3 = (f32[4096]{0:T(1024)S(1)}, f32[4096]{0:T(1024)}, u32[]{:S(2)}) copy-start(f32[4096]{0:T(1024)} %param.14) | copy-start | bytes 49156
  6.2 1.5 %collective-permute-start.1 = (f32[96,512]{1,0:T(8,128)S(1)}, f32[96,512]{1,0:T(8,128)S(1)}, u32[]{:S(2)}, u32[]{:S(2)}) collective-permute-start(f32[96,512]{1,0:T(8,128)S(1)} %get-tuple-element.35), channel_id=1, source_target_pairs={{0,1},{1,0},{2,3},{3,2},{4,5},{5,4},{6,7},{7,6},{8,9},{9,8},{10,11... | collective-permute-start | bytes 589832 | tf_op jit(solution)/shard_map/ppermute | solution.py:585
  6.3 1.4 %copy-start.4 = (f32[256]{0:T(256)S(1)}, f32[256]{0:T(256)}, u32[]{:S(2)}) copy-start(f32[256]{0:T(256)} %param.17) | copy-start | bytes 3076
  6.3 1.4 %copy-start.5 = (f32[256]{0:T(256)S(1)}, f32[256]{0:T(256)}, u32[]{:S(2)}) copy-start(f32[256]{0:T(256)} %param.18) | copy-start | bytes 3076
  6.3 15.8 %copy-start = (bf16[8,128,256]{2,1,0:T(8,128)(2,1)S(1)}, bf16[8,128,256]{2,1,0:T(8,128)(2,1)}, u32[]{:S(2)}) copy-start(bf16[8,128,256]{2,1,0:T(8,128)(2,1)} %key_ref.1) | copy-start | bytes 1572868
  6.3 15.8 %copy-start.2 = (bf16[8,2048]{1,0:T(8,128)(2,1)S(1)}, bf16[8,2048]{1,0:T(8,128)(2,1)}, u32[]{:S(2)}) copy-start(bf16[8,2048]{1,0:T(8,128)(2,1)} %queries_ref) | copy-start | bytes 98308
  6.3 15.8 %copy-start.6 = (s32[8]{0:T(128)S(1)}, s32[8]{0:T(128)}, u32[]{:S(2)}) copy-start(s32[8]{0:T(128)} %param.22) | copy-start | bytes 100
  6.3 15.8 %copy-start.7 = (s32[8]{0:T(128)S(1)}, s32[8]{0:T(128)}, u32[]{:S(2)}) copy-start(s32[8]{0:T(128)} %param.23) | copy-start | bytes 100
  6.4 18.8 %copy-start.1 = (bf16[8,128,256]{2,1,0:T(8,128)(2,1)S(1)}, bf16[8,128,256]{2,1,0:T(8,128)(2,1)}, u32[]{:S(2)}) copy-start(bf16[8,128,256]{2,1,0:T(8,128)(2,1)} %cache_ref.1) | copy-start | bytes 1572868
  7.9 6.4 %collective-permute-start.2 = (bf16[272,128]{1,0:T(8,128)(2,1)S(1)}, bf16[272,128]{1,0:T(8,128)(2,1)S(1)}, u32[]{:S(2)}, u32[]{:S(2)}) collective-permute-start(bf16[272,128]{1,0:T(8,128)(2,1)S(1)} %get-tuple-element.44), channel_id=1, source_target_pairs={{0,18},{2,16},{4,22},{6,20},{8,26},{10,24},{12,30},{14,28},{16,2},... | collective-permute-start | bytes 208904 | tf_op jit(solution)/shard_map/ppermute | solution.py:590
  11.6 4.3 %collective-permute-start.3 = (bf16[272,128]{1,0:T(8,128)(2,1)S(1)}, bf16[272,128]{1,0:T(8,128)(2,1)S(1)}, u32[]{:S(2)}, u32[]{:S(2)}) collective-permute-start(bf16[272,128]{1,0:T(8,128)(2,1)S(1)} %get-tuple-element.45), channel_id=1, source_target_pairs={{0,2},{2,0},{4,6},{6,4},{8,10},{10,8},{12,14},{14,12},{16,18},{18,... | collective-permute-start | bytes 208904 | tf_op jit(solution)/shard_map/ppermute | solution.py:590
  12.1 4.3 %collective-permute-start.4 = (bf16[272,128]{1,0:T(8,128)(2,1)S(1)}, bf16[272,128]{1,0:T(8,128)(2,1)S(1)}, u32[]{:S(2)}, u32[]{:S(2)}) collective-permute-start(bf16[272,128]{1,0:T(8,128)(2,1)S(1)} %get-tuple-element.46), channel_id=1, source_target_pairs={{0,16},{2,18},{4,20},{6,22},{8,24},{10,26},{12,28},{14,30},{16,0},... | collective-permute-start | bytes 208904 | tf_op jit(solution)/shard_map/ppermute | solution.py:590
  16.4 8.0 %collective-permute-start.5 = (bf16[272,128]{1,0:T(8,128)(2,1)S(1)}, bf16[272,128]{1,0:T(8,128)(2,1)S(1)}, u32[]{:S(2)}, u32[]{:S(2)}) collective-permute-start(bf16[272,128]{1,0:T(8,128)(2,1)S(1)} %get-tuple-element.48), channel_id=1, source_target_pairs={{0,4},{2,6},{4,12},{6,14},{8,0},{10,2},{12,8},{14,10},{16,20},{18,... | collective-permute-start | bytes 208904 | tf_op jit(solution)/shard_map/ppermute | solution.py:590
  18.1 6.5 %collective-permute-start.6 = (bf16[272,128]{1,0:T(8,128)(2,1)S(1)}, bf16[272,128]{1,0:T(8,128)(2,1)S(1)}, u32[]{:S(2)}, u32[]{:S(2)}) collective-permute-start(bf16[272,128]{1,0:T(8,128)(2,1)S(1)} %get-tuple-element.49), channel_id=1, source_target_pairs={{0,12},{2,14},{4,8},{6,10},{8,4},{10,6},{12,0},{14,2},{16,28},{18,... | collective-permute-start | bytes 208904 | tf_op jit(solution)/shard_map/ppermute | solution.py:590
  20.5 4.6 %collective-permute-start.7 = (bf16[272,128]{1,0:T(8,128)(2,1)S(1)}, bf16[272,128]{1,0:T(8,128)(2,1)S(1)}, u32[]{:S(2)}, u32[]{:S(2)}) collective-permute-start(bf16[272,128]{1,0:T(8,128)(2,1)S(1)} %get-tuple-element.50), channel_id=1, source_target_pairs={{0,8},{2,10},{4,0},{6,2},{8,12},{10,14},{12,4},{14,6},{16,24},{18,... | collective-permute-start | bytes 208904 | tf_op jit(solution)/shard_map/ppermute | solution.py:590

commit v13 on v11

--- a/solution.py
+++ b/solution.py
@@ -225,8 +225,14 @@
     session_ref,
     w_key_ref,
     w_value_ref,
+    gain_ref,
+    key_bias_ref,
+    value_bias_ref,
     held_key_ref,
     held_value_ref,
+    held_gain_ref,
+    held_key_bias_ref,
+    held_value_bias_ref,
     pick_ref,
     ids_ref,
     session,
@@ -238,6 +244,9 @@
             (session_ref, session),
             (w_key_ref, held_key_ref),
             (w_value_ref, held_value_ref),
+            (gain_ref, held_gain_ref),
+            (key_bias_ref, held_key_bias_ref),
+            (value_bias_ref, held_value_bias_ref),
         )
     ):
         copies.append(pltpu.make_async_copy(source, held, arrived.at[at]))
@@ -248,25 +257,27 @@
         copy.wait()
 
 
-def beside(here, session, w_key, w_value, sizes):
+def beside(here, session, weights, sizes):
     partitions, _, capacity, near, _ = sizes
     slots, rows = partitions * capacity, session.shape[1]
     id_rows = -(-partitions // len(near) * slots // (16 * HEAD)) * 16 * len(near)
     return pl.pallas_call(
         functools.partial(beside_kernel, *sizes[1:]),
         out_shape=(
-            jax.ShapeDtypeStruct(w_key.shape, w_key.dtype),
-            jax.ShapeDtypeStruct(w_value.shape, w_value.dtype),
+            *(jax.ShapeDtypeStruct(array.shape, array.dtype) for array in weights),
             jax.ShapeDtypeStruct((slots, rows), jnp.bfloat16),
             jax.ShapeDtypeStruct((id_rows, HEAD), jnp.float32),
         ),
-        in_specs=[SMEM] + [HBM] * 3,
-        out_specs=(VMEM,) * 4,
-        scratch_shapes=[pltpu.VMEM(session.shape, session.dtype), pltpu.SemaphoreType.DMA((3,))],
+        in_specs=[SMEM] + [HBM] * (1 + len(weights)),
+        out_specs=(VMEM,) * (2 + len(weights)),
+        scratch_shapes=[
+            pltpu.VMEM(session.shape, session.dtype),
+            pltpu.SemaphoreType.DMA((1 + len(weights),)),
+        ],
         compiler_params=params(24),
-        cost_estimate=cost(4 * rows * rows * slots, 4 * w_key.size),
+        cost_estimate=cost(4 * rows * rows * slots, 4 * weights[0].size),
         name="beside",
-    )(here, in_hbm(session), in_hbm(w_key), in_hbm(w_value))
+    )(here, in_hbm(session), *map(in_hbm, weights))
 
 
 def cached_scores(start, length, queries, cache_key):
@@ -550,15 +561,16 @@
     here = lax.axis_index(("grp", "seq")).astype(jnp.int32).reshape(1)
     own, held = partial_squares(frames)
     other = lax.ppermute(own, "mp", swap)
-    held_key, held_value, pick, ids = beside(
-        here, token_session[None, :], w_key, w_value, (partitions, per_shard, capacity, near, members)
+    weights = (w_key, w_value, ln_gain[None, :], k_bias[None, :], v_bias[None, :])
+    held_key, held_value, gain, key_bias, value_bias, pick, ids = beside(
+        here, token_session[None, :], weights, (partitions, per_shard, capacity, near, members)
     )
     normed, sent = send_products(
-        index, held, own, other, ln_gain[None, :], held_key, held_value, frames.shape[1] * shares
+        index, held, own, other, gain, held_key, held_value, frames.shape[1] * shares
     )
     arrived = lax.ppermute(sent, "mp", swap)
     kept = keep_products(index, normed, held_key, held_value)
-    blocks = pack(pick, ids, kept, arrived, k_bias[None, :], v_bias[None, :], len(near))
+    blocks = pack(pick, ids, kept, arrived, key_bias, value_bias, len(near))
 
     def step(arrays, pairs):
         sent = [lax.ppermute(a, ("grp", "seq"), p) for a, p in zip(arrays[1:], pairs[1:])]

time: 26.5 us -> 26.5 us (level)
  no operation moved by 1% of the time
where the time goes in v13:
time: 26.5 us; the launch traced here: 26.3 us
  starting transfers between devices  10.7 us (40%)
  Pallas kernels  8.37 us (32%)
  waiting for transfers between devices  7.23 us (27%)
    ppermute x6, starting transfers between devices, step(): lax.ppermute(a, ('grp', 'seq'), p)  10 us
    ppermute x6, waiting for transfers between devices, step(): lax.ppermute(a, ('grp', 'seq'), p)  6.69 us
    pallas_call x1, Pallas kernels, beside(): pl.pallas_call(functools.partial(beside_kernel, *sizes[1:]), out_shape=(*...  3.53 us
    pallas_call x1, Pallas kernels, attend(): pl.pallas_call(functools.partial(attend_kernel, near, capacity), out_shap...  1.23 us
    pallas_call x1, Pallas kernels, partial_squares(): pl.pallas_call(squares_kernel, out_shape=(jax.ShapeDtypeStruct((rows, HEA...  1.21 us
    pallas_call x1, Pallas kernels, send_products(): pl.pallas_call(functools.partial(send_kernel, features), out_shape=(jax.S...  0.88 us
    pallas_call x1, Pallas kernels, keep_products(): pl.pallas_call(keep_kernel, out_shape=jax.ShapeDtypeStruct((rows, width),...  0.8 us
    ppermute x1, waiting for transfers between devices, local(): arrived = lax.ppermute(sent, 'mp', swap)  0.54 us
  transfers between devices with their start and end apart: 8, of which 6 were waited for; matrix products, arithmetic and copies ran while one was open for 0% of the time, Pallas kernels for 18%

profile of v13, /device:TPU:0, one launch (start us, length us, event | category | flops | bytes accessed | tf_op | source)
XLA Modules:
  0.0 26.3 jit_solution(15249123211629717072)
XLA Ops:
  0.0 1.2 %partial_squares.1 = (f32[96,128]{1,0:T(8,128)S(1)}, bf16[96,4096]{1,0:T(8,128)(2,1)S(1)}) custom-call(bf16[96,4096]{1,0:T(8,128)(2,1)} %frames_ref.1), custom_call_target="tpu_custom_call" | custom-call | flops 786432 | bytes 786432 | tf_op jit(solution)/shard_map/partial_squares/pallas_call | solution.py:64
  1.2 0.5 %collective-permute-start = (f32[96,128]{1,0:T(8,128)S(1)}, f32[96,128]{1,0:T(8,128)S(1)}, u32[]{:S(2)}, u32[]{:S(2)}) collective-permute-start(f32[96,128]{1,0:T(8,128)S(1)} %get-tuple-element.34.own_ref), channel_id=1, source_target_pairs={{0,1},{1,0},{2,3},{3,2},{4,5},{5,4},{6,7},{7,6},{8,9},{9,8},{10,11... | collective-permute-start | bytes 147464 | tf_op jit(solution)/shard_map/ppermute | solution.py:563
  1.7 3.5 %beside.1 = (bf16[4096,512]{1,0:T(8,128)(2,1)S(1)}, bf16[4096,512]{1,0:T(8,128)(2,1)S(1)}, f32[1,4096]{1,0:T(1,128)S(1)}, f32[1,256]{1,0:T(1,128)S(1)}, f32[1,25...) custom-call(s32[1]{0:T(128)} %bitcast.2.here_ref, s32[1,96]{1,0:T(1,128)} %bitcast.13, ...), custom_call_target="tpu_custom_call" | custom-call | flops 9437184 | bytes 8388608 | tf_op jit(solution)/shard_map/beside/pallas_call | solution.py:264
  5.3 0.0 collective-permute-done.other_ref
  5.3 0.9 %send_products.1 = (bf16[96,4096]{1,0:T(8,128)(2,1)S(1)}, f32[96,512]{1,0:T(8,128)S(1)}) custom-call(s32[1]{0:T(128)} %bitcast.7.index_ref, bf16[96,4096]{1,0:T(8,128)(2,1)S(1)} %get-tuple-element.33.frames_ref, f32[96,128]{1,0:T(8,128)S(1)} %get-tuple-element.34.own_ref, f32[96,128]{1,0:T(8,128)S(1)} %collective-permute-done.other_ref, ...), custom_call_target="tpu_custom_call" | custom-call | flops 402653184 | bytes 4194304 | tf_op jit(solution)/shard_map/send_products/pallas_call | solution.py:100
  6.2 0.1 collective-permute-start.1
  6.3 0.0 copy-start
  6.3 0.0 copy-start.2
  6.3 0.0 copy-start.3
  6.3 0.0 copy-start.4
  6.3 0.0 copy-start.1
  6.3 0.8 %keep_products.1.kept_ref = f32[96,512]{1,0:T(8,128)S(1)} custom-call(s32[1]{0:T(128)} %bitcast.7.index_ref, bf16[96,4096]{1,0:T(8,128)(2,1)S(1)} %get-tuple-element.38.normed_ref, bf16[4096,512]{1,0:T(8,128)(2,1)S(1)} %get-tuple-element.36.key_ref, bf16[4096,512]{1,0:T(8,128)(2,1)S(1)} %get-tuple-element.37.value_ref), custom_call_target="tpu_custom_call" | custom-call | flops 402653184 | bytes 4194304 | tf_op jit(solution)/shard_map/keep_products/pallas_call | solution.py:121
  7.2 0.5 %collective-permute-done.1.got_ref = f32[96,512]{1,0:T(8,128)S(1)} collective-permute-done((f32[96,512]{1,0:T(8,128)S(1)}, f32[96,512]{1,0:T(8,128)S(1)}, u32[]{:S(2)}, u32[]{:S(2)}) %collective-permute-start.1) | collective-permute-done | bytes 196640 | tf_op jit(solution)/shard_map/ppermute | solution.py:571
  7.7 0.2 pack.1
  7.9 3.7 %collective-permute-start.2 = (bf16[272,128]{1,0:T(8,128)(2,1)S(1)}, bf16[272,128]{1,0:T(8,128)(2,1)S(1)}, u32[]{:S(2)}, u32[]{:S(2)}) collective-permute-start(bf16[272,128]{1,0:T(8,128)(2,1)S(1)} %get-tuple-element.50), channel_id=1, source_target_pairs={{0,18},{2,16},{4,22},{6,20},{8,26},{10,24},{12,30},{14,28},{16,2},... | collective-permute-start | bytes 208904 | tf_op jit(solution)/shard_map/ppermute | solution.py:576
  11.6 0.5 %collective-permute-start.3 = (bf16[272,128]{1,0:T(8,128)(2,1)S(1)}, bf16[272,128]{1,0:T(8,128)(2,1)S(1)}, u32[]{:S(2)}, u32[]{:S(2)}) collective-permute-start(bf16[272,128]{1,0:T(8,128)(2,1)S(1)} %get-tuple-element.51), channel_id=1, source_target_pairs={{0,2},{2,0},{4,6},{6,4},{8,10},{10,8},{12,14},{14,12},{16,18},{18,... | collective-permute-start | bytes 208904 | tf_op jit(solution)/shard_map/ppermute | solution.py:576
  12.1 0.1 collective-permute-start.4
  12.2 2.1 %collective-permute-done.2.refs_1_ = bf16[272,128]{1,0:T(8,128)(2,1)S(1)} collective-permute-done((bf16[272,128]{1,0:T(8,128)(2,1)S(1)}, bf16[272,128]{1,0:T(8,128)(2,1)S(1)}, u32[]{:S(2)}, u32[]{:S(2)}) %collective-permute-start.2) | collective-permute-done | bytes 69664 | tf_op jit(solution)/shard_map/ppermute | solution.py:576
  14.3 1.6 %collective-permute-done.3.refs_2_ = bf16[272,128]{1,0:T(8,128)(2,1)S(1)} collective-permute-done((bf16[272,128]{1,0:T(8,128)(2,1)S(1)}, bf16[272,128]{1,0:T(8,128)(2,1)S(1)}, u32[]{:S(2)}, u32[]{:S(2)}) %collective-permute-start.3) | collective-permute-done | bytes 69664 | tf_op jit(solution)/shard_map/ppermute | solution.py:576
  15.9 0.5 %collective-permute-done.4.refs_3_ = bf16[272,128]{1,0:T(8,128)(2,1)S(1)} collective-permute-done((bf16[272,128]{1,0:T(8,128)(2,1)S(1)}, bf16[272,128]{1,0:T(8,128)(2,1)S(1)}, u32[]{:S(2)}, u32[]{:S(2)}) %collective-permute-start.4) | collective-permute-done | bytes 69664 | tf_op jit(solution)/shard_map/ppermute | solution.py:576
  16.5 1.6 %collective-permute-start.5 = (bf16[272,128]{1,0:T(8,128)(2,1)S(1)}, bf16[272,128]{1,0:T(8,128)(2,1)S(1)}, u32[]{:S(2)}, u32[]{:S(2)}) collective-permute-start(bf16[272,128]{1,0:T(8,128)(2,1)S(1)} %get-tuple-element.54), channel_id=1, source_target_pairs={{0,4},{2,6},{4,12},{6,14},{8,0},{10,2},{12,8},{14,10},{16,20},{18,... | collective-permute-start | bytes 208904 | tf_op jit(solution)/shard_map/ppermute | solution.py:576
  18.1 2.5 %collective-permute-start.6 = (bf16[272,128]{1,0:T(8,128)(2,1)S(1)}, bf16[272,128]{1,0:T(8,128)(2,1)S(1)}, u32[]{:S(2)}, u32[]{:S(2)}) collective-permute-start(bf16[272,128]{1,0:T(8,128)(2,1)S(1)} %get-tuple-element.55), channel_id=1, source_target_pairs={{0,12},{2,14},{4,8},{6,10},{8,4},{10,6},{12,0},{14,2},{16,28},{18,... | collective-permute-start | bytes 208904 | tf_op jit(solution)/shard_map/ppermute | solution.py:576
  20.6 1.6 %collective-permute-start.7 = (bf16[272,128]{1,0:T(8,128)(2,1)S(1)}, bf16[272,128]{1,0:T(8,128)(2,1)S(1)}, u32[]{:S(2)}, u32[]{:S(2)}) collective-permute-start(bf16[272,128]{1,0:T(8,128)(2,1)S(1)} %get-tuple-element.56), channel_id=1, source_target_pairs={{0,8},{2,10},{4,0},{6,2},{8,12},{10,14},{12,4},{14,6},{16,24},{18,... | collective-permute-start | bytes 208904 | tf_op jit(solution)/shard_map/ppermute | solution.py:576
  22.1 0.0 copy-done
  22.1 0.0 copy-done.2
  22.1 0.0 copy-done.3
  22.1 0.0 copy-done.4
  22.1 0.5 %cached_scores.1 = (f32[128,128]{1,0:T(8,128)S(1)}, bf16[128,256]{1,0:T(8,128)(2,1)S(1)}) custom-call(s32[1,8]{1,0:T(1,128)S(1)} %bitcast.8, s32[1,8]{1,0:T(1,128)S(1)} %bitcast.9, bf16[8,2048]{1,0:T(8,128)(2,1)S(1)} %copy-done.2, bf16[8,128,256]{2,1,0:T(8,128)(2,1)S(1)} %copy-done), custom_call_target="tpu_custom_call" | custom-call | flops 33554432 | bytes 524288 | tf_op jit(solution)/shard_map/cached_scores/pallas_call | solution.py:286
  22.6 1.8 %collective-permute-done.5.refs_1_ = bf16[272,128]{1,0:T(8,128)(2,1)S(1)} collective-permute-done((bf16[272,128]{1,0:T(8,128)(2,1)S(1)}, bf16[272,128]{1,0:T(8,128)(2,1)S(1)}, u32[]{:S(2)}, u32[]{:S(2)}) %collective-permute-start.5) | collective-permute-done | bytes 69664 | tf_op jit(solution)/shard_map/ppermute | solution.py:576
  24.4 0.0 collective-permute-done.6.refs_2_
  24.4 0.7 %collective-permute-done.7.refs_3_ = bf16[272,128]{1,0:T(8,128)(2,1)S(1)} collective-permute-done((bf16[272,128]{1,0:T(8,128)(2,1)S(1)}, bf16[272,128]{1,0:T(8,128)(2,1)S(1)}, u32[]{:S(2)}, u32[]{:S(2)}) %collective-permute-start.7) | collective-permute-done | bytes 69664 | tf_op jit(solution)/shard_map/ppermute | solution.py:576
  25.1 0.0 copy-done.1
  25.1 1.2 %attend.1 = bf16[8,2048]{1,0:T(8,128)(2,1)} custom-call(bf16[128,256]{1,0:T(8,128)(2,1)S(1)} %get-tuple-element.47.queries_ref, f32[128,128]{1,0:T(8,128)S(1)} %get-tuple-element.48.score_ref, bf16[8,128,256]{2,1,0:T(8,128)(2,1)S(1)} %copy-done.1, bf16[272,128]{1,0:T(8,128)(2,1)S(1)} %get-tuple-element.53.refs_0_, ...), custom_call_target="tpu_custom_call" | custom-call | flops 134217728 | bytes 524288 | tf_op jit(solution)/shard_map/attend/pallas_call | solution.py:414
  (1 shorter events, 0.0 us)
Async XLA Ops:
  1.2 4.1 %collective-permute-start = (f32[96,128]{1,0:T(8,128)S(1)}, f32[96,128]{1,0:T(8,128)S(1)}, u32[]{:S(2)}, u32[]{:S(2)}) collective-permute-start(f32[96,128]{1,0:T(8,128)S(1)} %get-tuple-element.34.own_ref), channel_id=1, source_target_pairs={{0,1},{1,0},{2,3},{3,2},{4,5},{5,4},{6,7},{7,6},{8,9},{9,8},{10,11... | collective-permute-start | bytes 147464 | tf_op jit(solution)/shard_map/ppermute | solution.py:563
  6.2 1.5 %collective-permute-start.1 = (f32[96,512]{1,0:T(8,128)S(1)}, f32[96,512]{1,0:T(8,128)S(1)}, u32[]{:S(2)}, u32[]{:S(2)}) collective-permute-start(f32[96,512]{1,0:T(8,128)S(1)} %get-tuple-element.39), channel_id=1, source_target_pairs={{0,1},{1,0},{2,3},{3,2},{4,5},{5,4},{6,7},{7,6},{8,9},{9,8},{10,11... | collective-permute-start | bytes 589832 | tf_op jit(solution)/shard_map/ppermute | solution.py:571
  6.3 15.8 %copy-start = (bf16[8,128,256]{2,1,0:T(8,128)(2,1)S(1)}, bf16[8,128,256]{2,1,0:T(8,128)(2,1)}, u32[]{:S(2)}) copy-start(bf16[8,128,256]{2,1,0:T(8,128)(2,1)} %key_ref.1) | copy-start | bytes 1572868
  6.3 15.8 %copy-start.2 = (bf16[8,2048]{1,0:T(8,128)(2,1)S(1)}, bf16[8,2048]{1,0:T(8,128)(2,1)}, u32[]{:S(2)}) copy-start(bf16[8,2048]{1,0:T(8,128)(2,1)} %queries_ref) | copy-start | bytes 98308
  6.3 15.8 %copy-start.3 = (s32[8]{0:T(128)S(1)}, s32[8]{0:T(128)}, u32[]{:S(2)}) copy-start(s32[8]{0:T(128)} %param.22) | copy-start | bytes 100
  6.3 15.8 %copy-start.4 = (s32[8]{0:T(128)S(1)}, s32[8]{0:T(128)}, u32[]{:S(2)}) copy-start(s32[8]{0:T(128)} %param.23) | copy-start | bytes 100
  6.3 18.8 %copy-start.1 = (bf16[8,128,256]{2,1,0:T(8,128)(2,1)S(1)}, bf16[8,128,256]{2,1,0:T(8,128)(2,1)}, u32[]{:S(2)}) copy-start(bf16[8,128,256]{2,1,0:T(8,128)(2,1)} %cache_ref.1) | copy-start | bytes 1572868
  7.9 6.4 %collective-permute-start.2 = (bf16[272,128]{1,0:T(8,128)(2,1)S(1)}, bf16[272,128]{1,0:T(8,128)(2,1)S(1)}, u32[]{:S(2)}, u32[]{:S(2)}) collective-permute-start(bf16[272,128]{1,0:T(8,128)(2,1)S(1)} %get-tuple-element.50), channel_id=1, source_target_pairs={{0,18},{2,16},{4,22},{6,20},{8,26},{10,24},{12,30},{14,28},{16,2},... | collective-permute-start | bytes 208904 | tf_op jit(solution)/shard_map/ppermute | solution.py:576
  11.6 4.3 %collective-permute-start.3 = (bf16[272,128]{1,0:T(8,128)(2,1)S(1)}, bf16[272,128]{1,0:T(8,128)(2,1)S(1)}, u32[]{:S(2)}, u32[]{:S(2)}) collective-permute-start(bf16[272,128]{1,0:T(8,128)(2,1)S(1)} %get-tuple-element.51), channel_id=1, source_target_pairs={{0,2},{2,0},{4,6},{6,4},{8,10},{10,8},{12,14},{14,12},{16,18},{18,... | collective-permute-start | bytes 208904 | tf_op jit(solution)/shard_map/ppermute | solution.py:576
  12.1 4.3 %collective-permute-start.4 = (bf16[272,128]{1,0:T(8,128)(2,1)S(1)}, bf16[272,128]{1,0:T(8,128)(2,1)S(1)}, u32[]{:S(2)}, u32[]{:S(2)}) collective-permute-start(bf16[272,128]{1,0:T(8,128)(2,1)S(1)} %get-tuple-element.52), channel_id=1, source_target_pairs={{0,16},{2,18},{4,20},{6,22},{8,24},{10,26},{12,28},{14,30},{16,0},... | collective-permute-start | bytes 208904 | tf_op jit(solution)/shard_map/ppermute | solution.py:576
  16.5 8.0 %collective-permute-start.5 = (bf16[272,128]{1,0:T(8,128)(2,1)S(1)}, bf16[272,128]{1,0:T(8,128)(2,1)S(1)}, u32[]{:S(2)}, u32[]{:S(2)}) collective-permute-start(bf16[272,128]{1,0:T(8,128)(2,1)S(1)} %get-tuple-element.54), channel_id=1, source_target_pairs={{0,4},{2,6},{4,12},{6,14},{8,0},{10,2},{12,8},{14,10},{16,20},{18,... | collective-permute-start | bytes 208904 | tf_op jit(solution)/shard_map/ppermute | solution.py:576
  18.1 6.3 %collective-permute-start.6 = (bf16[272,128]{1,0:T(8,128)(2,1)S(1)}, bf16[272,128]{1,0:T(8,128)(2,1)S(1)}, u32[]{:S(2)}, u32[]{:S(2)}) collective-permute-start(bf16[272,128]{1,0:T(8,128)(2,1)S(1)} %get-tuple-element.55), channel_id=1, source_target_pairs={{0,12},{2,14},{4,8},{6,10},{8,4},{10,6},{12,0},{14,2},{16,28},{18,... | collective-permute-start | bytes 208904 | tf_op jit(solution)/shard_map/ppermute | solution.py:576
  20.6 4.6 %collective-permute-start.7 = (bf16[272,128]{1,0:T(8,128)(2,1)S(1)}, bf16[272,128]{1,0:T(8,128)(2,1)S(1)}, u32[]{:S(2)}, u32[]{:S(2)}) collective-permute-start(bf16[272,128]{1,0:T(8,128)(2,1)S(1)} %get-tuple-element.56), channel_id=1, source_target_pairs={{0,8},{2,10},{4,0},{6,2},{8,12},{10,14},{12,4},{14,6},{16,24},{18,... | collective-permute-start | bytes 208904 | tf_op jit(solution)/shard_map/ppermute | solution.py:576

commit v14 on v11

--- a/solution.py
+++ b/solution.py
@@ -235,16 +235,16 @@
     copies = []
     for at, (source, held) in enumerate(
         (
-            (session_ref, session),
             (w_key_ref, held_key_ref),
             (w_value_ref, held_value_ref),
+            (session_ref, session),
         )
     ):
         copies.append(pltpu.make_async_copy(source, held, arrived.at[at]))
         copies[-1].start()
-    copies[0].wait()
+    copies[2].wait()
     route(per_shard, capacity, near, members, here_ref[0], session[...], pick_ref, ids_ref)
-    for copy in copies[1:]:
+    for copy in copies[:2]:
         copy.wait()
 
 
@@ -382,8 +382,9 @@
     cached = jnp.exp(cached - largest)
     fresh = jnp.exp(fresh - largest)
     total = jnp.sum(cached, axis=1, keepdims=True) + jnp.sum(fresh, axis=1, keepdims=True)
-    cached = cached / total
-    attended = dot((fresh / total).astype(jnp.bfloat16), rows_of(range(heads, 2 * heads)))
+    share = 1.0 / total
+    cached = cached * share
+    attended = dot((fresh * share).astype(jnp.bfloat16), rows_of(range(heads, 2 * heads)))
     row_session = lax.broadcasted_iota(jnp.int32, (rows, window), 0) % sessions
     for session in range(0, sessions, 2):
         weights = jnp.concatenate(

time: 26.5 us -> 26.5 us (level)
  no operation moved by 1% of the time
where the time goes in v14:
time: 26.5 us; the launch traced here: 26.3 us
  starting transfers between devices  10.7 us (40%)
  Pallas kernels  8.33 us (31%)
  waiting for transfers between devices  7.2 us (27%)
    ppermute x6, starting transfers between devices, step(): lax.ppermute(a, ('grp', 'seq'), p)  10 us
    ppermute x6, waiting for transfers between devices, step(): lax.ppermute(a, ('grp', 'seq'), p)  6.68 us
    pallas_call x1, Pallas kernels, beside(): pl.pallas_call(functools.partial(beside_kernel, *sizes[1:]), out_shape=(j...  3.5 us
    pallas_call x1, Pallas kernels, attend(): pl.pallas_call(functools.partial(attend_kernel, near, capacity), out_shap...  1.23 us
    pallas_call x1, Pallas kernels, partial_squares(): pl.pallas_call(squares_kernel, out_shape=(jax.ShapeDtypeStruct((rows, HEA...  1.21 us
    pallas_call x1, Pallas kernels, send_products(): pl.pallas_call(functools.partial(send_kernel, features), out_shape=(jax.S...  0.89 us
    pallas_call x1, Pallas kernels, keep_products(): pl.pallas_call(keep_kernel, out_shape=jax.ShapeDtypeStruct((rows, width),...  0.8 us
  transfers between devices with their start and end apart: 8, of which 6 were waited for; matrix products, arithmetic and copies ran while one was open for 0% of the time, Pallas kernels for 18%

profile of v14, /device:TPU:0, one launch (start us, length us, event | category | flops | bytes accessed | tf_op | source)
XLA Modules:
  0.0 26.3 jit_solution(5552216908499455600)
XLA Ops:
  0.0 1.2 %partial_squares.1 = (f32[96,128]{1,0:T(8,128)S(1)}, bf16[96,4096]{1,0:T(8,128)(2,1)S(1)}) custom-call(bf16[96,4096]{1,0:T(8,128)(2,1)} %frames_ref.1), custom_call_target="tpu_custom_call" | custom-call | flops 786432 | bytes 786432 | tf_op jit(solution)/shard_map/partial_squares/pallas_call | solution.py:64
  1.2 0.5 %collective-permute-start = (f32[96,128]{1,0:T(8,128)S(1)}, f32[96,128]{1,0:T(8,128)S(1)}, u32[]{:S(2)}, u32[]{:S(2)}) collective-permute-start(f32[96,128]{1,0:T(8,128)S(1)} %get-tuple-element.31.own_ref), channel_id=1, source_target_pairs={{0,1},{1,0},{2,3},{3,2},{4,5},{5,4},{6,7},{7,6},{8,9},{9,8},{10,11... | collective-permute-start | bytes 147464 | tf_op jit(solution)/shard_map/ppermute | solution.py:553
  1.7 0.0 copy-start.3
  1.7 3.5 %beside.1 = (bf16[4096,512]{1,0:T(8,128)(2,1)S(1)}, bf16[4096,512]{1,0:T(8,128)(2,1)S(1)}, bf16[256,96]{1,0:T(8,128)(2,1)S(1)}, f32[64,128]{1,0:T(8,128)S(1)}) custom-call(s32[1]{0:T(128)} %bitcast.2.here_ref, s32[1,96]{1,0:T(1,128)} %bitcast.13, bf16[4096,512]{1,0:T(8,128)(2,1)} %w_key_ref.1, bf16[4096,512]{1,0:T(8,128)(2,1)} %w_value_ref.1), custom_call_target="tpu_custom_call" | custom-call | flops 9437184 | bytes 8388608 | tf_op jit(solution)/shard_map/beside/pallas_call | solution.py:255
  5.2 0.0 collective-permute-done.other_ref
  5.3 0.0 copy-done.3
  5.3 0.9 %send_products.1 = (bf16[96,4096]{1,0:T(8,128)(2,1)S(1)}, f32[96,512]{1,0:T(8,128)S(1)}) custom-call(s32[1]{0:T(128)} %bitcast.4.index_ref, bf16[96,4096]{1,0:T(8,128)(2,1)S(1)} %get-tuple-element.30.frames_ref, f32[96,128]{1,0:T(8,128)S(1)} %get-tuple-element.31.own_ref, f32[96,128]{1,0:T(8,128)S(1)} %collective-permute-done.other_ref, ...), custom_call_target="tpu_custom_call" | custom-call | flops 402653184 | bytes 4194304 | tf_op jit(solution)/shard_map/send_products/pallas_call | solution.py:100
  6.2 0.1 collective-permute-start.1
  6.3 0.0 copy-start.4
  6.3 0.0 copy-start.5
  6.3 0.0 copy-start
  6.3 0.0 copy-start.2
  6.3 0.0 copy-start.6
  6.3 0.0 copy-start.7
  6.3 0.0 copy-start.1
  6.4 0.8 %keep_products.1.kept_ref = f32[96,512]{1,0:T(8,128)S(1)} custom-call(s32[1]{0:T(128)} %bitcast.4.index_ref, bf16[96,4096]{1,0:T(8,128)(2,1)S(1)} %get-tuple-element.34.normed_ref, bf16[4096,512]{1,0:T(8,128)(2,1)S(1)} %get-tuple-element.32.key_ref, bf16[4096,512]{1,0:T(8,128)(2,1)S(1)} %get-tuple-element.33.value_ref), custom_call_target="tpu_custom_call" | custom-call | flops 402653184 | bytes 4194304 | tf_op jit(solution)/shard_map/keep_products/pallas_call | solution.py:121
  7.2 0.5 %collective-permute-done.1.got_ref = f32[96,512]{1,0:T(8,128)S(1)} collective-permute-done((f32[96,512]{1,0:T(8,128)S(1)}, f32[96,512]{1,0:T(8,128)S(1)}, u32[]{:S(2)}, u32[]{:S(2)}) %collective-permute-start.1) | collective-permute-done | bytes 196640 | tf_op jit(solution)/shard_map/ppermute | solution.py:560
  7.7 0.0 copy-done.4
  7.7 0.0 copy-done.5
  7.7 0.2 pack.1
  7.9 3.7 %collective-permute-start.2 = (bf16[272,128]{1,0:T(8,128)(2,1)S(1)}, bf16[272,128]{1,0:T(8,128)(2,1)S(1)}, u32[]{:S(2)}, u32[]{:S(2)}) collective-permute-start(bf16[272,128]{1,0:T(8,128)(2,1)S(1)} %get-tuple-element.44), channel_id=1, source_target_pairs={{0,18},{2,16},{4,22},{6,20},{8,26},{10,24},{12,30},{14,28},{16,2},... | collective-permute-start | bytes 208904 | tf_op jit(solution)/shard_map/ppermute | solution.py:565
  11.6 0.5 %collective-permute-start.3 = (bf16[272,128]{1,0:T(8,128)(2,1)S(1)}, bf16[272,128]{1,0:T(8,128)(2,1)S(1)}, u32[]{:S(2)}, u32[]{:S(2)}) collective-permute-start(bf16[272,128]{1,0:T(8,128)(2,1)S(1)} %get-tuple-element.45), channel_id=1, source_target_pairs={{0,2},{2,0},{4,6},{6,4},{8,10},{10,8},{12,14},{14,12},{16,18},{18,... | collective-permute-start | bytes 208904 | tf_op jit(solution)/shard_map/ppermute | solution.py:565
  12.1 0.1 collective-permute-start.4
  12.2 2.1 %collective-permute-done.2.refs_1_ = bf16[272,128]{1,0:T(8,128)(2,1)S(1)} collective-permute-done((bf16[272,128]{1,0:T(8,128)(2,1)S(1)}, bf16[272,128]{1,0:T(8,128)(2,1)S(1)}, u32[]{:S(2)}, u32[]{:S(2)}) %collective-permute-start.2) | collective-permute-done | bytes 69664 | tf_op jit(solution)/shard_map/ppermute | solution.py:565
  14.3 1.6 %collective-permute-done.3.refs_2_ = bf16[272,128]{1,0:T(8,128)(2,1)S(1)} collective-permute-done((bf16[272,128]{1,0:T(8,128)(2,1)S(1)}, bf16[272,128]{1,0:T(8,128)(2,1)S(1)}, u32[]{:S(2)}, u32[]{:S(2)}) %collective-permute-start.3) | collective-permute-done | bytes 69664 | tf_op jit(solution)/shard_map/ppermute | solution.py:565
  15.9 0.5 %collective-permute-done.4.refs_3_ = bf16[272,128]{1,0:T(8,128)(2,1)S(1)} collective-permute-done((bf16[272,128]{1,0:T(8,128)(2,1)S(1)}, bf16[272,128]{1,0:T(8,128)(2,1)S(1)}, u32[]{:S(2)}, u32[]{:S(2)}) %collective-permute-start.4) | collective-permute-done | bytes 69664 | tf_op jit(solution)/shard_map/ppermute | solution.py:565
  16.4 1.6 %collective-permute-start.5 = (bf16[272,128]{1,0:T(8,128)(2,1)S(1)}, bf16[272,128]{1,0:T(8,128)(2,1)S(1)}, u32[]{:S(2)}, u32[]{:S(2)}) collective-permute-start(bf16[272,128]{1,0:T(8,128)(2,1)S(1)} %get-tuple-element.48), channel_id=1, source_target_pairs={{0,4},{2,6},{4,12},{6,14},{8,0},{10,2},{12,8},{14,10},{16,20},{18,... | collective-permute-start | bytes 208904 | tf_op jit(solution)/shard_map/ppermute | solution.py:565
  18.1 2.5 %collective-permute-start.6 = (bf16[272,128]{1,0:T(8,128)(2,1)S(1)}, bf16[272,128]{1,0:T(8,128)(2,1)S(1)}, u32[]{:S(2)}, u32[]{:S(2)}) collective-permute-start(bf16[272,128]{1,0:T(8,128)(2,1)S(1)} %get-tuple-element.49), channel_id=1, source_target_pairs={{0,12},{2,14},{4,8},{6,10},{8,4},{10,6},{12,0},{14,2},{16,28},{18,... | collective-permute-start | bytes 208904 | tf_op jit(solution)/shard_map/ppermute | solution.py:565
  20.5 1.6 %collective-permute-start.7 = (bf16[272,128]{1,0:T(8,128)(2,1)S(1)}, bf16[272,128]{1,0:T(8,128)(2,1)S(1)}, u32[]{:S(2)}, u32[]{:S(2)}) collective-permute-start(bf16[272,128]{1,0:T(8,128)(2,1)S(1)} %get-tuple-element.50), channel_id=1, source_target_pairs={{0,8},{2,10},{4,0},{6,2},{8,12},{10,14},{12,4},{14,6},{16,24},{18,... | collective-permute-start | bytes 208904 | tf_op jit(solution)/shard_map/ppermute | solution.py:565
  22.1 0.0 copy-done
  22.1 0.0 copy-done.2
  22.1 0.0 copy-done.6
  22.1 0.0 copy-done.7
  22.1 0.5 %cached_scores.1 = (f32[128,128]{1,0:T(8,128)S(1)}, bf16[128,256]{1,0:T(8,128)(2,1)S(1)}) custom-call(s32[1,8]{1,0:T(1,128)S(1)} %bitcast.11, s32[1,8]{1,0:T(1,128)S(1)} %bitcast.12, bf16[8,2048]{1,0:T(8,128)(2,1)S(1)} %copy-done.2, bf16[8,128,256]{2,1,0:T(8,128)(2,1)S(1)} %copy-done), custom_call_target="tpu_custom_call" | custom-call | flops 33554432 | bytes 524288 | tf_op jit(solution)/shard_map/cached_scores/pallas_call | solution.py:275
  22.6 1.8 %collective-permute-done.5.refs_1_ = bf16[272,128]{1,0:T(8,128)(2,1)S(1)} collective-permute-done((bf16[272,128]{1,0:T(8,128)(2,1)S(1)}, bf16[272,128]{1,0:T(8,128)(2,1)S(1)}, u32[]{:S(2)}, u32[]{:S(2)}) %collective-permute-start.5) | collective-permute-done | bytes 69664 | tf_op jit(solution)/shard_map/ppermute | solution.py:565
  24.4 0.0 collective-permute-done.6.refs_2_
  24.4 0.7 %collective-permute-done.7.refs_3_ = bf16[272,128]{1,0:T(8,128)(2,1)S(1)} collective-permute-done((bf16[272,128]{1,0:T(8,128)(2,1)S(1)}, bf16[272,128]{1,0:T(8,128)(2,1)S(1)}, u32[]{:S(2)}, u32[]{:S(2)}) %collective-permute-start.7) | collective-permute-done | bytes 69664 | tf_op jit(solution)/shard_map/ppermute | solution.py:565
  25.1 0.0 copy-done.1
  25.1 1.2 %attend.1 = bf16[8,2048]{1,0:T(8,128)(2,1)} custom-call(bf16[128,256]{1,0:T(8,128)(2,1)S(1)} %get-tuple-element.41.queries_ref, f32[128,128]{1,0:T(8,128)S(1)} %get-tuple-element.42.score_ref, bf16[8,128,256]{2,1,0:T(8,128)(2,1)S(1)} %copy-done.1, bf16[272,128]{1,0:T(8,128)(2,1)S(1)} %get-tuple-element.47.refs_0_, ...), custom_call_target="tpu_custom_call" | custom-call | flops 134217728 | bytes 524288 | tf_op jit(solution)/shard_map/attend/pallas_call | solution.py:404
  (1 shorter events, 0.0 us)
Async XLA Ops:
  1.2 4.0 %collective-permute-start = (f32[96,128]{1,0:T(8,128)S(1)}, f32[96,128]{1,0:T(8,128)S(1)}, u32[]{:S(2)}, u32[]{:S(2)}) collective-permute-start(f32[96,128]{1,0:T(8,128)S(1)} %get-tuple-element.31.own_ref), channel_id=1, source_target_pairs={{0,1},{1,0},{2,3},{3,2},{4,5},{5,4},{6,7},{7,6},{8,9},{9,8},{10,11... | collective-permute-start | bytes 147464 | tf_op jit(solution)/shard_map/ppermute | solution.py:553
  1.7 3.5 %copy-start.3 = (f32[4096]{0:T(1024)S(1)}, f32[4096]{0:T(1024)}, u32[]{:S(2)}) copy-start(f32[4096]{0:T(1024)} %param.14) | copy-start | bytes 49156
  6.2 1.5 %collective-permute-start.1 = (f32[96,512]{1,0:T(8,128)S(1)}, f32[96,512]{1,0:T(8,128)S(1)}, u32[]{:S(2)}, u32[]{:S(2)}) collective-permute-start(f32[96,512]{1,0:T(8,128)S(1)} %get-tuple-element.35), channel_id=1, source_target_pairs={{0,1},{1,0},{2,3},{3,2},{4,5},{5,4},{6,7},{7,6},{8,9},{9,8},{10,11... | collective-permute-start | bytes 589832 | tf_op jit(solution)/shard_map/ppermute | solution.py:560
  6.3 1.4 %copy-start.4 = (f32[256]{0:T(256)S(1)}, f32[256]{0:T(256)}, u32[]{:S(2)}) copy-start(f32[256]{0:T(256)} %param.17) | copy-start | bytes 3076
  6.3 1.4 %copy-start.5 = (f32[256]{0:T(256)S(1)}, f32[256]{0:T(256)}, u32[]{:S(2)}) copy-start(f32[256]{0:T(256)} %param.18) | copy-start | bytes 3076
  6.3 15.8 %copy-start = (bf16[8,128,256]{2,1,0:T(8,128)(2,1)S(1)}, bf16[8,128,256]{2,1,0:T(8,128)(2,1)}, u32[]{:S(2)}) copy-start(bf16[8,128,256]{2,1,0:T(8,128)(2,1)} %key_ref.1) | copy-start | bytes 1572868
  6.3 15.8 %copy-start.2 = (bf16[8,2048]{1,0:T(8,128)(2,1)S(1)}, bf16[8,2048]{1,0:T(8,128)(2,1)}, u32[]{:S(2)}) copy-start(bf16[8,2048]{1,0:T(8,128)(2,1)} %queries_ref) | copy-start | bytes 98308
  6.3 15.8 %copy-start.6 = (s32[8]{0:T(128)S(1)}, s32[8]{0:T(128)}, u32[]{:S(2)}) copy-start(s32[8]{0:T(128)} %param.22) | copy-start | bytes 100
  6.3 15.8 %copy-start.7 = (s32[8]{0:T(128)S(1)}, s32[8]{0:T(128)}, u32[]{:S(2)}) copy-start(s32[8]{0:T(128)} %param.23) | copy-start | bytes 100
  6.3 18.8 %copy-start.1 = (bf16[8,128,256]{2,1,0:T(8,128)(2,1)S(1)}, bf16[8,128,256]{2,1,0:T(8,128)(2,1)}, u32[]{:S(2)}) copy-start(bf16[8,128,256]{2,1,0:T(8,128)(2,1)} %cache_ref.1) | copy-start | bytes 1572868
  7.9 6.4 %collective-permute-start.2 = (bf16[272,128]{1,0:T(8,128)(2,1)S(1)}, bf16[272,128]{1,0:T(8,128)(2,1)S(1)}, u32[]{:S(2)}, u32[]{:S(2)}) collective-permute-start(bf16[272,128]{1,0:T(8,128)(2,1)S(1)} %get-tuple-element.44), channel_id=1, source_target_pairs={{0,18},{2,16},{4,22},{6,20},{8,26},{10,24},{12,30},{14,28},{16,2},... | collective-permute-start | bytes 208904 | tf_op jit(solution)/shard_map/ppermute | solution.py:565
  11.6 4.3 %collective-permute-start.3 = (bf16[272,128]{1,0:T(8,128)(2,1)S(1)}, bf16[272,128]{1,0:T(8,128)(2,1)S(1)}, u32[]{:S(2)}, u32[]{:S(2)}) collective-permute-start(bf16[272,128]{1,0:T(8,128)(2,1)S(1)} %get-tuple-element.45), channel_id=1, source_target_pairs={{0,2},{2,0},{4,6},{6,4},{8,10},{10,8},{12,14},{14,12},{16,18},{18,... | collective-permute-start | bytes 208904 | tf_op jit(solution)/shard_map/ppermute | solution.py:565
  12.1 4.3 %collective-permute-start.4 = (bf16[272,128]{1,0:T(8,128)(2,1)S(1)}, bf16[272,128]{1,0:T(8,128)(2,1)S(1)}, u32[]{:S(2)}, u32[]{:S(2)}) collective-permute-start(bf16[272,128]{1,0:T(8,128)(2,1)S(1)} %get-tuple-element.46), channel_id=1, source_target_pairs={{0,16},{2,18},{4,20},{6,22},{8,24},{10,26},{12,28},{14,30},{16,0},... | collective-permute-start | bytes 208904 | tf_op jit(solution)/shard_map/ppermute | solution.py:565
  16.4 8.0 %collective-permute-start.5 = (bf16[272,128]{1,0:T(8,128)(2,1)S(1)}, bf16[272,128]{1,0:T(8,128)(2,1)S(1)}, u32[]{:S(2)}, u32[]{:S(2)}) collective-permute-start(bf16[272,128]{1,0:T(8,128)(2,1)S(1)} %get-tuple-element.48), channel_id=1, source_target_pairs={{0,4},{2,6},{4,12},{6,14},{8,0},{10,2},{12,8},{14,10},{16,20},{18,... | collective-permute-start | bytes 208904 | tf_op jit(solution)/shard_map/ppermute | solution.py:565
  18.1 6.3 %collective-permute-start.6 = (bf16[272,128]{1,0:T(8,128)(2,1)S(1)}, bf16[272,128]{1,0:T(8,128)(2,1)S(1)}, u32[]{:S(2)}, u32[]{:S(2)}) collective-permute-start(bf16[272,128]{1,0:T(8,128)(2,1)S(1)} %get-tuple-element.49), channel_id=1, source_target_pairs={{0,12},{2,14},{4,8},{6,10},{8,4},{10,6},{12,0},{14,2},{16,28},{18,... | collective-permute-start | bytes 208904 | tf_op jit(solution)/shard_map/ppermute | solution.py:565
  20.5 4.6 %collective-permute-start.7 = (bf16[272,128]{1,0:T(8,128)(2,1)S(1)}, bf16[272,128]{1,0:T(8,128)(2,1)S(1)}, u32[]{:S(2)}, u32[]{:S(2)}) collective-permute-start(bf16[272,128]{1,0:T(8,128)(2,1)S(1)} %get-tuple-element.50), channel_id=1, source_target_pairs={{0,8},{2,10},{4,0},{6,2},{8,12},{10,14},{12,4},{14,6},{16,24},{18,... | collective-permute-start | bytes 208904 | tf_op jit(solution)/shard_map/ppermute | solution.py:565
